TPU v7x, 32 devices: a whole 2x2x4 slice. The times are simulated.
32 devices in a mesh: seq: 8 (over z, core), dp: 4 (over y, x).
Axes of the slice: x: 2, y: 2, z: 4, core: 2. Of those that a mesh axis runs over, the one named last changes fastest.
Arguments:
- inputs: bfloat16 [4, 1024, 2048], P('dp', 'seq'), may hold values from -6 to 6
- segments: int32 [4, 1024], P('dp'), may hold values from -1 to 2, as said below
- routes: int32 [4, 1024, 6], P('dp', 'seq'), may hold values from 0 to 15, all different within a row; in each aligned block of 128 rows (0 to 127, 128 to 255, ..., all dimensions but the last counted through in order) at most 96 rows name the same one
- cotangent: bfloat16 [4, 1024, 2048], P('dp', 'seq'), may hold values from -6 to 6
- attention_gain: bfloat16 [2048], P('dp'), may hold values from 0.5 to 1.5
- query_weight: bfloat16 [2048, 3072], P('dp'), may hold values from -0.25 to 0.25
- latent_weight: bfloat16 [2048, 576], P('dp'), may hold values from -0.125 to 0.125
- latent_gain: bfloat16 [512], P('dp'), may hold values from 0.5 to 1.5
- expand_weight: bfloat16 [512, 4096], P('dp'), may hold values from -0.25 to 0.25
- output_weight: bfloat16 [2048, 2048], P('dp'), may hold values from -1.5 to 1.5
- feedforward_gain: bfloat16 [2048], P('dp'), may hold values from 0.5 to 1.5
- router_weight: bfloat16 [2048, 16], P('dp'), may hold values from -0.0625 to 0.0625
- shared_gate: bfloat16 [2048, 2816], P('dp'), may hold values from -0.125 to 0.125
- shared_up: bfloat16 [2048, 2816], P('dp'), may hold values from -0.125 to 0.125
- shared_down: bfloat16 [2816, 2048], P('dp'), may hold values from -0.109375 to 0.109375
- expert_gate: bfloat16 [16, 2048, 1408], P('seq', 'dp'), may hold values from -0.125 to 0.125
- expert_up: bfloat16 [16, 2048, 1408], P('seq', 'dp'), may hold values from -0.125 to 0.125
- expert_down: bfloat16 [16, 1408, 2048], P('seq', None, 'dp'), may hold values from -0.625 to 0.625
Outputs:
- layer_out: bfloat16 [4, 1024, 2048], P('dp', 'seq')
- grad_inputs: float32 [4, 1024, 2048], P('dp', 'seq')
- grad_attention_gain: float32 [2048], P('dp')
- grad_query_weight: float32 [2048, 3072], P('dp')
- grad_latent_weight: float32 [2048, 576], P('dp')
- grad_latent_gain: float32 [512], P('dp')
- grad_expand_weight: float32 [512, 4096], P('dp')
- grad_output_weight: float32 [2048, 2048], P('dp')
- grad_feedforward_gain: float32 [2048], P('dp')
- grad_router_weight: float32 [2048, 16], P('dp')
- grad_shared_gate: float32 [2048, 2816], P('dp')
- grad_shared_up: float32 [2048, 2816], P('dp')
- grad_shared_down: float32 [2816, 2048], P('dp')
- grad_expert_gate: float32 [16, 2048, 1408], P('seq', 'dp')
- grad_expert_up: float32 [16, 2048, 1408], P('seq', 'dp')
- grad_expert_down: float32 [16, 1408, 2048], P('seq', None, 'dp')
Inputs may be any that keep to these rules, and one draw needn't show every extreme that they name: `segments`: in each group ids never fall except that its last 1 to 32 positions are -1; document 1 begins within the group's first 128 positions and ends within its last 128. `routes`: each row names 6 different experts; in the rows of one device no expert is named by more than 96 rows, a bound that some block reaches.
All inputs are finite; a program needn't handle non-finite values.
Results may differ from a plain program's by a relative error of at most 0.024.
Values may be sent and summed in bfloat16 or wider, within the bound.
A program may use at most 448 MiB of HBM per device.

v0:
```python
import math

import jax
import jax.numpy as jnp
from jax import lax
from jax.sharding import PartitionSpec as P

HEADS = 16
NOPE = 128
ROPE = 64
VDIM = 128
KV_RANK = 512
TOP = 6
EXP_DEV = 2
CAP = 480


EPSILON = 1e-06
MASKED = -1e30
HIGHEST = lax.Precision.HIGHEST


def normalized_rows(values, gain):
    return values * lax.rsqrt(jnp.mean(values * values, axis=-1, keepdims=True) + EPSILON) * gain


def angles(positions, width):
    frequency = 10000.0 ** (-(2.0 * jnp.arange(width // 2, dtype=jnp.float32)) / width)
    turned = positions.astype(jnp.float32)[:, None] * frequency[None, :]
    return (jnp.cos(turned), jnp.sin(turned))


def rotate(values, cosine, sine):
    half_width = values.shape[-1] // 2
    lower_half = values[..., :half_width]
    upper_half = values[..., half_width:]
    return jnp.concatenate(
        [lower_half * cosine - upper_half * sine, upper_half * cosine + lower_half * sine], axis=-1
    )


def swiglu(gate_portion, up_part):
    return jax.nn.silu(gate_portion) * up_part


def local(
    inputs,
    segments,
    routes,
    cotangent,
    attention_gain,
    query_weight,
    latent_weight,
    latent_gain,
    expand_weight,
    output_weight,
    feedforward_gain,
    router_weight,
    shared_gate,
    shared_up,
    shared_down,
    expert_gate,
    expert_up,
    expert_down,
):
    seq_count = lax.axis_size("seq")
    rank_seq = lax.axis_index("seq")
    tokens = inputs.shape[1]
    width = inputs.shape[2]
    group = tokens * seq_count
    experts = EXP_DEV * seq_count
    slot_most = 2 * tokens * TOP // experts
    slab_rows = EXP_DEV * slot_most
    heads_dev = HEADS // seq_count
    qk_width = NOPE + ROPE
    score_scale = 1.0 / math.sqrt(qk_width)
    pair_count = tokens * TOP
    gathered = (
        lax.all_gather(attention_gain, "dp", axis=0, tiled=True),
        lax.all_gather(query_weight, "dp", axis=0, tiled=True),
        lax.all_gather(latent_weight, "dp", axis=0, tiled=True),
        lax.all_gather(latent_gain, "dp", axis=0, tiled=True),
        lax.all_gather(expand_weight, "dp", axis=0, tiled=True),
        lax.all_gather(output_weight, "dp", axis=0, tiled=True),
        lax.all_gather(feedforward_gain, "dp", axis=0, tiled=True),
        lax.all_gather(router_weight, "dp", axis=0, tiled=True),
        lax.all_gather(shared_gate, "dp", axis=0, tiled=True),
        lax.all_gather(shared_up, "dp", axis=0, tiled=True),
        lax.all_gather(shared_down, "dp", axis=0, tiled=True),
        lax.all_gather(expert_gate, "dp", axis=1, tiled=True),
        lax.all_gather(expert_up, "dp", axis=1, tiled=True),
        lax.all_gather(expert_down, "dp", axis=2, tiled=True),
    )
    (
        g_attn,
        w_query,
        w_latent,
        g_latent,
        w_expand,
        w_output,
        g_ffn,
        w_router,
        w_sgate,
        w_sup,
        w_sdown,
        w_egate,
        expert_up_weight,
        w_edown,
    ) = gathered
    x_float = inputs[0].astype(jnp.float32)
    seg_all = segments[0]
    route_ids = routes[0]
    grad_out = cotangent[0].astype(jnp.float32)
    local_pos = rank_seq * tokens + jnp.arange(tokens, dtype=jnp.int32)
    cosine, sine = angles(local_pos, ROPE)
    attn_in = normalized_rows(x_float, g_attn.astype(jnp.float32)).astype(jnp.bfloat16)
    q_raw = jnp.dot(attn_in, w_query, preferred_element_type=jnp.float32).reshape(
        tokens, HEADS, qk_width
    )
    latent_raw = jnp.dot(attn_in, w_latent, preferred_element_type=jnp.float32)
    latent = latent_raw[:, :KV_RANK]
    k_pe = latent_raw[:, KV_RANK:]
    latent_normed = normalized_rows(latent, g_latent.astype(jnp.float32)).astype(jnp.bfloat16)
    key_value = jnp.dot(latent_normed, w_expand, preferred_element_type=jnp.float32).reshape(
        tokens, HEADS, NOPE + VDIM
    )
    q_full = jnp.concatenate(
        [q_raw[..., :NOPE], rotate(q_raw[..., NOPE:], cosine[:, None, :], sine[:, None, :])],
        axis=-1,
    )
    k_rot = rotate(k_pe, cosine, sine)
    k_full = jnp.concatenate(
        [key_value[..., :NOPE], jnp.broadcast_to(k_rot[:, None, :], (tokens, HEADS, ROPE))], axis=-1
    )
    packed = jnp.concatenate([q_full, k_full], axis=-1).astype(jnp.bfloat16)
    values = key_value[..., NOPE:].astype(jnp.bfloat16)
    head_qk, head_v = (
        lax.all_to_all(packed, "seq", split_axis=1, concat_axis=0, tiled=True),
        lax.all_to_all(values, "seq", split_axis=1, concat_axis=0, tiled=True),
    )
    head_q = head_qk[..., :qk_width]
    head_k = head_qk[..., qk_width:]
    block_rows = min(512, group)
    block_count = group // block_rows
    positions = jnp.arange(group, dtype=jnp.int32)

    def block_scores(row_start):
        query_block = lax.dynamic_slice_in_dim(head_q, row_start, block_rows, 0)
        seg_query = lax.dynamic_slice_in_dim(seg_all, row_start, block_rows, 0)
        pos_query = row_start + jnp.arange(block_rows, dtype=jnp.int32)
        visible = (seg_query[:, None] == seg_all[None, :]) & (seg_query[:, None] >= 0) & (
            positions[None, :] <= pos_query[:, None]
        ) | (positions[None, :] == pos_query[:, None])
        scores = (
            jnp.einsum("qhd,khd->hqk", query_block, head_k, preferred_element_type=jnp.float32)
            * score_scale
        )
        return (query_block, jnp.where(visible[None], scores, MASKED))

    def forward_block(block_index):
        query_block, scores = block_scores(block_index * block_rows)
        row_peak = jnp.max(scores, axis=-1, keepdims=True)
        exponent = jnp.exp(scores - row_peak)
        row_total = jnp.sum(exponent, axis=-1, keepdims=True)
        soft = (exponent / row_total).astype(jnp.bfloat16)
        block_out = jnp.einsum("hqk,khd->qhd", soft, head_v, preferred_element_type=jnp.float32)
        return (block_out.astype(jnp.bfloat16), (row_peak + jnp.log(row_total))[..., 0])

    head_out, log_totals = lax.map(forward_block, jnp.arange(block_count))
    head_out = head_out.reshape(group, heads_dev, VDIM)
    token_out = lax.all_to_all(head_out, "seq", split_axis=0, concat_axis=1, tiled=True)
    flat_out = token_out.reshape(tokens, HEADS * VDIM)
    attn_out = jnp.dot(flat_out, w_output, preferred_element_type=jnp.float32)
    residual = x_float + attn_out
    ffn_in = normalized_rows(residual, g_ffn.astype(jnp.float32)).astype(jnp.bfloat16)
    logits = jnp.dot(ffn_in, w_router, preferred_element_type=jnp.float32)
    router_probs = jax.nn.softmax(logits, axis=-1)
    route_hot = (
        route_ids[:, :, None] == jnp.arange(experts, dtype=jnp.int32)[None, None, :]
    ).astype(jnp.float32)
    chosen = jnp.einsum("tje,te->tj", route_hot, router_probs, precision=HIGHEST)
    chosen_sum = jnp.sum(chosen, axis=-1, keepdims=True)
    route_gates = chosen / chosen_sum
    flat_route = route_ids.reshape(pair_count)
    pair_hot = (flat_route[:, None] == jnp.arange(experts, dtype=jnp.int32)[None, :]).astype(
        jnp.int32
    )
    running = jnp.cumsum(pair_hot, axis=0)
    pair_rank = jnp.sum((running - 1) * pair_hot, axis=1)
    expert_load = running[-1]
    all_load = lax.all_gather(expert_load[None, :], "seq", axis=0, tiled=True)
    earlier = jnp.cumsum(all_load, axis=0) - all_load
    mine_before = lax.dynamic_index_in_dim(earlier, rank_seq, 0, keepdims=False)
    pair_slot = jnp.sum(pair_hot * mine_before[None, :], axis=1) + pair_rank
    kept_mask = (pair_slot < CAP).astype(jnp.float32).reshape(tokens, TOP)
    send_at = flat_route * slot_most + pair_rank
    pair_ids = jnp.arange(pair_count, dtype=jnp.int32)
    pair_table = jnp.full((experts * slot_most,), pair_count, jnp.int32).at[send_at].set(pair_ids)
    token_table = jnp.where(pair_table < pair_count, pair_table // TOP, tokens)
    mine_load = lax.dynamic_slice_in_dim(all_load, rank_seq * EXP_DEV, EXP_DEV, 1)
    mine_start = jnp.cumsum(mine_load, axis=0) - mine_load
    mine_end = mine_start + mine_load
    slot_ids = jnp.arange(CAP, dtype=jnp.int32)
    source = jnp.sum((mine_end[:, :, None] <= slot_ids[None, None, :]).astype(jnp.int32), axis=0)
    filled = slot_ids[None, :] < mine_end[-1][:, None]
    source_hot = (source[None] == jnp.arange(seq_count, dtype=jnp.int32)[:, None, None]).astype(
        jnp.int32
    )
    source_start = jnp.sum(source_hot * mine_start[:, :, None], axis=0)
    within = slot_ids[None, :] - source_start
    local_expert = jnp.arange(EXP_DEV, dtype=jnp.int32)
    gather_at = jnp.where(
        filled,
        source * slab_rows + local_expert[:, None] * slot_most + within,
        seq_count * slab_rows,
    )
    row_rank = jnp.arange(slot_most, dtype=jnp.int32)
    back_slot = mine_start[:, :, None] + row_rank[None, None, :]
    back_ok = (row_rank[None, None, :] < mine_load[:, :, None]) & (back_slot < CAP)
    scatter_at = jnp.where(
        back_ok, local_expert[None, :, None] * CAP + back_slot, EXP_DEV * CAP
    ).reshape(seq_count, slab_rows)

    def to_send(row_block, table):
        padded = jnp.concatenate([row_block, jnp.zeros((1, width), row_block.dtype)], axis=0)
        return padded[table].reshape(seq_count, slab_rows, width)

    def compact(received):
        flat_rows = jnp.concatenate(
            [received.reshape(seq_count * slab_rows, width), jnp.zeros((1, width), received.dtype)],
            axis=0,
        )
        return flat_rows[gather_at]

    def spread(result):
        flat_rows = jnp.concatenate(
            [result.reshape(EXP_DEV * CAP, width), jnp.zeros((1, width), result.dtype)], axis=0
        )
        return flat_rows[scatter_at]

    def collect(returned):
        return (
            returned.reshape(experts * slot_most, width)[send_at]
            .astype(jnp.float32)
            .reshape(tokens, TOP, width)
        )

    arrived = lax.all_to_all(
        to_send(ffn_in, token_table), "seq", split_axis=0, concat_axis=0, tiled=True
    )
    expert_input_rows = compact(arrived)
    hidden_gate = jnp.einsum(
        "nmh,nhq->nmq", expert_input_rows, w_egate, preferred_element_type=jnp.float32
    )
    hidden_up_rows = jnp.einsum(
        "nmh,nhq->nmq", expert_input_rows, expert_up_weight, preferred_element_type=jnp.float32
    )
    expert_act = swiglu(hidden_gate, hidden_up_rows).astype(jnp.bfloat16)
    expert_out = jnp.einsum(
        "kcf,kfd->kcd", expert_act, w_edown, preferred_element_type=jnp.float32
    ).astype(jnp.bfloat16)
    returned = lax.all_to_all(spread(expert_out), "seq", split_axis=0, concat_axis=0, tiled=True)
    pair_out = collect(returned) * kept_mask[:, :, None]
    mixture_experts_output = jnp.sum(pair_out * route_gates[:, :, None], axis=1)
    side_gate = jnp.dot(ffn_in, w_sgate, preferred_element_type=jnp.float32)
    side_up = jnp.dot(ffn_in, w_sup, preferred_element_type=jnp.float32)
    side_act = swiglu(side_gate, side_up).astype(jnp.bfloat16)
    side_out = jnp.dot(side_act, w_sdown, preferred_element_type=jnp.float32)
    layer_out = (residual + side_out + mixture_experts_output).astype(jnp.bfloat16)
    side_grad = grad_out.astype(jnp.bfloat16)
    grad_sdown = jnp.einsum("tf,td->fd", side_act, side_grad, preferred_element_type=jnp.float32)
    d_side_act = jnp.einsum("td,fd->tf", side_grad, w_sdown, preferred_element_type=jnp.float32)
    _, side_pull = jax.vjp(swiglu, side_gate, side_up)
    d_side_gate, d_side_up = side_pull(d_side_act)
    d_side_gate = d_side_gate.astype(jnp.bfloat16)
    d_side_up = d_side_up.astype(jnp.bfloat16)
    grad_sgate = jnp.einsum("td,tf->df", ffn_in, d_side_gate, preferred_element_type=jnp.float32)
    grad_sup = jnp.einsum("td,tf->df", ffn_in, d_side_up, preferred_element_type=jnp.float32)
    d_ffn = jnp.einsum(
        "tf,df->td", d_side_gate, w_sgate, preferred_element_type=jnp.float32
    ) + jnp.einsum("tf,df->td", d_side_up, w_sup, preferred_element_type=jnp.float32)
    pair_grad = (
        ((kept_mask * route_gates)[:, :, None] * grad_out[:, None, :])
        .astype(jnp.bfloat16)
        .reshape(pair_count, width)
    )
    arrived_grad = lax.all_to_all(
        to_send(pair_grad, pair_table), "seq", split_axis=0, concat_axis=0, tiled=True
    )
    expert_grad = compact(arrived_grad)
    grad_edown = jnp.einsum(
        "kcf,kcd->kfd", expert_act, expert_grad, preferred_element_type=jnp.float32
    )
    d_expert_act = jnp.einsum(
        "kcd,kfd->kcf", expert_grad, w_edown, preferred_element_type=jnp.float32
    )
    _, expert_pull = jax.vjp(swiglu, hidden_gate, hidden_up_rows)
    d_hidden_gate, grad_hidden_up_rows = expert_pull(d_expert_act)
    d_hidden_gate = d_hidden_gate.astype(jnp.bfloat16)
    grad_hidden_up_rows = grad_hidden_up_rows.astype(jnp.bfloat16)
    grad_egate = jnp.einsum(
        "kcd,kcf->kdf", expert_input_rows, d_hidden_gate, preferred_element_type=jnp.float32
    )
    grad_expert_up_weight = jnp.einsum(
        "kcd,kcf->kdf", expert_input_rows, grad_hidden_up_rows, preferred_element_type=jnp.float32
    )
    d_expert_in = (
        jnp.einsum("sta,sra->str", d_hidden_gate, w_egate, preferred_element_type=jnp.float32)
        + jnp.einsum(
            "sta,sra->str",
            grad_hidden_up_rows,
            expert_up_weight,
            preferred_element_type=jnp.float32,
        )
    ).astype(jnp.bfloat16)
    back_in = lax.all_to_all(spread(d_expert_in), "seq", split_axis=0, concat_axis=0, tiled=True)
    d_moe_in = jnp.sum(collect(back_in) * kept_mask[:, :, None], axis=1)
    d_gate = jnp.sum(pair_out * grad_out[:, None, :], axis=-1)
    d_chosen = (d_gate - jnp.sum(d_gate * route_gates, axis=-1, keepdims=True)) / chosen_sum
    d_probs = jnp.einsum("tje,tj->te", route_hot, d_chosen, precision=HIGHEST)
    d_logits = router_probs * (d_probs - jnp.sum(router_probs * d_probs, axis=-1, keepdims=True))
    grad_router = jnp.einsum("td,te->de", ffn_in.astype(jnp.float32), d_logits, precision=HIGHEST)
    d_ffn = (
        d_ffn
        + jnp.einsum("te,de->td", d_logits, w_router.astype(jnp.float32), precision=HIGHEST)
        + d_moe_in
    )
    _, ffn_pull = jax.vjp(normalized_rows, residual, g_ffn.astype(jnp.float32))
    d_resid_part, grad_ffn_gain = ffn_pull(d_ffn)
    d_residual = grad_out + d_resid_part
    d_attn = d_residual.astype(jnp.bfloat16)
    grad_output = jnp.einsum("tc,td->cd", flat_out, d_attn, preferred_element_type=jnp.float32)
    d_head = jnp.einsum("td,cd->tc", d_attn, w_output, preferred_element_type=jnp.float32)
    d_head = d_head.reshape(tokens, HEADS, VDIM).astype(jnp.bfloat16)
    head_grad = lax.all_to_all(d_head, "seq", split_axis=1, concat_axis=0, tiled=True)

    def backward_block(carried, block_index):
        d_key, d_val = carried
        row_start = block_index * block_rows
        query_block, scores = block_scores(row_start)
        level = lax.dynamic_index_in_dim(log_totals, block_index, 0, keepdims=False)
        soft_float = jnp.exp(scores - level[..., None])
        soft = soft_float.astype(jnp.bfloat16)
        grad_block = lax.dynamic_slice_in_dim(head_grad, row_start, block_rows, 0)
        d_val = d_val + jnp.einsum(
            "hqk,qhd->khd", soft, grad_block, preferred_element_type=jnp.float32
        )
        d_prob = jnp.einsum("qhd,khd->hqk", grad_block, head_v, preferred_element_type=jnp.float32)
        d_score = (
            soft_float * (d_prob - jnp.sum(soft_float * d_prob, axis=-1, keepdims=True))
        ).astype(jnp.bfloat16)
        d_query = (
            jnp.einsum("hqk,khd->qhd", d_score, head_k, preferred_element_type=jnp.float32)
            * score_scale
        )
        d_key = (
            d_key
            + jnp.einsum("hqk,qhd->khd", d_score, query_block, preferred_element_type=jnp.float32)
            * score_scale
        )
        return ((d_key, d_val), d_query.astype(jnp.bfloat16))

    start_carry = (
        jnp.zeros((group, heads_dev, qk_width), jnp.float32),
        jnp.zeros((group, heads_dev, VDIM), jnp.float32),
    )
    (d_key, d_val), d_query = lax.scan(backward_block, start_carry, jnp.arange(block_count))
    d_query = d_query.reshape(group, heads_dev, qk_width)
    d_packed = jnp.concatenate([d_query, d_key.astype(jnp.bfloat16)], axis=-1)
    token_dqk, token_dv = (
        lax.all_to_all(d_packed, "seq", split_axis=0, concat_axis=1, tiled=True),
        lax.all_to_all(d_val.astype(jnp.bfloat16), "seq", split_axis=0, concat_axis=1, tiled=True),
    )
    dq_full = token_dqk[..., :qk_width].astype(jnp.float32)
    d_q_raw = jnp.concatenate(
        [dq_full[..., :NOPE], rotate(dq_full[..., NOPE:], cosine[:, None, :], -sine[:, None, :])],
        axis=-1,
    )
    d_q_raw = d_q_raw.astype(jnp.bfloat16).reshape(tokens, HEADS * qk_width)
    dk_rope = jnp.sum(token_dqk[..., qk_width + NOPE :].astype(jnp.float32), axis=1)
    d_k_pe = rotate(dk_rope, cosine, -sine)
    d_key_value = jnp.concatenate(
        [token_dqk[..., qk_width : qk_width + NOPE], token_dv], axis=-1
    ).reshape(tokens, HEADS * (NOPE + VDIM))
    grad_expand = jnp.einsum(
        "tr,tc->rc", latent_normed, d_key_value, preferred_element_type=jnp.float32
    )
    d_latent_normed = jnp.einsum(
        "tc,rc->tr", d_key_value, w_expand, preferred_element_type=jnp.float32
    )
    _, latent_pull = jax.vjp(normalized_rows, latent, g_latent.astype(jnp.float32))
    d_latent, grad_latent_gain = latent_pull(d_latent_normed)
    d_latent_raw = jnp.concatenate([d_latent, d_k_pe], axis=-1).astype(jnp.bfloat16)
    grad_query = jnp.einsum("td,tc->dc", attn_in, d_q_raw, preferred_element_type=jnp.float32)
    grad_latent = jnp.einsum("td,tc->dc", attn_in, d_latent_raw, preferred_element_type=jnp.float32)
    d_attn_in = jnp.einsum(
        "tc,dc->td", d_q_raw, w_query, preferred_element_type=jnp.float32
    ) + jnp.einsum("tc,dc->td", d_latent_raw, w_latent, preferred_element_type=jnp.float32)
    _, attn_pull = jax.vjp(normalized_rows, x_float, g_attn.astype(jnp.float32))
    d_x_part, grad_attn_gain = attn_pull(d_attn_in)
    grad_inputs = d_residual + d_x_part
    dense_grads = (
        grad_attn_gain,
        grad_query,
        grad_latent,
        grad_latent_gain,
        grad_expand,
        grad_output,
        grad_ffn_gain,
        grad_router,
        grad_sgate,
        grad_sup,
        grad_sdown,
    )
    shards = (
        lax.psum_scatter(
            dense_grads[0].astype(jnp.bfloat16), "dp", scatter_dimension=0, tiled=True
        ).astype(jnp.float32),
        lax.psum_scatter(
            dense_grads[1].astype(jnp.bfloat16), "dp", scatter_dimension=0, tiled=True
        ).astype(jnp.float32),
        lax.psum_scatter(
            dense_grads[2].astype(jnp.bfloat16), "dp", scatter_dimension=0, tiled=True
        ).astype(jnp.float32),
        lax.psum_scatter(
            dense_grads[3].astype(jnp.bfloat16), "dp", scatter_dimension=0, tiled=True
        ).astype(jnp.float32),
        lax.psum_scatter(
            dense_grads[4].astype(jnp.bfloat16), "dp", scatter_dimension=0, tiled=True
        ).astype(jnp.float32),
        lax.psum_scatter(
            dense_grads[5].astype(jnp.bfloat16), "dp", scatter_dimension=0, tiled=True
        ).astype(jnp.float32),
        lax.psum_scatter(
            dense_grads[6].astype(jnp.bfloat16), "dp", scatter_dimension=0, tiled=True
        ).astype(jnp.float32),
        lax.psum_scatter(
            dense_grads[7].astype(jnp.bfloat16), "dp", scatter_dimension=0, tiled=True
        ).astype(jnp.float32),
        lax.psum_scatter(
            dense_grads[8].astype(jnp.bfloat16), "dp", scatter_dimension=0, tiled=True
        ).astype(jnp.float32),
        lax.psum_scatter(
            dense_grads[9].astype(jnp.bfloat16), "dp", scatter_dimension=0, tiled=True
        ).astype(jnp.float32),
        lax.psum_scatter(
            dense_grads[10].astype(jnp.bfloat16), "dp", scatter_dimension=0, tiled=True
        ).astype(jnp.float32),
        lax.psum_scatter(
            grad_egate.astype(jnp.bfloat16), "dp", scatter_dimension=1, tiled=True
        ).astype(jnp.float32),
        lax.psum_scatter(
            grad_expert_up_weight.astype(jnp.bfloat16), "dp", scatter_dimension=1, tiled=True
        ).astype(jnp.float32),
        lax.psum_scatter(
            grad_edown.astype(jnp.bfloat16), "dp", scatter_dimension=2, tiled=True
        ).astype(jnp.float32),
    )
    dense_sums = (
        lax.psum(shards[0].astype(jnp.bfloat16), "seq").astype(jnp.float32),
        lax.psum(shards[1].astype(jnp.bfloat16), "seq").astype(jnp.float32),
        lax.psum(shards[2].astype(jnp.bfloat16), "seq").astype(jnp.float32),
        lax.psum(shards[3].astype(jnp.bfloat16), "seq").astype(jnp.float32),
        lax.psum(shards[4].astype(jnp.bfloat16), "seq").astype(jnp.float32),
        lax.psum(shards[5].astype(jnp.bfloat16), "seq").astype(jnp.float32),
        lax.psum(shards[6].astype(jnp.bfloat16), "seq").astype(jnp.float32),
        lax.psum(shards[7].astype(jnp.bfloat16), "seq").astype(jnp.float32),
        lax.psum(shards[8].astype(jnp.bfloat16), "seq").astype(jnp.float32),
        lax.psum(shards[9].astype(jnp.bfloat16), "seq").astype(jnp.float32),
        lax.psum(shards[10].astype(jnp.bfloat16), "seq").astype(jnp.float32),
    )
    return (
        layer_out[None],
        grad_inputs[None],
        dense_sums[0],
        dense_sums[1],
        dense_sums[2],
        dense_sums[3],
        dense_sums[4],
        dense_sums[5],
        dense_sums[6],
        dense_sums[7],
        dense_sums[8],
        dense_sums[9],
        dense_sums[10],
        shards[11],
        shards[12],
        shards[13],
    )


def solution(mesh):
    placed = (
        P("dp", "seq", None),
        P("dp", None),
        P("dp", "seq", None),
        P("dp", "seq", None),
        P("dp"),
        P("dp", None),
        P("dp", None),
        P("dp"),
        P("dp", None),
        P("dp", None),
        P("dp"),
        P("dp", None),
        P("dp", None),
        P("dp", None),
        P("dp", None),
        P("seq", "dp", None),
        P("seq", "dp", None),
        P("seq", None, "dp"),
    )
    return jax.shard_map(
        local,
        mesh=mesh,
        in_specs=placed,
        out_specs=(
            P("dp", "seq", None),
            P("dp", "seq", None),
            P("dp"),
            P("dp", None),
            P("dp", None),
            P("dp"),
            P("dp", None),
            P("dp", None),
            P("dp"),
            P("dp", None),
            P("dp", None),
            P("dp", None),
            P("dp", None),
            P("seq", "dp", None),
            P("seq", "dp", None),
            P("seq", None, "dp"),
        ),
        check_vma=False,
    )
```

profile of v0, /device:TPU:0, one launch (start us, length us, event | category | flops | bytes accessed | tf_op | source)
XLA Modules:
  0.0 2596.8 jit_solution(4560087902232468192)
XLA Ops:
  31.9 18.0 all-gather.17.cloned.1.call-done
  52.6 51.9 %all-gather.19.cloned.1.call-done = bf16[512,4096]{1,0:T(8,128)(2,1)} async-done(((bf16[128,4096]{1,0:T(8,128)(2,1)}), bf16[512,4096]{1,0:T(8,128)(2,1)}) %all-gather.19.cloned.1.call-update) | async-done | bytes 4194320 | tf_op jit(solution)/shard_map/all_gather | solution.py:83
  108.2 120.7 %all-gather.15.cloned.1.call-done = bf16[2048,3072]{1,0:T(8,128)(2,1)} async-done(((bf16[512,3072]{1,0:T(8,128)(2,1)}), bf16[2048,3072]{1,0:T(8,128)(2,1)}) %all-gather.15.cloned.1.call-update) | async-done | bytes 12582928 | tf_op jit(solution)/shard_map/all_gather | solution.py:80
  228.9 16.9 copy.151
  288.8 22.2 all-gather.3
  363.3 70.5 %all-gather.23.cloned.1.call-done = bf16[2048,2816]{1,0:T(8,128)(2,1)} async-done(((bf16[512,2816]{1,0:T(8,128)(2,1)}), bf16[2048,2816]{1,0:T(8,128)(2,1)}) %all-gather.23.cloned.1.call-update) | async-done | bytes 11534352 | tf_op jit(solution)/shard_map/all_gather | solution.py:87
  440.9 108.5 %all-gather.25.cloned.1.call-done = bf16[2048,2816]{1,0:T(8,128)(2,1)} async-done(((bf16[512,2816]{1,0:T(8,128)(2,1)}), bf16[2048,2816]{1,0:T(8,128)(2,1)}) %all-gather.25.cloned.1.call-update) | async-done | bytes 11534352 | tf_op jit(solution)/shard_map/all_gather | solution.py:88
  556.4 108.6 %all-gather.27.cloned.1.call-done = bf16[2816,2048]{1,0:T(8,128)(2,1)} async-done(((bf16[704,2048]{1,0:T(8,128)(2,1)}), bf16[2816,2048]{1,0:T(8,128)(2,1)}) %all-gather.27.cloned.1.call-update) | async-done | bytes 11534352 | tf_op jit(solution)/shard_map/all_gather | solution.py:89
  719.0 131.9 %all-to-all-done.5 = bf16[8,192,2048]{2,1,0:T(8,128)(2,1)} async-done(((bf16[8,192,2048]{2,1,0:T(8,128)(2,1)}), bf16[8,192,2048]{2,1,0:T(8,128)(2,1)}, u32[]{:S(2)}, u32[]{:S(2)}) %all-to-all-start.5) | async-done | bytes 6291488 | tf_op jit(solution)/shard_map/all_to_all | solution.py:287
  870.2 124.5 %all-to-all-done.3 = bf16[8,192,2048]{2,1,0:T(8,128)(2,1)} async-done(((bf16[8,192,2048]{2,1,0:T(8,128)(2,1)}), bf16[8,192,2048]{2,1,0:T(8,128)(2,1)}, u32[]{:S(2)}, u32[]{:S(2)}) %all-to-all-start.3) | async-done | bytes 6291488 | tf_op jit(solution)/shard_map/all_to_all | solution.py:248
  1052.4 17.4 multiply_convert_fusion.2
  1097.1 15.4 gather_fusion.6
  1144.3 112.2 %all-to-all-done.6 = bf16[8,192,2048]{2,1,0:T(8,128)(2,1)} async-done(((bf16[8,192,2048]{2,1,0:T(8,128)(2,1)}), bf16[8,192,2048]{2,1,0:T(8,128)(2,1)}, u32[]{:S(2)}, u32[]{:S(2)}) %all-to-all-start.6) | async-done | bytes 6291488 | tf_op jit(solution)/shard_map/all_to_all | solution.py:316
  1299.6 100.8 %all-to-all-done.4 = bf16[8,192,2048]{2,1,0:T(8,128)(2,1)} async-done(((bf16[8,192,2048]{2,1,0:T(8,128)(2,1)}), bf16[8,192,2048]{2,1,0:T(8,128)(2,1)}, u32[]{:S(2)}, u32[]{:S(2)}) %all-to-all-start.4) | async-done | bytes 6291488 | tf_op jit(solution)/shard_map/all_to_all | solution.py:262
  1458.0 44.0 %while.31 = (s32[]{:T(128)}, f32[1024,2,192]{0,2,1:T(8,128)}, f32[1024,2,128]{0,2,1:T(8,128)}, bf16[2,512,2,192]{1,3,2,0:T(8,128)(2,1)}, s32[2]{0:T(128)S(1)}, /...) while((s32[]{:T(128)}, f32[1024,2,192]{0,2,1:T(8,128)}, ...), condition=%wide.region_27.28_spmd.clone.clone, body=%wide.region_25.27_spmd.clone.clone.sunk | while | flops 1765801984 | bytes 88780272 | solution.py:367
  1527.3 37.2 %all-to-all-done.8 = bf16[1024,2,384]{2,1,0:T(2,128)(2,1)S(1)} async-done(((bf16[1024,2,384]{2,1,0:T(2,128)(2,1)}), bf16[1024,2,384]{2,1,0:T(2,128)(2,1)S(1)}, u32[]{:S(2)}, u32[]{:S(2)}) %all-to-all-start.8) | async-done | bytes 1572896 | tf_op jit(solution)/shard_map/all_to_all | solution.py:371
  1633.3 34.0 %reduce-scatter.16.cloned.1.call-done = bf16[128,4096]{1,0:T(8,128)(2,1)} async-done(((bf16[512,4096]{1,0:T(8,128)(2,1)}), bf16[128,4096]{1,0:T(8,128)(2,1)}) %reduce-scatter.16.cloned.1.call-update) | async-done | bytes 1048592 | tf_op jit(solution)/shard_map/reduce_scatter | solution.py:428
  1667.3 89.6 %reduce-scatter.18.cloned.1.call-done = bf16[512,2048]{1,0:T(8,128)(2,1)} async-done(((bf16[2048,2048]{1,0:T(8,128)(2,1)}), bf16[512,2048]{1,0:T(8,128)(2,1)}) %reduce-scatter.18.cloned.1.call-update) | async-done | bytes 2097168 | tf_op jit(solution)/shard_map/reduce_scatter | solution.py:431
  1757.0 123.7 %reduce-scatter.12.cloned.1.call-done = bf16[512,3072]{1,0:T(8,128)(2,1)} async-done(((bf16[2048,3072]{1,0:T(8,128)(2,1)}), bf16[512,3072]{1,0:T(8,128)(2,1)}) %reduce-scatter.12.cloned.1.call-update) | async-done | bytes 3145744 | tf_op jit(solution)/shard_map/reduce_scatter | solution.py:419
  1910.9 27.1 %all-reduce.9 = (bf16[512]{0:T(512)(128)(2,1)S(1)}, bf16[128]{0:T(256)(128)(2,1)S(1)}, bf16[512]{0:T(512)(128)(2,1)S(1)}, bf16[512,16]{0,1:T(8,128)(2,1)S(1)}) all-reduce(bf16[512]{0:T(512)(128)(2,1)S(1)} %dynamic-slice.2, bf16[128]{0:T(256)(128)(2,1)S(1)} %dynamic-slice.4, ...), channel_id=1, replica_groups=mesh['seq'=8,'dp'=4] {'seq'}, use_global_device_ids=true, to_apply=%region_33.34 | all-reduce | flops 9344 | bytes 37376 | tf_op jit(solution)/shard_map/psum | solution.py:460
  1942.9 80.2 %reduce-scatter.32.cloned.1.call-done = bf16[2,1408,512]{2,1,0:T(8,128)(2,1)} async-done(((bf16[2,1408,2048]{2,1,0:T(8,128)(2,1)}), bf16[2,1408,512]{2,1,0:T(8,128)(2,1)}) %reduce-scatter.32.cloned.1.call-update) | async-done | bytes 2883600 | tf_op jit(solution)/shard_map/reduce_scatter | solution.py:455
  2028.3 110.3 %reduce-scatter.28.cloned.1.call-done = bf16[2,512,1408]{2,1,0:T(8,128)(2,1)} async-done(((bf16[2,2048,1408]{2,1,0:T(8,128)(2,1)}), bf16[2,512,1408]{2,1,0:T(8,128)(2,1)}) %reduce-scatter.28.cloned.1.call-update) | async-done | bytes 2883600 | tf_op jit(solution)/shard_map/reduce_scatter | solution.py:449
  2143.3 110.9 %reduce-scatter.30.cloned.1.call-done = bf16[2,512,1408]{2,1,0:T(8,128)(2,1)} async-done(((bf16[2,2048,1408]{2,1,0:T(8,128)(2,1)}), bf16[2,512,1408]{2,1,0:T(8,128)(2,1)}) %reduce-scatter.30.cloned.1.call-update) | async-done | bytes 2883600 | tf_op jit(solution)/shard_map/reduce_scatter | solution.py:452
  2258.8 310.9 %all-reduce.14.cloned.1.call-done = (bf16[512,3072]{1,0:T(8,128)(2,1)}, bf16[512,576]{0,1:T(8,128)(2,1)}, bf16[128,4096]{1,0:T(8,128)(2,1)}, bf16[512,2048]{1,0:...) async-done(((bf16[512,3072]{1,0:T(8,128)(2,1)}, bf16[512,576]{0,1:T(8,128)(2,1)}, bf16[128,4096]{1,0:T(8,128)(2,1)}, ...) | async-done | bytes 15532048 | tf_op jit(solution)/shard_map/psum | solution.py:461
  (526 shorter events, 643.2 us)
Async XLA Ops:
  7.9 96.6 %all-gather.19.cloned.1.call-start = ((), (), s32[]{:S(2)}) async-start(), calls=%async_computation.23 | async-start | bytes 5242880 | tf_op jit(solution)/shard_map/all_gather | solution.py:83
  8.7 220.3 %all-gather.15.cloned.1.call-start = ((), (), s32[]{:S(2)}) async-start(), calls=%async_computation.21 | async-start | bytes 15728640 | tf_op jit(solution)/shard_map/all_gather | solution.py:80
  9.4 347.8 %all-gather.21.cloned.1.call-start = ((), (), s32[]{:S(2)}) async-start(), calls=%async_computation.24 | async-start | bytes 10485760 | tf_op jit(solution)/shard_map/all_gather | solution.py:84
  10.0 423.9 %all-gather.23.cloned.1.call-start = ((), (), s32[]{:S(2)}) async-start(), calls=%async_computation.25 | async-start | bytes 14417920 | tf_op jit(solution)/shard_map/all_gather | solution.py:87
  10.6 538.8 %all-gather.25.cloned.1.call-start = ((), (), s32[]{:S(2)}) async-start(), calls=%async_computation.26 | async-start | bytes 14417920 | tf_op jit(solution)/shard_map/all_gather | solution.py:88
  11.1 653.9 %all-gather.27.cloned.1.call-start = ((), (), s32[]{:S(2)}) async-start(), calls=%async_computation.27 | async-start | bytes 14417920 | tf_op jit(solution)/shard_map/all_gather | solution.py:89
  11.9 1014.0 %all-gather.29.cloned.1.call-start = ((), (), s32[]{:S(2)}) async-start(), calls=%async_computation.28 | async-start | bytes 14417920 | tf_op jit(solution)/shard_map/all_gather | solution.py:90
  12.7 1026.5 %all-gather.31.cloned.1.call-start = ((), (), s32[]{:S(2)}) async-start(), calls=%async_computation.29 | async-start | bytes 14417920 | tf_op jit(solution)/shard_map/all_gather | solution.py:91
  13.4 1039.0 %all-gather.33.cloned.1.call-start = ((), (), s32[]{:S(2)}) async-start(), calls=%async_computation.30 | async-start | bytes 14417920 | tf_op jit(solution)/shard_map/all_gather | solution.py:92
  340.3 1292.9 %reduce-scatter.22.cloned.1.call-start = ((), (), s32[]{:S(2)}) async-start(), calls=%async_computation.36 | async-start | bytes 14417920 | tf_op jit(solution)/shard_map/reduce_scatter | solution.py:440
  707.0 143.9 %all-to-all-start.5 = ((bf16[8,192,2048]{2,1,0:T(8,128)(2,1)}), bf16[8,192,2048]{2,1,0:T(8,128)(2,1)}, u32[]{:S(2)}, u32[]{:S(2)}) async-start(bf16[8,192,2048]{2,1,0:T(8,128)(2,1)} %bitcast.290), calls=%async_computation.5 | async-start | bytes 12582912 | tf_op jit(solution)/shard_map/all_to_all | solution.py:287
  850.9 143.8 %all-to-all-start.3 = ((bf16[8,192,2048]{2,1,0:T(8,128)(2,1)}), bf16[8,192,2048]{2,1,0:T(8,128)(2,1)}, u32[]{:S(2)}, u32[]{:S(2)}) async-start(bf16[8,192,2048]{2,1,0:T(8,128)(2,1)} %bitcast.287), calls=%async_computation.3 | async-start | bytes 12582912 | tf_op jit(solution)/shard_map/all_to_all | solution.py:248
  855.7 777.5 %reduce-scatter.24.cloned.1.call-start = ((), (), s32[]{:S(2)}) async-start(), calls=%async_computation.37 | async-start | bytes 14417920 | tf_op jit(solution)/shard_map/reduce_scatter | solution.py:443
  1112.5 144.0 %all-to-all-start.6 = ((bf16[8,192,2048]{2,1,0:T(8,128)(2,1)}), bf16[8,192,2048]{2,1,0:T(8,128)(2,1)}, u32[]{:S(2)}, u32[]{:S(2)}) async-start(bf16[8,192,2048]{2,1,0:T(8,128)(2,1)} %bitcast.289), calls=%async_computation.6 | async-start | bytes 12582912 | tf_op jit(solution)/shard_map/all_to_all | solution.py:316
  1256.5 143.9 %all-to-all-start.4 = ((bf16[8,192,2048]{2,1,0:T(8,128)(2,1)}), bf16[8,192,2048]{2,1,0:T(8,128)(2,1)}, u32[]{:S(2)}, u32[]{:S(2)}) async-start(bf16[8,192,2048]{2,1,0:T(8,128)(2,1)} %bitcast.288), calls=%async_computation.4 | async-start | bytes 12582912 | tf_op jit(solution)/shard_map/all_to_all | solution.py:262
  1261.4 371.9 %reduce-scatter.26.cloned.1.call-start = ((), (), s32[]{:S(2)}) async-start(), calls=%async_computation.38 | async-start | bytes 14417920 | tf_op jit(solution)/shard_map/reduce_scatter | solution.py:446
  1526.8 106.6 %reduce-scatter.14.cloned.1.call-start = ((), (), s32[]{:S(2)}) async-start(), calls=%async_computation.32 | async-start | bytes 2949120 | tf_op jit(solution)/shard_map/reduce_scatter | solution.py:422
  1581.4 175.6 %reduce-scatter.18.cloned.1.call-start = ((), (), s32[]{:S(2)}) async-start(), calls=%async_computation.34 | async-start | bytes 10485760 | tf_op jit(solution)/shard_map/reduce_scatter | solution.py:431
  1587.3 293.4 %reduce-scatter.12.cloned.1.call-start = ((), (), s32[]{:S(2)}) async-start(), calls=%async_computation.31 | async-start | bytes 15728640 | tf_op jit(solution)/shard_map/reduce_scatter | solution.py:419
  1595.6 315.3 %reduce-scatter.20.cloned.1.call-start = ((), (), s32[]{:S(2)}) async-start(), calls=%async_computation.35 | async-start | bytes 81920 | tf_op jit(solution)/shard_map/reduce_scatter | solution.py:437
  1597.6 425.5 %reduce-scatter.32.cloned.1.call-start = ((), (), s32[]{:S(2)}) async-start(), calls=%async_computation.41 | async-start | bytes 14417920 | tf_op jit(solution)/shard_map/reduce_scatter | solution.py:455
  1609.1 529.4 %reduce-scatter.28.cloned.1.call-start = ((), (), s32[]{:S(2)}) async-start(), calls=%async_computation.39 | async-start | bytes 14417920 | tf_op jit(solution)/shard_map/reduce_scatter | solution.py:449
  1621.1 633.1 %reduce-scatter.30.cloned.1.call-start = ((), (), s32[]{:S(2)}) async-start(), calls=%async_computation.40 | async-start | bytes 14417920 | tf_op jit(solution)/shard_map/reduce_scatter | solution.py:452
  1633.2 936.5 %all-reduce.14.cloned.1.call-start = ((), (), s32[]{:S(2)}) async-start(), calls=%async_computation.42 | async-start | bytes 31064064 | tf_op jit(solution)/shard_map/psum | solution.py:461
  (120 other events, 4362.8 us)
Sparse Core Ops, SparseCore 0:
  9.8 40.0 all-gather.16
  51.8 52.6 all-gather.18
  106.4 122.5 all-gather.14
  230.6 87.6 all-gather.20
  320.0 113.7 all-gather.22
  435.5 113.7 all-gather.24
  551.2 113.7 all-gather.26
  666.9 114.3 all-gather.28
  783.1 113.7 all-gather.30
  898.6 113.6 all-gather.32
  1015.4 112.1 reduce-scatter.21
  1130.5 112.0 reduce-scatter.23
  1267.8 111.5 reduce-scatter.25
  1576.8 34.3 reduce-scatter.13
  1614.6 52.6 reduce-scatter.15
  1670.5 86.3 reduce-scatter.17
  1759.9 120.7 reduce-scatter.11
  1883.8 23.6 reduce-scatter.19
  1910.9 112.1 reduce-scatter.31
  2026.4 112.1 reduce-scatter.27
  2141.9 112.1 reduce-scatter.29
  2257.3 312.3 all-reduce.13
where the time goes:
time: 2600 us
  waiting for transfers between devices  1890 us (73%)
  matrix products  279 us (11%)
  local copies, waits for them, and re-layouts  187 us (7%)
  blocking collectives  92.8 us (4%)
  other arithmetic  71.5 us (3%)
  starting transfers between devices  47.2 us (2%)
    psum x1, waiting for transfers between devices, local(): lax.psum(shards[1].astype(jnp.bfloat16), 'seq').astype(jnp.float32)  311 us
    all_to_all x1, waiting for transfers between devices, local(): lax.all_to_all(to_send(pair_grad, pair_table), 'seq', split_axis=0, conca...  132 us
    all_to_all x1, waiting for transfers between devices, local(): lax.all_to_all(to_send(ffn_in, token_table), 'seq', split_axis=0, concat_...  124 us
    reduce_scatter x1, waiting for transfers between devices, local(): lax.psum_scatter(dense_grads[1].astype(jnp.bfloat16), 'dp', scatter_dimen...  124 us
    all_gather x1, waiting for transfers between devices, local(): lax.all_gather(query_weight, 'dp', axis=0, tiled=True)  121 us
    all_to_all x1, waiting for transfers between devices, local(): lax.all_to_all(spread(d_expert_in), 'seq', split_axis=0, concat_axis=0, t...  112 us
    reduce_scatter x1, waiting for transfers between devices, local(): lax.psum_scatter(grad_expert_up_weight.astype(jnp.bfloat16), 'dp', scatte...  111 us
    reduce_scatter x1, waiting for transfers between devices, local(): lax.psum_scatter(grad_egate.astype(jnp.bfloat16), 'dp', scatter_dimension...  110 us
  transfers between devices with their start and end apart: 32, of which 23 were waited for; matrix products, arithmetic and copies ran while one was open for 20% of the time, Pallas kernels for 0%

commit v1 on v0

v1 whole, which is shorter than its diff:
```python
import math

import jax
import jax.numpy as jnp
from jax import lax
from jax.sharding import PartitionSpec as P

HEADS = 16
NOPE = 128
ROPE = 64
VDIM = 128
KV_RANK = 512
TOP = 6
EXP_DEV = 2
CAP = 480

EPSILON = 1e-06
MASKED = -1e30
HIGHEST = lax.Precision.HIGHEST
F32 = jnp.float32
BF16 = jnp.bfloat16
QK = NOPE + ROPE


def normalized_rows(values, gain):
    return values * lax.rsqrt(jnp.mean(values * values, axis=-1, keepdims=True) + EPSILON) * gain


def norm_backward(values, gain, upstream):
    scale = lax.rsqrt(jnp.mean(values * values, axis=-1, keepdims=True) + EPSILON)
    normed = values * scale
    weighted = upstream * gain
    d_values = scale * (weighted - normed * jnp.mean(weighted * normed, axis=-1, keepdims=True))
    return d_values, jnp.sum(upstream * normed, axis=0)


def angles(positions, width):
    frequency = 10000.0 ** (-(2.0 * jnp.arange(width // 2, dtype=F32)) / width)
    turned = positions.astype(F32)[:, None] * frequency[None, :]
    return (jnp.cos(turned), jnp.sin(turned))


def rotate(values, cosine, sine):
    half_width = values.shape[-1] // 2
    lower_half = values[..., :half_width]
    upper_half = values[..., half_width:]
    return jnp.concatenate(
        [lower_half * cosine - upper_half * sine, upper_half * cosine + lower_half * sine], axis=-1
    )


def swiglu(gate_portion, up_part):
    return jax.nn.silu(gate_portion) * up_part


def dot(left, right):
    return jnp.dot(left, right, preferred_element_type=F32)


def dot_t(left, right):
    return lax.dot_general(left, right, (((1,), (1,)), ((), ())), preferred_element_type=F32)


def t_dot(left, right):
    return lax.dot_general(left, right, (((0,), (0,)), ((), ())), preferred_element_type=F32)


def swap(value, axis, mask):
    count = lax.axis_size(axis)
    return lax.ppermute(value, axis, [(i, i ^ mask) for i in range(count)])


def flip_blocks(value, index, bit, axis):
    shape = value.shape
    count = shape[axis]
    step = 1 << bit
    split = value.reshape(shape[:axis] + (count // (2 * step), 2, step) + shape[axis + 1 :])
    flipped = jnp.flip(split, axis + 1).reshape(shape)
    return jnp.where(((index >> bit) & 1) == 1, flipped, value)


def xor_order(value, index, axis):
    for bit in range(value.shape[axis].bit_length() - 1):
        value = flip_blocks(value, index, bit, axis)
    return value


def to_own_order(value, me):
    count = value.shape[0]
    pairs = xor_order(value, me, 0).reshape((count // 2, 2) + value.shape[1:])
    return jnp.swapaxes(pairs, 0, 1).reshape(value.shape)


def from_own_order(value, me):
    count = value.shape[0]
    pairs = jnp.swapaxes(value.reshape((2, count // 2) + value.shape[1:]), 0, 1)
    return xor_order(pairs.reshape(value.shape), me, 0)


def own_masks():
    chips = lax.axis_size("seq") // 2
    return [2 * k + c for c in range(2) for k in range(chips)]


def gather_seq(block):
    chips = lax.axis_size("seq") // 2
    half = jnp.concatenate([block] + [swap(block, "seq", 2 * k) for k in range(1, chips)], axis=0)
    return jnp.concatenate([half, swap(half, "seq", 1)], axis=0)


def scatter_seq(partial):
    chips = lax.axis_size("seq") // 2
    half = partial.shape[0] // 2
    tokens = half // chips
    mine = partial.astype(BF16)
    peer = swap(mine[half:], "seq", 1)
    total = mine[:half].astype(F32) + peer.astype(F32)
    sent = total.astype(BF16)
    result = total[:tokens]
    for k in range(1, chips):
        result = result + swap(sent[k * tokens : (k + 1) * tokens], "seq", 2 * k).astype(F32)
    return result


def exchange_seq(blocks):
    return jnp.stack(
        [blocks[r] if m == 0 else swap(blocks[r], "seq", m) for r, m in enumerate(own_masks())]
    )


def gather_dp(value, axis):
    return lax.all_gather(value, "dp", axis=axis, tiled=True)


def reduce_dp(value, axis):
    return lax.psum_scatter(value.astype(BF16), "dp", scatter_dimension=axis, tiled=True)


def token_gradient(rows_in, upstream, d_rank):
    parts = lax.axis_size("dp")
    width = rows_in.shape[1] // parts
    lefts, rights = [], []
    for p in range(parts):
        piece = lax.dynamic_slice_in_dim(rows_in, (d_rank ^ p) * width, width, 1)
        lefts.append(piece if p == 0 else swap(piece, "dp", p))
        rights.append(upstream if p == 0 else swap(upstream, "dp", p))
    partial = t_dot(jnp.concatenate(lefts, axis=0), jnp.concatenate(rights, axis=0))
    return lax.psum(partial.astype(BF16), "seq").astype(F32)


def local(
    inputs,
    segments,
    routes,
    cotangent,
    attention_gain,
    query_weight,
    latent_weight,
    latent_gain,
    expand_weight,
    output_weight,
    feedforward_gain,
    router_weight,
    shared_gate,
    shared_up,
    shared_down,
    expert_gate,
    expert_up,
    expert_down,
):
    seq_count = lax.axis_size("seq")
    dp_count = lax.axis_size("dp")
    me = lax.axis_index("seq")
    d_rank = lax.axis_index("dp")
    tokens = inputs.shape[1]
    width = inputs.shape[2]
    group = tokens * seq_count
    experts = EXP_DEV * seq_count
    heads_dev = HEADS // seq_count
    score_scale = 1.0 / math.sqrt(QK)
    shard = width // dp_count

    small = gather_dp(
        jnp.concatenate(
            [attention_gain, feedforward_gain, latent_gain, router_weight.reshape(-1)]
        ).reshape(1, -1),
        0,
    )
    g_attn = small[:, :shard].reshape(width).astype(F32)
    g_ffn = small[:, shard : 2 * shard].reshape(width).astype(F32)
    rank_shard = latent_gain.shape[0]
    g_latent = small[:, 2 * shard : 2 * shard + rank_shard].reshape(KV_RANK).astype(F32)
    w_router = small[:, 2 * shard + rank_shard :].reshape(width, experts)

    hq = heads_dev * QK
    hkv = heads_dev * (NOPE + VDIM)
    x_all = gather_seq(inputs[0])
    w_query = gather_dp(lax.dynamic_slice_in_dim(query_weight, me * hq, hq, 1), 0)
    w_latent = gather_dp(latent_weight, 0)
    w_expand = gather_dp(lax.dynamic_slice_in_dim(expand_weight, me * hkv, hkv, 1), 0)
    core = me & 1
    out_half = output_weight.shape[0] // 2
    out_mine = gather_dp(
        lax.dynamic_slice_in_dim(output_weight, core * out_half, out_half, 0)[None], 0
    )
    out_peer = swap(out_mine, "seq", 1)
    w_output = jnp.where(
        core == 0,
        jnp.stack([out_mine, out_peer], axis=1),
        jnp.stack([out_peer, out_mine], axis=1),
    ).reshape(width, width)

    g_all = gather_seq(cotangent[0])
    w_egate = gather_dp(expert_gate, 1)
    w_eup = gather_dp(expert_up, 1)
    w_edown = gather_dp(expert_down, 2)
    hidden = shared_gate.shape[1]
    unit = hidden // (dp_count * seq_count)

    def columns_of(weight):
        split = weight.reshape(weight.shape[0], dp_count, seq_count, unit)
        mine = lax.dynamic_index_in_dim(split, me, 2, keepdims=False)
        return mine.reshape(weight.shape[0], dp_count * unit)

    w_sgate = gather_dp(columns_of(shared_gate), 0)
    w_sup = gather_dp(columns_of(shared_up), 0)
    w_sdown = gather_dp(
        lax.dynamic_slice_in_dim(shared_down, me * unit, unit, 0)[None], 0
    ).reshape(dp_count * unit, width)

    ranks = me ^ jnp.array(own_masks(), jnp.int32)
    positions = (ranks[:, None] * tokens + jnp.arange(tokens, dtype=jnp.int32)[None, :]).reshape(
        group
    )
    seg_all = to_own_order(segments[0].reshape(seq_count, tokens), me).reshape(group)
    cosine, sine = angles(positions, ROPE)
    routes_abs = lax.all_gather(routes[0], "seq", axis=0, tiled=True)
    my_experts = me * EXP_DEV + jnp.arange(EXP_DEV, dtype=jnp.int32)
    hit_abs = jnp.any(routes_abs[None] == my_experts[:, None, None], axis=-1).astype(jnp.int32)
    slot_abs = jnp.where(hit_abs == 1, jnp.cumsum(hit_abs, axis=1) - hit_abs, CAP)
    slot_own = jnp.swapaxes(
        to_own_order(jnp.swapaxes(slot_abs.reshape(EXP_DEV, seq_count, tokens), 0, 1), me), 0, 1
    ).reshape(EXP_DEV, group)
    routes_own = to_own_order(routes_abs.reshape(seq_count, tokens, TOP), me).reshape(group, TOP)
    expert_ids = jnp.arange(experts, dtype=jnp.int32)
    route_hot = jnp.any(routes_own[:, :, None] == expert_ids[None, None, :], axis=1)
    placed = slot_own[:, None, :] == jnp.arange(CAP, dtype=jnp.int32)[None, :, None]
    dispatch = placed.astype(BF16).reshape(EXP_DEV * CAP, group)

    attn_in = normalized_rows(x_all.astype(F32), g_attn).astype(BF16)
    q_raw = dot(attn_in, w_query).reshape(group, heads_dev, QK)
    latent_raw = dot(attn_in, w_latent)
    latent = latent_raw[:, :KV_RANK]
    latent_normed = normalized_rows(latent, g_latent).astype(BF16)
    key_value = dot(latent_normed, w_expand).reshape(group, heads_dev, NOPE + VDIM)
    q_full = jnp.concatenate(
        [q_raw[..., :NOPE], rotate(q_raw[..., NOPE:], cosine[:, None, :], sine[:, None, :])],
        axis=-1,
    ).astype(BF16)
    k_rot = rotate(latent_raw[:, KV_RANK:], cosine, sine)
    k_full = jnp.concatenate(
        [key_value[..., :NOPE], jnp.broadcast_to(k_rot[:, None, :], (group, heads_dev, ROPE))],
        axis=-1,
    ).astype(BF16)
    values = key_value[..., NOPE:].astype(BF16)
    visible = (seg_all[:, None] == seg_all[None, :]) & (seg_all[:, None] >= 0) & (
        positions[None, :] <= positions[:, None]
    ) | (positions[None, :] == positions[:, None])
    scores = jnp.einsum("qhd,khd->hqk", q_full, k_full, preferred_element_type=F32) * score_scale
    scores = jnp.where(visible[None], scores, MASKED)
    row_peak = jnp.max(scores, axis=-1, keepdims=True)
    exponent = jnp.exp(scores - row_peak)
    soft_float = exponent / jnp.sum(exponent, axis=-1, keepdims=True)
    soft = soft_float.astype(BF16)
    head_out = jnp.einsum("hqk,khd->qhd", soft, values, preferred_element_type=F32)
    head_out = head_out.astype(BF16).reshape(seq_count, tokens, heads_dev * VDIM)
    flat_out = jnp.swapaxes(from_own_order(exchange_seq(head_out), me), 0, 1).reshape(
        tokens, HEADS * VDIM
    )
    x_float = inputs[0].astype(F32)
    residual = x_float + dot(flat_out, w_output)
    ffn_in = normalized_rows(residual, g_ffn).astype(BF16)
    ffn_all = gather_seq(ffn_in)

    router_probs = jax.nn.softmax(dot(ffn_all, w_router), axis=-1)
    chosen = jnp.where(route_hot, router_probs, 0.0)
    chosen_sum = jnp.sum(chosen, axis=-1, keepdims=True)
    gates = chosen / chosen_sum
    my_gates = lax.dynamic_slice_in_dim(gates.T, me * EXP_DEV, EXP_DEV, 0)
    gate_rows = jnp.sum(jnp.where(placed, my_gates[:, None, :], 0.0), axis=-1)

    rows_shape = (EXP_DEV, CAP, width)
    expert_in = dot(dispatch, ffn_all).astype(BF16).reshape(rows_shape)
    grad_rows = dot(dispatch, g_all).reshape(rows_shape)
    expert_grad = (gate_rows[:, :, None] * grad_rows).astype(BF16)
    hidden_gate = jnp.einsum("nmh,nhq->nmq", expert_in, w_egate, preferred_element_type=F32)
    hidden_up = jnp.einsum("nmh,nhq->nmq", expert_in, w_eup, preferred_element_type=F32)
    expert_act = swiglu(hidden_gate, hidden_up).astype(BF16)
    expert_out = jnp.einsum(
        "kcf,kfd->kcd", expert_act, w_edown, preferred_element_type=F32
    ).astype(BF16).astype(F32)
    d_gate_rows = jnp.sum(expert_out * grad_rows, axis=-1)
    moe_rows = (gate_rows[:, :, None] * expert_out).astype(BF16).reshape(EXP_DEV * CAP, width)

    side_gate = dot(ffn_all, w_sgate)
    side_up = dot(ffn_all, w_sup)
    side_act = swiglu(side_gate, side_up).astype(BF16)
    ffn_out = scatter_seq(dot(side_act, w_sdown) + t_dot(dispatch, moe_rows))
    layer_out = (residual + ffn_out).astype(BF16)

    grad_sdown = t_dot(side_act, g_all)
    d_side_act = dot_t(g_all, w_sdown)
    _, side_pull = jax.vjp(swiglu, side_gate, side_up)
    d_side_gate, d_side_up = side_pull(d_side_act)
    d_side_gate = d_side_gate.astype(BF16)
    d_side_up = d_side_up.astype(BF16)
    grad_sgate = t_dot(ffn_all, d_side_gate)
    grad_sup = t_dot(ffn_all, d_side_up)

    d_act = jnp.einsum("kcd,kfd->kcf", expert_grad, w_edown, preferred_element_type=F32)
    _, expert_pull = jax.vjp(swiglu, hidden_gate, hidden_up)
    d_hidden_gate, d_hidden_up = expert_pull(d_act)
    d_hidden_gate = d_hidden_gate.astype(BF16)
    d_hidden_up = d_hidden_up.astype(BF16)
    d_expert_in = (
        jnp.einsum("sta,sra->str", d_hidden_gate, w_egate, preferred_element_type=F32)
        + jnp.einsum("sta,sra->str", d_hidden_up, w_eup, preferred_element_type=F32)
    ).astype(BF16)
    d_ffn_partial = (
        dot_t(d_side_gate, w_sgate)
        + dot_t(d_side_up, w_sup)
        + t_dot(dispatch, d_expert_in.reshape(EXP_DEV * CAP, width))
    )
    d_ffn = scatter_seq(d_ffn_partial)
    grad_edown = jnp.einsum("kcf,kcd->kfd", expert_act, expert_grad, preferred_element_type=F32)
    grad_egate = jnp.einsum("kcd,kcf->kdf", expert_in, d_hidden_gate, preferred_element_type=F32)
    grad_eup = jnp.einsum("kcd,kcf->kdf", expert_in, d_hidden_up, preferred_element_type=F32)

    d_gate_own = jnp.sum(jnp.where(placed, d_gate_rows[:, :, None], 0.0), axis=1)
    d_gate_abs = from_own_order(
        jnp.swapaxes(d_gate_own.reshape(EXP_DEV, seq_count, tokens), 0, 1), me
    )
    d_gate_all = lax.all_gather(d_gate_abs, "seq", axis=0, tiled=False)
    d_gate = lax.dynamic_index_in_dim(d_gate_all, me, 1, keepdims=False).reshape(experts, tokens).T
    own_hot = route_hot[:tokens]
    own_probs = router_probs[:tokens]
    own_gates = gates[:tokens]
    d_chosen = (d_gate - jnp.sum(d_gate * own_gates, axis=-1, keepdims=True)) / chosen_sum[:tokens]
    d_probs = jnp.where(own_hot, d_chosen, 0.0)
    d_logits = own_probs * (d_probs - jnp.sum(own_probs * d_probs, axis=-1, keepdims=True))
    grad_router = jnp.einsum("td,te->de", ffn_in.astype(F32), d_logits, precision=HIGHEST)
    d_ffn = d_ffn + jnp.einsum("te,de->td", d_logits, w_router.astype(F32), precision=HIGHEST)

    grad_out = cotangent[0].astype(F32)
    d_resid_part, grad_ffn_gain = norm_backward(residual, g_ffn, d_ffn)
    d_residual = grad_out + d_resid_part
    d_attn = d_residual.astype(BF16)
    d_head = dot_t(d_attn, w_output).astype(BF16)
    d_head_blocks = jnp.swapaxes(d_head.reshape(tokens, seq_count, heads_dev * VDIM), 0, 1)
    head_grad = exchange_seq(to_own_order(d_head_blocks, me)).reshape(group, heads_dev, VDIM)

    d_values = jnp.einsum("hqk,qhd->khd", soft, head_grad, preferred_element_type=F32).astype(BF16)
    d_prob = jnp.einsum("qhd,khd->hqk", head_grad, values, preferred_element_type=F32)
    d_score = (
        soft_float * (d_prob - jnp.sum(soft_float * d_prob, axis=-1, keepdims=True))
    ).astype(BF16)
    d_query = jnp.einsum("hqk,khd->qhd", d_score, k_full, preferred_element_type=F32)
    d_query = (d_query * score_scale).astype(BF16).astype(F32)
    d_key = jnp.einsum("hqk,qhd->khd", d_score, q_full, preferred_element_type=F32)
    d_key = (d_key * score_scale).astype(BF16)
    d_q_raw = jnp.concatenate(
        [d_query[..., :NOPE], rotate(d_query[..., NOPE:], cosine[:, None, :], -sine[:, None, :])],
        axis=-1,
    )
    d_q_raw = d_q_raw.astype(BF16).reshape(group, hq)
    d_key_value = jnp.concatenate([d_key[..., :NOPE], d_values], axis=-1).reshape(group, hkv)
    dk_rope = jnp.sum(d_key[..., NOPE:].astype(F32), axis=1)
    d_latent_part = jnp.concatenate([dot_t(d_key_value, w_expand), dk_rope], axis=-1)
    d_latent_sum = scatter_seq(d_latent_part)
    d_attn_in = scatter_seq(dot_t(d_q_raw, w_query))
    grad_expand = t_dot(latent_normed, d_key_value)
    grad_query = t_dot(attn_in, d_q_raw)

    d_k_pe = rotate(d_latent_sum[:, KV_RANK:], cosine[:tokens], -sine[:tokens])
    d_latent, grad_latent_gain = norm_backward(
        latent[:tokens], g_latent, d_latent_sum[:, :KV_RANK]
    )
    d_latent_raw = jnp.concatenate([d_latent, d_k_pe], axis=-1).astype(BF16)
    d_attn_in = d_attn_in + dot_t(d_latent_raw, w_latent)
    d_x_part, grad_attn_gain = norm_backward(x_float, g_attn, d_attn_in)
    grad_inputs = d_residual + d_x_part

    shard_edown = reduce_dp(grad_edown, 2).astype(F32)
    shard_egate = reduce_dp(grad_egate, 1).astype(F32)
    shard_eup = reduce_dp(grad_eup, 1).astype(F32)

    def joined(piece):
        return lax.all_gather(piece, "seq", axis=0, tiled=False)

    def shared_columns(gradient):
        all_units = joined(reduce_dp(gradient, 0)).reshape(seq_count, shard, dp_count, unit)
        return all_units.transpose(1, 2, 0, 3).reshape(shard, hidden).astype(F32)

    out_sgate = shared_columns(grad_sgate)
    out_sup = shared_columns(grad_sup)
    out_sdown = joined(reduce_dp(grad_sdown, 0)).reshape(hidden // dp_count, width).astype(F32)
    out_output = token_gradient(flat_out, d_attn, d_rank)
    out_query = (
        joined(reduce_dp(grad_query, 0)).transpose(1, 0, 2).reshape(shard, HEADS * QK).astype(F32)
    )
    out_expand = (
        joined(reduce_dp(grad_expand, 0))
        .transpose(1, 0, 2)
        .reshape(KV_RANK // dp_count, HEADS * (NOPE + VDIM))
        .astype(F32)
    )
    out_latent = token_gradient(attn_in[:tokens], d_latent_raw, d_rank)

    early = lax.psum(
        jnp.concatenate([grad_ffn_gain, grad_router.reshape(-1)]), ("seq", "dp")
    )
    late = lax.psum(jnp.concatenate([grad_attn_gain, grad_latent_gain]), ("seq", "dp"))
    out_ffn_gain = lax.dynamic_slice_in_dim(early, d_rank * shard, shard, 0)
    out_router = lax.dynamic_slice_in_dim(
        early[width:].reshape(width, experts), d_rank * shard, shard, 0
    )
    out_attn_gain = lax.dynamic_slice_in_dim(late, d_rank * shard, shard, 0)
    out_latent_gain = lax.dynamic_slice_in_dim(late, width + d_rank * rank_shard, rank_shard, 0)

    return (
        layer_out[None],
        grad_inputs[None],
        out_attn_gain,
        out_query,
        out_latent,
        out_latent_gain,
        out_expand,
        out_output,
        out_ffn_gain,
        out_router,
        out_sgate,
        out_sup,
        out_sdown,
        shard_egate,
        shard_eup,
        shard_edown,
    )


def solution(mesh):
    placed = (
        P("dp", "seq", None),
        P("dp", None),
        P("dp", "seq", None),
        P("dp", "seq", None),
        P("dp"),
        P("dp", None),
        P("dp", None),
        P("dp"),
        P("dp", None),
        P("dp", None),
        P("dp"),
        P("dp", None),
        P("dp", None),
        P("dp", None),
        P("dp", None),
        P("seq", "dp", None),
        P("seq", "dp", None),
        P("seq", None, "dp"),
    )
    return jax.shard_map(
        local,
        mesh=mesh,
        in_specs=placed,
        out_specs=(
            P("dp", "seq", None),
            P("dp", "seq", None),
            P("dp"),
            P("dp", None),
            P("dp", None),
            P("dp"),
            P("dp", None),
            P("dp", None),
            P("dp"),
            P("dp", None),
            P("dp", None),
            P("dp", None),
            P("dp", None),
            P("seq", "dp", None),
            P("seq", "dp", None),
            P("seq", None, "dp"),
        ),
        check_vma=False,
    )
```

time: 2600 us -> 1640 us (0.63)
  waiting for transfers between devices: 1890 us -> 929 us
  local copies, waits for them, and re-layouts: 187 us -> 108 us
  starting transfers between devices: 47.2 us -> 91.8 us
  blocking collectives: 92.8 us -> 135 us
  matrix products: 279 us -> 246 us
  other arithmetic: 71.5 us -> 100 us
    all_to_all x10 -> x0, waiting for transfers between devices: 551 us -> none  [the longest x1 132 us: local(): lax.all_to_all(to_send(pair_grad, pair_table), 'seq', split_axis=0, conca...]
    reduce_scatter x11 -> x7, waiting for transfers between devices: 549 us -> 329 us  [reduce_dp(): lax.psum_scatter(value.astype(BF16), 'dp', scatter_dimension=axis, tiled=...]
    psum x1 -> x2, waiting for transfers between devices: 311 us -> 138 us  [the longest x1 70.7 us: local(): lax.psum(jnp.concatenate([grad_ffn_gain, grad_router.reshape(-1)]), ('seq...]
    all_gather x10 -> x14, waiting for transfers between devices: 478 us -> 332 us  [the longest x9 258 us: gather_dp(): return lax.all_gather(value, 'dp', axis=axis, tiled=True)]
    ppermute x0 -> x55, waiting for transfers between devices: none -> 126 us  [swap(): return lax.ppermute(value, axis, [(i, i ^ mask) for i in range(count)])]
    ppermute x0 -> x55, starting transfers between devices: none -> 90 us  [swap(): return lax.ppermute(value, axis, [(i, i ^ mask) for i in range(count)])]
    gather x8 -> x0, local copies, waits for them, and re-layouts: 89.3 us -> none  [the longest x2 30.7 us: spread(): return flat_rows[scatter_at]]
    unnamed x204 -> x246, local copies, waits for them, and re-layouts: 9.47 us -> 61.3 us
  transfers between devices with their start and end apart: 32 -> 79, of which waited for: 23 -> 29; matrix products, arithmetic and copies ran while one was open for 20% -> 26% of each run, Pallas kernels for 0% -> 0%
where the time goes in v1:
time: 1640 us; the launch traced here: 1630 us
  waiting for transfers between devices  929 us (57%)
  matrix products  246 us (15%)
  blocking collectives  135 us (8%)
  local copies, waits for them, and re-layouts  108 us (7%)
  other arithmetic  100 us (6%)
  starting transfers between devices  91.8 us (6%)
  between operations  17.2 us (1%)
    reduce_scatter x7, waiting for transfers between devices, reduce_dp(): lax.psum_scatter(value.astype(BF16), 'dp', scatter_dimension=axis, tiled=...  329 us
    all_gather x9, waiting for transfers between devices, gather_dp(): return lax.all_gather(value, 'dp', axis=axis, tiled=True)  258 us
    ppermute x55, waiting for transfers between devices, swap(): return lax.ppermute(value, axis, [(i, i ^ mask) for i in range(count)])  126 us
    ppermute x55, starting transfers between devices, swap(): return lax.ppermute(value, axis, [(i, i ^ mask) for i in range(count)])  90 us
    all_gather x5, waiting for transfers between devices, joined(): return lax.all_gather(piece, 'seq', axis=0, tiled=False)  74.1 us
    psum x1, waiting for transfers between devices, local(): lax.psum(jnp.concatenate([grad_ffn_gain, grad_router.reshape(-1)]), ('seq...  70.7 us
    psum x1, waiting for transfers between devices, token_gradient(): return lax.psum(partial.astype(BF16), 'seq').astype(F32)  67.1 us
    unnamed x246, local copies, waits for them, and re-layouts  61.3 us
  transfers between devices with their start and end apart: 79, of which 29 were waited for; matrix products, arithmetic and copies ran while one was open for 26% of the time, Pallas kernels for 0%

profile of v1, /device:TPU:0, one launch (start us, length us, event | category | flops | bytes accessed | tf_op | source)
XLA Modules:
  0.0 1627.6 jit_solution(943937158184980594)
XLA Ops:
  48.3 44.9 %all-gather.3 = s32[1,1024,6]{1,0,2:T(1,128)S(1)} all-gather(s32[1,128,6]{1,0,2:T(1,128)S(1)} %copy-done.88), channel_id=5, replica_groups=mesh['seq'=8,'dp'=4] {'seq'}, dimensions={1}, use_global_device_ids=true | all-gather | bytes 27648 | tf_op jit(solution)/shard_map/all_gather | solution.py:237
  97.1 13.0 collective-permute-start.22
  121.2 16.6 %all_gather.72 = bf16[512,512]{1,0:T(8,128)(2,1)} all-gather(bf16[128,512]{1,0:T(8,128)(2,1)S(1)} %constant_dynamic-slice_fusion.15), channel_id=1, replica_groups=mesh['seq'=8,'dp'=4] {'dp'}, dimensions={0}, use_global_device_ids=true | all-gather | bytes 655360 | tf_op jit(solution)/shard_map/all_gather | solution.py:132
  210.8 18.4 %collective-permute-done.12 = bf16[128,2048]{1,0:T(8,128)(2,1)} collective-permute-done((bf16[128,2048]{1,0:T(8,128)(2,1)S(1)}, bf16[128,2048]{1,0:T(8,128)(2,1)}, u32[]{:S(2)}, u32[]{:S(2)}) %collective-permute-start.12) | collective-permute-done | bytes 524320 | tf_op jit(solution)/shard_map/ppermute | solution.py:70
  229.2 15.7 collective-permute-done.13
  301.4 53.7 %all-gather.33.cloned.1.call-done = bf16[2,2048,1408]{2,1,0:T(8,128)(2,1)} async-done(((bf16[2,512,1408]{2,1,0:T(8,128)(2,1)}), bf16[2,2048,1408]{2,1,0:T(8,128)(2,1)}) %all-gather.33.cloned.1.call-update) | async-done | bytes 11534352 | tf_op jit(solution)/shard_map/all_gather | solution.py:132
  355.2 13.0 fusion.159
  368.2 102.7 %all-gather.35.cloned.1.call-done = bf16[2,2048,1408]{2,1,0:T(8,128)(2,1)} async-done(((bf16[2,512,1408]{2,1,0:T(8,128)(2,1)}), bf16[2,2048,1408]{2,1,0:T(8,128)(2,1)}) %all-gather.35.cloned.1.call-update) | async-done | bytes 11534352 | tf_op jit(solution)/shard_map/all_gather | solution.py:132
  470.8 14.2 multiply_convert_fusion.3
  485.1 101.3 %all-gather.37.cloned.1.call-done = bf16[2,1408,2048]{2,1,0:T(8,128)(2,1)} async-done(((bf16[2,1408,512]{2,1,0:T(8,128)(2,1)}), bf16[2,1408,2048]{2,1,0:T(8,128)(2,1)}) %all-gather.37.cloned.1.call-update) | async-done | bytes 11534352 | tf_op jit(solution)/shard_map/all_gather | solution.py:132
  605.6 15.7 multiply_convert_fusion.2
  660.4 14.4 all_gather.82
  683.5 19.6 %collective-permute-done.25 = bf16[128,2048]{1,0:T(8,128)(2,1)S(1)} collective-permute-done((bf16[128,2048]{1,0:T(8,128)(2,1)S(1)}, bf16[128,2048]{1,0:T(8,128)(2,1)S(1)}, u32[]{:S(2)}, u32[]{:S(2)}) %collective-permute-start.25) | collective-permute-done | bytes 524320 | tf_op jit(solution)/shard_map/ppermute | solution.py:70
  703.0 15.0 collective-permute-done.26
  814.4 30.3 %collective-permute-done.50 = bf16[128,512]{0,1:T(8,128)(2,1)S(1)} collective-permute-done((bf16[128,512]{0,1:T(8,128)(2,1)S(1)}, bf16[128,512]{0,1:T(8,128)(2,1)S(1)}, u32[]{:S(2)}, u32[]{:S(2)}) %collective-permute-start.50) | collective-permute-done | bytes 131104 | tf_op jit(solution)/shard_map/ppermute | solution.py:70
  940.4 70.7 %all-reduce.5.cloned.1.call-done = f32[34816]{0:T(1024)} async-done(((f32[34816]{0:T(1024)}), f32[34816]{0:T(1024)}) %all-reduce.5.cloned.1.call-update) | async-done | bytes 139280 | tf_op jit(solution)/shard_map/psum | solution.py:419
  1014.4 36.3 %all-gather.47.cloned.1.call-done = bf16[4096,352]{0,1:T(8,128)(2,1)} async-done(((bf16[512,352]{0,1:T(8,128)(2,1)}), bf16[4096,352]{0,1:T(8,128)(2,1)}) %all-gather.47.cloned.1.call-update) | async-done | bytes 2883600 | tf_op jit(solution)/shard_map/all_gather | solution.py:398
  1071.0 16.2 all-gather.49.cloned.1.call-done
  1107.5 16.3 all-gather.51.cloned.1.call-done
  1128.9 67.1 %all-reduce.7.cloned.1.call-done = (bf16[512,576]{0,1:T(8,128)(2,1)}, bf16[512,2048]{1,0:T(8,128)(2,1)}) async-done(((bf16[512,576]{0,1:T(8,128)(2,1)}, bf16[512,2048]{1,0:T(8,128)(2,1)}), (bf16[512,576]{0,1:T(8,128)(2,1)}, bf16[512,2048]{1,0:T(8,128)(2,1)})) %all-reduce.7.cloned.1.call-update) | async-done | bytes 2686992 | tf_op jit(solution)/shard_map/psum | solution.py:148
  1206.7 50.6 %psum.28 = f32[2560]{0:T(1024)S(1)} all-reduce(f32[2560]{0:T(1024)S(1)} %pad_maximum_fusion.18), channel_id=1, replica_groups=mesh['seq'=8,'dp'=4] {'seq','dp'}, use_global_device_ids=true, to_apply=%region_26.27 | all-reduce | flops 2560 | bytes 20480 | tf_op jit(solution)/shard_map/psum | solution.py:422
  1276.9 108.4 %reduce-scatter.23.cloned.1.call-done = bf16[2,1408,512]{2,1,0:T(8,128)(2,1)} async-done(((bf16[2,1408,2048]{2,1,0:T(8,128)(2,1)}), bf16[2,1408,512]{2,1,0:T(8,128)(2,1)}) %reduce-scatter.23.cloned.1.call-update) | async-done | bytes 2883600 | tf_op jit(solution)/shard_map/reduce_scatter | solution.py:136
  1390.4 110.1 %reduce-scatter.19.cloned.1.call-done = bf16[2,512,1408]{2,1,0:T(8,128)(2,1)} async-done(((bf16[2,2048,1408]{2,1,0:T(8,128)(2,1)}), bf16[2,512,1408]{2,1,0:T(8,128)(2,1)}) %reduce-scatter.19.cloned.1.call-update) | async-done | bytes 2883600 | tf_op jit(solution)/shard_map/reduce_scatter | solution.py:136
  1505.4 110.2 %reduce-scatter.21.cloned.1.call-done = bf16[2,512,1408]{2,1,0:T(8,128)(2,1)} async-done(((bf16[2,2048,1408]{2,1,0:T(8,128)(2,1)}), bf16[2,512,1408]{2,1,0:T(8,128)(2,1)}) %reduce-scatter.21.cloned.1.call-update) | async-done | bytes 2883600 | tf_op jit(solution)/shard_map/reduce_scatter | solution.py:136
  (633 shorter events, 536.0 us)
Async XLA Ops:
  10.6 150.3 %all-gather.39.cloned.1.call-start = ((), (), s32[]{:S(2)}) async-start(), calls=%async_computation.23 | async-start | bytes 5242880 | tf_op jit(solution)/shard_map/all_gather | solution.py:132
  13.0 244.9 %all-gather.29.cloned.1.call-start = ((), (), s32[]{:S(2)}) async-start(), calls=%async_computation.10 | async-start | bytes 1802240 | tf_op jit(solution)/shard_map/all_gather | solution.py:132
  17.0 246.4 %all-gather.31.cloned.1.call-start = ((), (), s32[]{:S(2)}) async-start(), calls=%async_computation.11 | async-start | bytes 1802240 | tf_op jit(solution)/shard_map/all_gather | solution.py:132
  23.5 245.3 %all-gather.41.cloned.1.call-start = ((), (), s32[]{:S(2)}) async-start(), calls=%async_computation.24 | async-start | bytes 1802240 | tf_op jit(solution)/shard_map/all_gather | solution.py:132
  25.4 329.7 %all-gather.33.cloned.1.call-start = ((), (), s32[]{:S(2)}) async-start(), calls=%async_computation.12 | async-start | bytes 14417920 | tf_op jit(solution)/shard_map/all_gather | solution.py:132
  26.2 444.6 %all-gather.35.cloned.1.call-start = ((), (), s32[]{:S(2)}) async-start(), calls=%async_computation.13 | async-start | bytes 14417920 | tf_op jit(solution)/shard_map/all_gather | solution.py:132
  26.9 559.4 %all-gather.37.cloned.1.call-start = ((), (), s32[]{:S(2)}) async-start(), calls=%async_computation.14 | async-start | bytes 14417920 | tf_op jit(solution)/shard_map/all_gather | solution.py:132
  37.1 743.8 %reduce-scatter.15.cloned.1.call-start = ((), (), s32[]{:S(2)}) async-start(), calls=%async_computation.18 | async-start | bytes 1802240 | tf_op jit(solution)/shard_map/reduce_scatter | solution.py:136
  287.8 493.7 %reduce-scatter.17.cloned.1.call-start = ((), (), s32[]{:S(2)}) async-start(), calls=%async_computation.19 | async-start | bytes 1802240 | tf_op jit(solution)/shard_map/reduce_scatter | solution.py:136
  779.1 232.0 %all-reduce.5.cloned.1.call-start = ((), (), s32[]{:S(2)}) async-start(), calls=%async_computation.17 | async-start | bytes 278528 | tf_op jit(solution)/shard_map/psum | solution.py:419
  780.8 269.9 %all-gather.47.cloned.1.call-start = ((), (), s32[]{:S(2)}) async-start(), calls=%async_computation.27 | async-start | bytes 3244032 | tf_op jit(solution)/shard_map/all_gather | solution.py:398
  781.4 305.8 %all-gather.49.cloned.1.call-start = ((), (), s32[]{:S(2)}) async-start(), calls=%async_computation.28 | async-start | bytes 3244032 | tf_op jit(solution)/shard_map/all_gather | solution.py:398
  782.0 341.8 %all-gather.51.cloned.1.call-start = ((), (), s32[]{:S(2)}) async-start(), calls=%async_computation.29 | async-start | bytes 3244032 | tf_op jit(solution)/shard_map/all_gather | solution.py:398
  782.6 413.5 %all-reduce.7.cloned.1.call-start = ((), (), s32[]{:S(2)}) async-start(), calls=%async_computation.31 | async-start | bytes 5373952 | tf_op jit(solution)/shard_map/psum | solution.py:148
  859.2 403.6 %all-gather.45.cloned.1.call-start = ((), (), s32[]{:S(2)}) async-start(), calls=%async_computation.26 | async-start | bytes 1179648 | tf_op jit(solution)/shard_map/all_gather | solution.py:398
  859.7 411.3 %all-gather.43.cloned.1.call-start = ((), (), s32[]{:S(2)}) async-start(), calls=%async_computation.25 | async-start | bytes 3538944 | tf_op jit(solution)/shard_map/all_gather | solution.py:398
  860.5 524.8 %reduce-scatter.23.cloned.1.call-start = ((), (), s32[]{:S(2)}) async-start(), calls=%async_computation.22 | async-start | bytes 14417920 | tf_op jit(solution)/shard_map/reduce_scatter | solution.py:136
  872.5 628.0 %reduce-scatter.19.cloned.1.call-start = ((), (), s32[]{:S(2)}) async-start(), calls=%async_computation.20 | async-start | bytes 14417920 | tf_op jit(solution)/shard_map/reduce_scatter | solution.py:136
  885.9 729.7 %reduce-scatter.21.cloned.1.call-start = ((), (), s32[]{:S(2)}) async-start(), calls=%async_computation.21 | async-start | bytes 14417920 | tf_op jit(solution)/shard_map/reduce_scatter | solution.py:136
  928.6 273.0 %collective-permute-start.36 = (bf16[128,2048]{1,0:T(8,128)(2,1)}, bf16[128,2048]{1,0:T(8,128)(2,1)}, u32[]{:S(2)}, u32[]{:S(2)}) collective-permute-start(bf16[128,2048]{1,0:T(8,128)(2,1)} %get-tuple-element.126), channel_id=1, source_target_pairs={{0,8},{4,12},{8,0},{12,4},{16,24},{20,28},{24,16},{28,20},{1,9},{5... | collective-permute-start | bytes 1572872 | tf_op jit(solution)/shard_map/ppermute | solution.py:70
  930.6 272.5 %collective-permute-start.37 = (bf16[128,2048]{1,0:T(8,128)(2,1)}, bf16[128,2048]{1,0:T(8,128)(2,1)}, u32[]{:S(2)}, u32[]{:S(2)}) collective-permute-start(bf16[128,2048]{1,0:T(8,128)(2,1)} %get-tuple-element.128), channel_id=1, source_target_pairs={{0,16},{4,20},{8,24},{12,28},{16,0},{20,4},{24,8},{28,12},{1,17},{... | collective-permute-start | bytes 1572872 | tf_op jit(solution)/shard_map/ppermute | solution.py:70
  934.9 268.2 %collective-permute-start.38 = (bf16[128,2048]{1,0:T(8,128)(2,1)}, bf16[128,2048]{1,0:T(8,128)(2,1)}, u32[]{:S(2)}, u32[]{:S(2)}) collective-permute-start(bf16[128,2048]{1,0:T(8,128)(2,1)} %get-tuple-element.127), channel_id=1, source_target_pairs={{0,24},{4,28},{8,16},{12,20},{16,8},{20,12},{24,0},{28,4},{1,25},{... | collective-permute-start | bytes 1572872 | tf_op jit(solution)/shard_map/ppermute | solution.py:70
  936.1 322.5 %collective-permute-start.17 = (bf16[128,2048]{1,0:T(8,128)(2,1)}, bf16[128,2048]{1,0:T(8,128)(2,1)}, u32[]{:S(2)}, u32[]{:S(2)}) collective-permute-start(bf16[128,2048]{1,0:T(8,128)(2,1)} %get-tuple-element.132), channel_id=1, source_target_pairs={{0,8},{4,12},{8,0},{12,4},{16,24},{20,28},{24,16},{28,20},{1,9},{5... | collective-permute-start | bytes 1572872 | tf_op jit(solution)/shard_map/ppermute | solution.py:70
  936.6 321.9 %collective-permute-start.18 = (bf16[128,2048]{1,0:T(8,128)(2,1)}, bf16[128,2048]{1,0:T(8,128)(2,1)}, u32[]{:S(2)}, u32[]{:S(2)}) collective-permute-start(bf16[128,2048]{1,0:T(8,128)(2,1)} %get-tuple-element.134), channel_id=1, source_target_pairs={{0,16},{4,20},{8,24},{12,28},{16,0},{20,4},{24,8},{28,12},{1,17},{... | collective-permute-start | bytes 1572872 | tf_op jit(solution)/shard_map/ppermute | solution.py:70
  (159 other events, 5146.9 us)
Sparse Core Ops, SparseCore 0:
  10.4 33.8 all-gather.26
  46.2 38.1 all-gather.24
  86.9 56.9 all-gather.38
  146.1 29.7 all-gather.28
  178.1 29.7 all-gather.30
  209.6 29.8 all-gather.40
  241.3 113.7 all-gather.32
  357.0 113.7 all-gather.34
  472.7 113.6 all-gather.36
  589.1 30.1 reduce-scatter.14
  660.3 30.1 reduce-scatter.16
  738.7 28.9 reduce-scatter.24
  771.9 23.9 reduce-scatter.12
  799.3 57.1 reduce-scatter.10
  861.9 149.1 all-reduce.4
  1012.6 38.1 all-gather.46
  1052.2 34.9 all-gather.48
  1088.8 34.9 all-gather.50
  1126.8 69.2 all-reduce.6
  1197.5 33.4 all-gather.44
  1232.7 38.3 all-gather.42
  1274.1 111.1 reduce-scatter.22
  1388.4 112.0 reduce-scatter.18
  1503.5 112.0 reduce-scatter.20

commit v2 on v1

v2 whole, which is shorter than its diff:
```python
import math

import jax
import jax.numpy as jnp
from jax import lax
from jax.experimental import pallas as pl
from jax.experimental.pallas import tpu as pltpu
from jax.sharding import PartitionSpec as P

HEADS = 16
NOPE = 128
ROPE = 64
VDIM = 128
KV_RANK = 512
TOP = 6
EXP_DEV = 2
CAP = 480

EPSILON = 1e-06
MASKED = -1e30
HIGHEST = lax.Precision.HIGHEST
F32 = jnp.float32
BF16 = jnp.bfloat16
QK = NOPE + ROPE


def normalized_rows(values, gain):
    return values * lax.rsqrt(jnp.mean(values * values, axis=-1, keepdims=True) + EPSILON) * gain


def norm_backward(values, gain, upstream):
    scale = lax.rsqrt(jnp.mean(values * values, axis=-1, keepdims=True) + EPSILON)
    normed = values * scale
    weighted = upstream * gain
    d_values = scale * (weighted - normed * jnp.mean(weighted * normed, axis=-1, keepdims=True))
    return d_values, jnp.sum(upstream * normed, axis=0)


def angles(positions, width):
    frequency = 10000.0 ** (-(2.0 * jnp.arange(width // 2, dtype=F32)) / width)
    turned = positions.astype(F32)[:, None] * frequency[None, :]
    return (jnp.cos(turned), jnp.sin(turned))


def rotate(values, cosine, sine):
    half_width = values.shape[-1] // 2
    lower_half = values[..., :half_width]
    upper_half = values[..., half_width:]
    return jnp.concatenate(
        [lower_half * cosine - upper_half * sine, upper_half * cosine + lower_half * sine], axis=-1
    )


def swiglu(gate_portion, up_part):
    return jax.nn.silu(gate_portion) * up_part


def dot(left, right):
    return jnp.dot(left, right, preferred_element_type=F32)


def dot_t(left, right):
    return lax.dot_general(left, right, (((1,), (1,)), ((), ())), preferred_element_type=F32)


def t_dot(left, right):
    return lax.dot_general(left, right, (((0,), (0,)), ((), ())), preferred_element_type=F32)


def flip_copy(src, dst, send_sem, recv_sem, target):
    copy = pltpu.make_async_remote_copy(
        src_ref=src,
        dst_ref=dst,
        send_sem=send_sem,
        recv_sem=recv_sem,
        device_id=target,
        device_id_type=pl.DeviceIdType.MESH,
    )
    copy.start()
    return copy


def waiting(block, send_sem, recv_sem, target):
    return pltpu.make_async_remote_copy(
        src_ref=block,
        dst_ref=block,
        send_sem=send_sem,
        recv_sem=recv_sem,
        device_id=target,
        device_id_type=pl.DeviceIdType.MESH,
    )


def spread_seq(block, out, sems, place, chips):
    sends, recvs, near_send, near_recv, own_sem = sems
    chip, core, group = place
    beside = {"seq": 2 * chip + 1 - core}
    local_copy = pltpu.make_async_copy(block, out.at[chip, core], own_sem.at[0])
    local_copy.start()
    more = [chip + 1 < chips, chip > 0]
    onward = [{"seq": 2 * (chip + 1) + core}, {"seq": 2 * (chip - 1) + core}]
    for way in range(2):

        @pl.when(more[way])
        def _(way=way):
            flip_copy(
                block, out.at[chip, core], sends.at[way, 0], recvs.at[way, 0], onward[way]
            )

    flip_copy(block, out.at[chip, core], near_send.at[0, 0], near_recv.at[0, 0], beside)
    yield
    for step in range(1, chips):
        for way in range(2):
            source = chip - step if way == 0 else chip + step
            there = source >= 0 if way == 0 else source < chips

            @pl.when(there)
            def _(way=way, step=step, source=source):
                arrived = out.at[source, core]
                waiting(
                    arrived, sends.at[way, step - 1], recvs.at[way, step - 1], beside
                ).wait_recv()
                if step < chips - 1:

                    @pl.when(more[way])
                    def _():
                        flip_copy(
                            arrived,
                            arrived,
                            sends.at[way, step],
                            recvs.at[way, step],
                            onward[way],
                        )

                flip_copy(
                    arrived, arrived, near_send.at[way, step], near_recv.at[way, step], beside
                )

        yield
    own = out.at[chip, core]
    waiting(own, near_send.at[0, 0], near_recv.at[0, 0], beside).wait()
    for step in range(chips):
        for way in range(2):
            source = chip - step if way == 0 else chip + step
            there = source >= 0 if way == 0 else source < chips
            if step:

                @pl.when(there)
                def _(way=way, step=step):
                    waiting(
                        own, near_send.at[way, step], near_recv.at[way, step], beside
                    ).wait()

            if step < chips - 1:

                @pl.when(there & more[way])
                def _(way=way, step=step):
                    waiting(
                        own, sends.at[way, step], recvs.at[way, step], onward[way]
                    ).wait_send()

    local_copy.wait()


def spread_sems(chips):
    return [pltpu.SemaphoreType.DMA((2, chips)) for _ in range(4)] + [
        pltpu.SemaphoreType.DMA((1,))
    ]


class Part:
    axes = ("near", "far")

    def __init__(self, value):
        self.value = value
        self.chips = lax.axis_size("seq") // 2
        self.groups = lax.axis_size("dp")


class GatherSeq(Part):
    def result(self):
        shape = (self.chips, 2) + self.value.shape
        return jax.ShapeDtypeStruct(shape, self.value.dtype), pl.ANY

    def scratch(self):
        return spread_sems(self.chips)

    def steps(self, block, out, scratch, place):
        chip, core, group = place
        yield from spread_seq(block, out, scratch, place, self.chips)

    def finish(self, out):
        return out.reshape((2 * self.chips,) + self.value.shape)


class ExchangeSeq(Part):
    axes = ("near", "all")

    def result(self):
        return jax.ShapeDtypeStruct(self.value.shape, self.value.dtype), pl.ANY

    def scratch(self):
        count = 2 * self.chips
        return [pltpu.SemaphoreType.DMA((count,)), pltpu.SemaphoreType.DMA((count,))]

    def steps(self, block, out, scratch, place):
        chip, core, group = place
        send, recv = scratch
        me = 2 * chip + core
        local_copy = pltpu.make_async_copy(block.at[me], out.at[me], send.at[0])
        local_copy.start()
        copies = [
            flip_copy(block.at[me ^ m], out.at[me], send.at[m], recv.at[m], {"seq": me ^ m})
            for m in range(1, 2 * self.chips)
        ]
        yield
        for copy in copies:
            copy.wait()
        local_copy.wait()

    def finish(self, out):
        return out


class GatherDp(Part):
    axes = ("dp",)
    cores = False

    def result(self):
        lead = (self.groups, 2) if self.cores else (self.groups,)
        return jax.ShapeDtypeStruct(lead + self.value.shape, self.value.dtype), pl.ANY

    def scratch(self):
        return [pltpu.SemaphoreType.DMA((2, self.groups + 1)) for _ in range(2)] + [
            pltpu.SemaphoreType.DMA((2, 1)) for _ in range(2)
        ]

    def steps(self, block, out, scratch, place):
        chip, core, group = place
        send, recv, relay_send, relay_recv = scratch
        count = self.groups
        beside = {"seq": 2 * chip + 1 - core}
        relayed = count == 4

        def at(rank):
            return out.at[rank, core] if self.cores else out.at[rank]

        def near(p):
            return flip_copy(
                at(group ^ p), at(group ^ p), send.at[1, p], recv.at[1, p], beside
            )

        local_copy = pltpu.make_async_copy(block, at(group), send.at[0, count])
        local_copy.start()
        copies = {
            p: flip_copy(block, at(group), send.at[0, p], recv.at[0, p], {"dp": group ^ p})
            for p in range(1, count)
            if not (relayed and p == 3)
        }
        cores = []
        if self.cores:
            cores.append(
                flip_copy(block, at(group), send.at[1, 0], recv.at[1, 0], beside)
            )
        yield
        relays = []
        for p, copy in copies.items():
            copy.wait_recv()
            if relayed:
                first = self.value.shape[0] // 32 * 16
                rows = pl.ds(0, first) if p == 1 else pl.ds(first, self.value.shape[0] - first)
                half = at(group ^ p).at[rows]
                relays.append(
                    flip_copy(
                        half,
                        half,
                        relay_send.at[p - 1, 0],
                        relay_recv.at[p - 1, 0],
                        {"dp": group ^ (3 - p)},
                    )
                )
            if self.cores:
                cores.append(near(p))
        yield
        for copy in relays:
            copy.wait()
        if self.cores and relayed:
            cores.append(near(3))
        for copy in copies.values():
            copy.wait_send()
        yield
        for copy in cores:
            copy.wait()
        local_copy.wait()

    def finish(self, out):
        return out


class GatherDpCores(GatherDp):
    axes = ("dp", "near")
    cores = True


class PairCores(Part):
    axes = ("near",)

    def result(self):
        shape = (self.value.shape[0], 2) + self.value.shape[1:]
        return jax.ShapeDtypeStruct(shape, self.value.dtype), pl.ANY

    def scratch(self):
        return [pltpu.SemaphoreType.DMA((3,))]

    def steps(self, block, out, scratch, place):
        chip, core, group = place
        (sems,) = scratch
        local_copy = pltpu.make_async_copy(block, out.at[:, core], sems.at[0])
        local_copy.start()
        copy = flip_copy(
            block, out.at[:, core], sems.at[1], sems.at[2], {"seq": 2 * chip + 1 - core}
        )
        yield
        copy.wait()
        local_copy.wait()

    def finish(self, out):
        return out


class Pass(Part):
    axes = ()

    def result(self):
        return jax.ShapeDtypeStruct(self.value.shape, self.value.dtype), pl.ANY

    def scratch(self):
        return [pltpu.SemaphoreType.DMA((1,))]

    def steps(self, block, out, scratch, place):
        local_copy = pltpu.make_async_copy(block, out, scratch[0].at[0])
        local_copy.start()
        yield
        local_copy.wait()

    def finish(self, out):
        return out


class ExchangeDp(Part):
    axes = ("dp",)

    def result(self):
        return jax.ShapeDtypeStruct(self.value.shape, self.value.dtype), pl.ANY

    def scratch(self):
        return [pltpu.SemaphoreType.DMA((self.groups,)) for _ in range(2)]

    def steps(self, block, out, scratch, place):
        chip, core, group = place
        send, recv = scratch
        local_copy = pltpu.make_async_copy(block.at[group], out.at[group], send.at[0])
        local_copy.start()
        copies = [
            flip_copy(block.at[group ^ p], out.at[group], send.at[p], recv.at[p], {"dp": group ^ p})
            for p in range(1, self.groups)
        ]
        yield
        for copy in copies:
            copy.wait()
        local_copy.wait()

    def finish(self, out):
        return out


def add_rows(target, sources):
    rows = target.shape[0]

    @pl.loop(0, rows // 16)
    def _(i):
        at = pl.ds(pl.multiple_of(i * 16, 16), 16)
        total = sources[0][at, :].astype(F32)
        for source in sources[1:]:
            total = total + source[at, :].astype(F32)
        target[at, :] = total.astype(target.dtype)


class ScatterSeq(Part):
    axes = ("near", "far")

    def result(self):
        return jax.ShapeDtypeStruct(self.value.shape[1:], F32), pltpu.VMEM

    def prepare(self):
        shape = self.value.shape
        return self.value.reshape((self.chips, 2) + shape[1:])

    def scratch(self):
        block = self.value.shape[1:]
        return [
            pltpu.VMEM((self.chips,) + block, BF16),
            pltpu.VMEM((self.chips,) + block, BF16),
            pltpu.VMEM((2, self.chips) + block, BF16),
            pltpu.SemaphoreType.DMA((2, self.chips)),
            pltpu.SemaphoreType.DMA((2, self.chips)),
            pltpu.SemaphoreType.DMA((2,)),
            pltpu.SemaphoreType.DMA((1,)),
        ]

    def reduce(self, partial, out, scratch, place):
        chip, core, group = place
        chips = self.chips
        mine, peer, arrived, send, recv, near, own_sem = scratch
        local_copy = pltpu.make_async_copy(partial.at[:, core], mine, own_sem.at[0])
        local_copy.start()
        beside = flip_copy(
            partial.at[:, 1 - core], peer, near.at[0], near.at[1], {"seq": 2 * chip + 1 - core}
        )
        yield
        local_copy.wait()
        beside.wait()
        for k in range(chips):
            add_rows(mine.at[k], [mine.at[k], peer.at[k]])
        more = [chip + 1 < chips, chip > 0]
        onward = [{"seq": 2 * (chip + 1) + core}, {"seq": 2 * (chip - 1) + core}]
        for step in range(chips - 1):
            for way in range(2):
                to = chips - 1 - step if way == 0 else step
                ahead = chip < to if way == 0 else chip > to

                @pl.when(ahead)
                def _(way=way, to=to):
                    @pl.when(more[1 - way])
                    def _():
                        waiting(
                            arrived.at[way, to], send.at[way, to], recv.at[way, to], onward[way]
                        ).wait_recv()
                        add_rows(mine.at[to], [mine.at[to], arrived.at[way, to]])

                    flip_copy(
                        mine.at[to],
                        arrived.at[way, to],
                        send.at[way, to],
                        recv.at[way, to],
                        onward[way],
                    )

            yield
        for way in range(2):

            @pl.when(more[1 - way])
            def _(way=way):
                waiting(
                    arrived.at[way, chip], send.at[way, chip], recv.at[way, chip], onward[way]
                ).wait_recv()

        @pl.when(more[0] & more[1])
        def _():
            add_rows(out, [mine.at[chip], arrived.at[0, chip], arrived.at[1, chip]])

        for way in range(2):

            @pl.when(more[1 - way] & jnp.logical_not(more[way]))
            def _(way=way):
                add_rows(out, [mine.at[chip], arrived.at[way, chip]])

            for to in range(chips):
                ahead = chip < to if way == 0 else chip > to

                @pl.when(ahead)
                def _(way=way, to=to):
                    waiting(
                        mine.at[to], send.at[way, to], recv.at[way, to], onward[way]
                    ).wait_send()

    def steps(self, partial, out, scratch, place):
        yield from self.reduce(partial, out, scratch, place)

    def finish(self, out):
        return out


class SumSeq(ScatterSeq):
    def result(self):
        return jax.ShapeDtypeStruct((self.chips, 2) + self.value.shape[1:], BF16), pl.ANY

    def scratch(self):
        return (
            ScatterSeq.scratch(self)
            + [pltpu.VMEM(self.value.shape[1:], BF16)]
            + spread_sems(self.chips)
        )

    def steps(self, partial, out, scratch, place):
        chip, core, group = place
        total = scratch[7]
        yield from self.reduce(partial, total, scratch[:7], place)
        yield from spread_seq(total, out, scratch[8:], place, self.chips)

    def finish(self, out):
        return out.reshape(self.value.shape)


class ReduceDp(Part):
    axes = ("dp",)

    def result(self):
        return jax.ShapeDtypeStruct(self.value.shape[1:], self.value.dtype), pltpu.VMEM

    def scratch(self):
        return [
            pltpu.VMEM(self.value.shape, self.value.dtype),
            pltpu.SemaphoreType.DMA((self.groups,)),
            pltpu.SemaphoreType.DMA((self.groups,)),
        ]

    def reduce(self, value, out, scratch, place):
        chip, core, group = place
        arrived, send, recv = scratch
        local_copy = pltpu.make_async_copy(value.at[group], arrived.at[0], send.at[0])
        local_copy.start()
        copies = [
            flip_copy(value.at[group ^ p], arrived.at[p], send.at[p], recv.at[p], {"dp": group ^ p})
            for p in range(1, self.groups)
        ]
        yield
        local_copy.wait()
        for copy in copies:
            copy.wait()
        add_rows(out, [arrived.at[p] for p in range(self.groups)])

    def steps(self, value, out, scratch, place):
        yield from self.reduce(value, out, scratch, place)

    def finish(self, out):
        return out


class ReduceDpGatherSeq(ReduceDp):
    axes = ("dp", "near", "far")

    def result(self):
        shape = (self.chips, 2) + self.value.shape[1:]
        return jax.ShapeDtypeStruct(shape, self.value.dtype), pl.ANY

    def scratch(self):
        return (
            ReduceDp.scratch(self)
            + [pltpu.VMEM(self.value.shape[1:], self.value.dtype)]
            + spread_sems(self.chips)
        )

    def steps(self, value, out, scratch, place):
        chip, core, group = place
        total = scratch[3]
        yield from self.reduce(value, total, scratch[:3], place)
        yield from spread_seq(total, out, scratch[4:], place, self.chips)

    def finish(self, out):
        return out.reshape((2 * self.chips,) + self.value.shape[1:])


def communicate(number, parts):
    values = [part.prepare() if isinstance(part, ScatterSeq) else part.value for part in parts]
    results = [part.result() for part in parts]
    scratches = [part.scratch() for part in parts]
    chips, groups = parts[0].chips, parts[0].groups
    axes = set()
    for part in parts:
        axes.update(part.axes)

    def kernel(*refs):
        ins, outs = refs[: len(parts)], refs[len(parts) : 2 * len(parts)]
        rest = list(refs[2 * len(parts) :])
        me, group = lax.axis_index("seq"), lax.axis_index("dp")
        chip, core = me // 2, lax.rem(me, 2)
        targets = []
        for m in range(1, 2 * chips):
            if "all" in axes or (m == 1 and "near" in axes) or (m % 2 == 0 and "far" in axes):
                targets.append({"seq": me ^ m})
        if "dp" in axes:
            targets += [{"dp": group ^ p} for p in range(1, groups)]
        barrier = pltpu.get_barrier_semaphore()
        for target in targets:
            pl.semaphore_signal(
                barrier, inc=1, device_id=target, device_id_type=pl.DeviceIdType.MESH
            )
        pl.semaphore_wait(barrier, len(targets))
        running = []
        for part, value, out, scratch in zip(parts, ins, outs, scratches):
            own, rest = rest[: len(scratch)], rest[len(scratch) :]
            running.append(part.steps(value, out, own, (chip, core, group)))
        while running:
            running = [steps for steps in running if next(steps, "end") != "end"]

    outs = pl.pallas_call(
        kernel,
        out_shape=[shape for shape, _ in results],
        in_specs=[pl.BlockSpec(memory_space=pl.ANY)] * len(parts),
        out_specs=[pl.BlockSpec(memory_space=space) for _, space in results],
        scratch_shapes=[item for scratch in scratches for item in scratch],
        compiler_params=pltpu.CompilerParams(
            collective_id=number, has_side_effects=True, vmem_limit_bytes=48 * 1024 * 1024
        ),
    )(*values)
    return [part.finish(out) for part, out in zip(parts, outs)]


def padded_rows(value):
    rows = value.shape[-2]
    more = -rows % 16
    return jnp.pad(value, [(0, 0)] * (value.ndim - 2) + [(0, more), (0, 0)])


def local(
    inputs,
    segments,
    routes,
    cotangent,
    attention_gain,
    query_weight,
    latent_weight,
    latent_gain,
    expand_weight,
    output_weight,
    feedforward_gain,
    router_weight,
    shared_gate,
    shared_up,
    shared_down,
    expert_gate,
    expert_up,
    expert_down,
):
    seq_count = lax.axis_size("seq")
    dp_count = lax.axis_size("dp")
    me = lax.axis_index("seq")
    d_rank = lax.axis_index("dp")
    tokens = inputs.shape[1]
    width = inputs.shape[2]
    group = tokens * seq_count
    experts = EXP_DEV * seq_count
    heads_dev = HEADS // seq_count
    score_scale = 1.0 / math.sqrt(QK)
    shard = width // dp_count

    hq = heads_dev * QK
    hkv = heads_dev * (NOPE + VDIM)
    rank_shard = latent_gain.shape[0]
    latent_width = latent_weight.shape[1]
    small = jnp.concatenate(
        [attention_gain, feedforward_gain, latent_gain, router_weight.reshape(-1)]
    )
    fold = shard // rank_shard
    expand_part = lax.dynamic_slice_in_dim(expand_weight, me * hkv, hkv, 1)
    expand_part = (
        expand_part.reshape(rank_shard, fold, hkv // fold).transpose(1, 0, 2).reshape(shard, -1)
    )
    pack = jnp.concatenate(
        [lax.dynamic_slice_in_dim(query_weight, me * hq, hq, 1), expand_part], axis=1
    )
    pack_width = pack.shape[1]
    small_rows = -(-small.shape[0] // (16 * pack_width)) * 16
    small_pack = jnp.pad(small, (0, small_rows * pack_width - small.shape[0]))
    pack = jnp.concatenate([pack, small_pack.reshape(small_rows, pack_width)], axis=0)
    routes_pad = jnp.pad(routes[0], ((0, 0), (0, 128 - TOP))).astype(BF16)

    core = lax.rem(me, 2)

    def half_of(weight):
        rows = weight.shape[0] // 2
        return lax.dynamic_slice_in_dim(weight, core * rows, rows, 0)

    hidden = shared_gate.shape[1]
    unit = hidden // (dp_count * seq_count)
    side = dp_count * unit

    def columns_of(weight):
        split = weight.reshape(weight.shape[0], dp_count, seq_count, unit)
        mine = lax.dynamic_index_in_dim(split, me, 2, keepdims=False)
        return mine.reshape(weight.shape[0], side)

    w_output = lax.all_gather(half_of(output_weight), "dp", axis=0, tiled=False)
    w_sin = lax.all_gather(
        jnp.concatenate([columns_of(shared_gate), columns_of(shared_up)], axis=1),
        "dp",
        axis=0,
        tiled=True,
    )
    w_sdown = lax.all_gather(
        lax.dynamic_slice_in_dim(shared_down, me * unit, unit, 0), "dp", axis=0, tiled=True
    )
    w_egate = lax.all_gather(expert_gate, "dp", axis=1, tiled=True)
    w_eup = lax.all_gather(expert_up, "dp", axis=1, tiled=True)
    w_edown = lax.all_gather(expert_down, "dp", axis=2, tiled=True)

    x_all, routes_all, pack, w_latent = communicate(
        1,
        [
            GatherSeq(inputs[0]),
            GatherSeq(routes_pad),
            GatherDp(pack),
            GatherDpCores(half_of(latent_weight)),
        ],
    )
    x_all = x_all.reshape(group, width)
    w_query = pack[:, :shard, :hq].reshape(width, hq)
    w_latent = w_latent.reshape(width, latent_width)
    w_expand = (
        pack[:, :shard, hq:]
        .reshape(dp_count, fold, rank_shard, hkv // fold)
        .transpose(0, 2, 1, 3)
        .reshape(KV_RANK, hkv)
    )
    small = pack[:, shard:].reshape(dp_count, small_rows * pack_width)
    g_attn = small[:, :shard].reshape(width).astype(F32)
    g_ffn = small[:, shard : 2 * shard].reshape(width).astype(F32)
    g_latent = small[:, 2 * shard : 2 * shard + rank_shard].reshape(KV_RANK).astype(F32)
    w_router = small[:, 2 * shard + rank_shard :][:, : shard * experts].reshape(width, experts)

    routes_all = routes_all.reshape(group, 128)[:, :TOP].astype(jnp.int32)
    positions = jnp.arange(group, dtype=jnp.int32)
    seg_all = segments[0]
    cosine, sine = angles(positions, ROPE)
    my_experts = me * EXP_DEV + jnp.arange(EXP_DEV, dtype=jnp.int32)
    expert_ids = jnp.arange(experts, dtype=jnp.int32)
    hit = jnp.any(routes_all[None] == my_experts[:, None, None], axis=-1).astype(jnp.int32)
    slot = jnp.where(hit == 1, jnp.cumsum(hit, axis=1) - hit, CAP)
    route_hot = jnp.any(routes_all[:, :, None] == expert_ids[None, None, :], axis=1)
    placed = slot[:, None, :] == jnp.arange(CAP, dtype=jnp.int32)[None, :, None]
    dispatch = placed.astype(BF16).reshape(EXP_DEV * CAP, group)

    def own(value):
        return lax.dynamic_slice_in_dim(value, me * tokens, tokens, 0)

    attn_in = normalized_rows(x_all.astype(F32), g_attn).astype(BF16)
    q_raw = dot(attn_in, w_query).reshape(group, heads_dev, QK)
    latent_raw = dot(attn_in, w_latent)
    latent = latent_raw[:, :KV_RANK]
    latent_normed = normalized_rows(latent, g_latent).astype(BF16)
    key_value = dot(latent_normed, w_expand).reshape(group, heads_dev, NOPE + VDIM)
    q_full = jnp.concatenate(
        [q_raw[..., :NOPE], rotate(q_raw[..., NOPE:], cosine[:, None, :], sine[:, None, :])],
        axis=-1,
    ).astype(BF16)
    k_rot = rotate(latent_raw[:, KV_RANK:], cosine, sine)
    k_full = jnp.concatenate(
        [key_value[..., :NOPE], jnp.broadcast_to(k_rot[:, None, :], (group, heads_dev, ROPE))],
        axis=-1,
    ).astype(BF16)
    values = key_value[..., NOPE:].astype(BF16)
    visible = (seg_all[:, None] == seg_all[None, :]) & (seg_all[:, None] >= 0) & (
        positions[None, :] <= positions[:, None]
    ) | (positions[None, :] == positions[:, None])
    scores = jnp.einsum("qhd,khd->hqk", q_full, k_full, preferred_element_type=F32) * score_scale
    scores = jnp.where(visible[None], scores, MASKED)
    row_peak = jnp.max(scores, axis=-1, keepdims=True)
    exponent = jnp.exp(scores - row_peak)
    soft_float = exponent / jnp.sum(exponent, axis=-1, keepdims=True)
    soft = soft_float.astype(BF16)
    head_out = jnp.einsum("hqk,khd->qhd", soft, values, preferred_element_type=F32)
    head_out = head_out.astype(BF16).reshape(seq_count, tokens, heads_dev * VDIM)

    head_out, w_output = communicate(2, [ExchangeSeq(head_out), PairCores(w_output)])
    w_output = w_output.reshape(width, width)
    flat_out = jnp.swapaxes(head_out, 0, 1).reshape(tokens, HEADS * VDIM)
    x_float = inputs[0].astype(F32)
    residual = x_float + dot(flat_out, w_output)
    ffn_in = normalized_rows(residual, g_ffn).astype(BF16)

    (ffn_all,) = communicate(3, [GatherSeq(ffn_in)])
    ffn_all = ffn_all.reshape(group, width)

    router_probs = jax.nn.softmax(dot(ffn_all, w_router), axis=-1)
    chosen = jnp.where(route_hot, router_probs, 0.0)
    chosen_sum = jnp.sum(chosen, axis=-1, keepdims=True)
    gates = chosen / chosen_sum
    my_gates = lax.dynamic_slice_in_dim(gates.T, me * EXP_DEV, EXP_DEV, 0)
    gate_rows = jnp.sum(jnp.where(placed, my_gates[:, None, :], 0.0), axis=-1)

    g_own = lax.optimization_barrier((cotangent[0], ffn_all))[0]
    (g_all,) = communicate(4, [GatherSeq(g_own)])
    g_all = g_all.reshape(group, width)

    side_in = dot(ffn_all, w_sin)
    side_gate, side_up = side_in[:, :side], side_in[:, side:]
    side_act = swiglu(side_gate, side_up).astype(BF16)
    grad_sdown = t_dot(side_act, g_all)
    d_side_act = dot_t(g_all, w_sdown)
    _, side_pull = jax.vjp(swiglu, side_gate, side_up)
    d_side_gate, d_side_up = side_pull(d_side_act)
    d_side = jnp.concatenate([d_side_gate, d_side_up], axis=1).astype(BF16)
    grad_sin = t_dot(ffn_all, d_side)
    rows_shape = (EXP_DEV, CAP, width)
    expert_in = dot(dispatch, ffn_all).astype(BF16).reshape(rows_shape)
    hidden_gate = jnp.einsum("nmh,nhq->nmq", expert_in, w_egate, preferred_element_type=F32)
    expert_in, all_sin, all_sdown = communicate(
        5,
        [
            Pass(expert_in),
            ReduceDpGatherSeq(grad_sin.astype(BF16).reshape(dp_count, shard, 2 * side)),
            ReduceDpGatherSeq(padded_rows(grad_sdown.astype(BF16).reshape(dp_count, unit, width))),
        ],
    )
    all_side = all_sin.reshape(seq_count, shard, 2, dp_count, unit)
    all_side = all_side.transpose(2, 1, 3, 0, 4).reshape(2, shard, hidden).astype(F32)
    out_sgate, out_sup = all_side[0], all_side[1]
    out_sdown = all_sdown[:, :unit].reshape(hidden // dp_count, width).astype(F32)

    grad_rows = dot(dispatch, g_all).reshape(rows_shape)
    expert_grad = (gate_rows[:, :, None] * grad_rows).astype(BF16)
    hidden_up = jnp.einsum("nmh,nhq->nmq", expert_in, w_eup, preferred_element_type=F32)
    expert_act = swiglu(hidden_gate, hidden_up).astype(BF16)
    grad_edown = jnp.einsum("kcf,kcd->kfd", expert_act, expert_grad, preferred_element_type=F32)
    expert_out = jnp.einsum(
        "kcf,kfd->kcd", expert_act, w_edown, preferred_element_type=F32
    ).astype(BF16).astype(F32)
    d_gate_rows = jnp.sum(expert_out * grad_rows, axis=-1)
    moe_rows = (gate_rows[:, :, None] * expert_out).astype(BF16).reshape(EXP_DEV * CAP, width)
    ffn_out = (dot(side_act, w_sdown) + t_dot(dispatch, moe_rows)).astype(BF16)

    d_act = jnp.einsum("kcd,kfd->kcf", expert_grad, w_edown, preferred_element_type=F32)
    _, expert_pull = jax.vjp(swiglu, hidden_gate, hidden_up)
    d_hidden_gate, d_hidden_up = expert_pull(d_act)
    d_hidden_gate = d_hidden_gate.astype(BF16)
    d_hidden_up = d_hidden_up.astype(BF16)
    grad_egate = jnp.einsum("kcd,kcf->kdf", expert_in, d_hidden_gate, preferred_element_type=F32)
    grad_eup = jnp.einsum("kcd,kcf->kdf", expert_in, d_hidden_up, preferred_element_type=F32)
    shard_edown = lax.psum_scatter(
        grad_edown.astype(BF16), "dp", scatter_dimension=2, tiled=True
    ).astype(F32)
    shard_egate = lax.psum_scatter(
        grad_egate.astype(BF16), "dp", scatter_dimension=1, tiled=True
    ).astype(F32)
    shard_eup = lax.psum_scatter(
        grad_eup.astype(BF16), "dp", scatter_dimension=1, tiled=True
    ).astype(F32)
    d_expert_in = (
        jnp.einsum("sta,sra->str", d_hidden_gate, w_egate, preferred_element_type=F32)
        + jnp.einsum("sta,sra->str", d_hidden_up, w_eup, preferred_element_type=F32)
    ).astype(BF16)
    d_ffn_partial = dot_t(d_side, w_sin) + t_dot(
        dispatch, d_expert_in.reshape(EXP_DEV * CAP, width)
    )
    d_gate_own = jnp.sum(jnp.where(placed, d_gate_rows[:, :, None], 0.0), axis=1)
    mine_hot = (my_experts[:, None] == expert_ids[None, :]).astype(F32)
    d_gate_wide = jnp.sum(d_gate_own[:, :, None] * mine_hot[:, None, :], axis=0)
    d_gate_high = d_gate_wide.astype(BF16)
    d_gate_low = (d_gate_wide - d_gate_high.astype(F32)).astype(BF16)
    d_gate_pack = jnp.concatenate(
        [d_gate_high, d_gate_low, jnp.zeros((group, 128 - 2 * experts), BF16)], axis=1
    )
    d_ffn, d_gate = communicate(
        6,
        [
            ScatterSeq(d_ffn_partial.astype(BF16).reshape(seq_count, tokens, width)),
            ScatterSeq(d_gate_pack.reshape(seq_count, tokens, 128)),
        ],
    )
    d_gate = d_gate[:, :experts] + d_gate[:, experts : 2 * experts]

    own_hot = own(route_hot)
    own_probs = own(router_probs)
    own_gates = own(gates)
    d_chosen = (d_gate - jnp.sum(d_gate * own_gates, axis=-1, keepdims=True)) / own(chosen_sum)
    d_probs = jnp.where(own_hot, d_chosen, 0.0)
    d_logits = own_probs * (d_probs - jnp.sum(own_probs * d_probs, axis=-1, keepdims=True))
    grad_router = jnp.einsum("td,te->de", ffn_in.astype(F32), d_logits, precision=HIGHEST)
    d_ffn = d_ffn + jnp.einsum("te,de->td", d_logits, w_router.astype(F32), precision=HIGHEST)

    grad_out = cotangent[0].astype(F32)
    d_resid_part, grad_ffn_gain = norm_backward(residual, g_ffn, d_ffn)
    d_residual = grad_out + d_resid_part
    d_attn = d_residual.astype(BF16)
    d_head = dot_t(d_attn, w_output).astype(BF16)
    d_head = jnp.swapaxes(d_head.reshape(tokens, seq_count, heads_dev * VDIM), 0, 1)
    (head_grad,) = communicate(7, [ExchangeSeq(d_head)])
    head_grad = head_grad.reshape(group, heads_dev, VDIM)

    d_values = jnp.einsum("hqk,qhd->khd", soft, head_grad, preferred_element_type=F32).astype(BF16)
    d_prob = jnp.einsum("qhd,khd->hqk", head_grad, values, preferred_element_type=F32)
    d_score = (
        soft_float * (d_prob - jnp.sum(soft_float * d_prob, axis=-1, keepdims=True))
    ).astype(BF16)
    d_query = jnp.einsum("hqk,khd->qhd", d_score, k_full, preferred_element_type=F32)
    d_query = (d_query * score_scale).astype(BF16).astype(F32)
    d_key = jnp.einsum("hqk,qhd->khd", d_score, q_full, preferred_element_type=F32)
    d_key = (d_key * score_scale).astype(BF16)
    d_q_raw = jnp.concatenate(
        [d_query[..., :NOPE], rotate(d_query[..., NOPE:], cosine[:, None, :], -sine[:, None, :])],
        axis=-1,
    )
    d_q_raw = d_q_raw.astype(BF16).reshape(group, hq)
    d_key_value = jnp.concatenate([d_key[..., :NOPE], d_values], axis=-1).reshape(group, hkv)
    dk_rope = jnp.sum(d_key[..., NOPE:].astype(F32), axis=1)
    latent_pad = -latent_width % 128
    d_latent_part = jnp.concatenate(
        [dot_t(d_key_value, w_expand), dk_rope, jnp.zeros((group, latent_pad), F32)], axis=-1
    ).astype(BF16)
    d_attn_part = dot_t(d_q_raw, w_query).astype(BF16)
    grad_expand = t_dot(latent_normed, d_key_value).astype(BF16)
    grad_query = t_dot(attn_in, d_q_raw).astype(BF16)

    def by_group(rows):
        return jnp.swapaxes(rows.reshape(tokens, dp_count, -1), 0, 1)

    own_attn_in = own(attn_in)
    d_latent_sum, d_attn_in, sum_query, sum_expand, left_out, right_out, left_latent = communicate(
        8,
        [
            ScatterSeq(d_latent_part.reshape(seq_count, tokens, latent_width + latent_pad)),
            ScatterSeq(d_attn_part.reshape(seq_count, tokens, width)),
            ReduceDp(grad_query.reshape(dp_count, shard, hq)),
            ReduceDp(grad_expand.reshape(dp_count, rank_shard, hkv)),
            ExchangeDp(by_group(flat_out)),
            GatherDp(d_attn),
            ExchangeDp(by_group(own_attn_in)),
        ],
    )
    d_k_pe = rotate(d_latent_sum[:, KV_RANK:latent_width], own(cosine), -own(sine))
    d_latent, grad_latent_gain = norm_backward(
        own(latent), g_latent, d_latent_sum[:, :KV_RANK]
    )
    d_latent_raw = jnp.concatenate([d_latent, d_k_pe], axis=-1).astype(BF16)
    d_attn_in = d_attn_in + dot_t(d_latent_raw, w_latent)
    d_x_part, grad_attn_gain = norm_backward(x_float, g_attn, d_attn_in)
    grad_inputs = d_residual + d_x_part

    all_tokens = dp_count * tokens
    grad_output = t_dot(left_out.reshape(all_tokens, shard), right_out.reshape(all_tokens, width))
    grad_output = grad_output.astype(BF16).reshape(seq_count, shard // seq_count, width)
    latent_rows = jnp.pad(d_latent_raw, ((0, 0), (0, latent_pad)))

    gains = jnp.concatenate(
        [
            grad_attn_gain.reshape(dp_count, -1),
            grad_ffn_gain.reshape(dp_count, -1),
            grad_latent_gain.reshape(dp_count, -1),
            grad_router.reshape(dp_count, -1),
        ],
        axis=1,
    )
    gain_width = gains.shape[1]
    gain_rows = -(-gain_width // (16 * 128)) * 16
    gains = jnp.pad(gains, ((0, 0), (0, gain_rows * 128 - gain_width)))

    moe, all_query, all_expand, out_output, right_latent, all_gains = communicate(
        9,
        [
            ScatterSeq(ffn_out.reshape(seq_count, tokens, width)),
            GatherSeq(sum_query),
            GatherSeq(sum_expand),
            SumSeq(grad_output),
            GatherDp(latent_rows),
            ReduceDpGatherSeq(gains.reshape(dp_count, gain_rows, 128)),
        ],
    )
    layer_out = (residual + moe).astype(BF16)
    out_query = jnp.swapaxes(all_query, 0, 1).reshape(shard, HEADS * QK).astype(F32)
    out_expand = (
        jnp.swapaxes(all_expand, 0, 1).reshape(rank_shard, HEADS * (NOPE + VDIM)).astype(F32)
    )
    out_output = out_output.reshape(shard, width).astype(F32)
    grad_latent = t_dot(
        left_latent.reshape(all_tokens, shard),
        right_latent.reshape(all_tokens, -1)[:, :latent_width],
    ).astype(BF16)
    latent_blocks = jnp.pad(
        grad_latent.reshape(seq_count, shard // seq_count, latent_width),
        ((0, 0), (0, 0), (0, latent_pad)),
    )
    (out_latent,) = communicate(10, [SumSeq(latent_blocks)])
    out_latent = out_latent.reshape(shard, -1)[:, :latent_width].astype(F32)

    sums = jnp.sum(all_gains, axis=0).reshape(-1)
    out_attn_gain = sums[:shard]
    out_ffn_gain = sums[shard : 2 * shard]
    out_latent_gain = sums[2 * shard : 2 * shard + rank_shard]
    out_router = sums[2 * shard + rank_shard : gain_width].reshape(shard, experts)

    return (
        layer_out[None],
        grad_inputs[None],
        out_attn_gain,
        out_query,
        out_latent,
        out_latent_gain,
        out_expand,
        out_output,
        out_ffn_gain,
        out_router,
        out_sgate,
        out_sup,
        out_sdown,
        shard_egate,
        shard_eup,
        shard_edown,
    )


def solution(mesh):
    placed = (
        P("dp", "seq", None),
        P("dp", None),
        P("dp", "seq", None),
        P("dp", "seq", None),
        P("dp"),
        P("dp", None),
        P("dp", None),
        P("dp"),
        P("dp", None),
        P("dp", None),
        P("dp"),
        P("dp", None),
        P("dp", None),
        P("dp", None),
        P("dp", None),
        P("seq", "dp", None),
        P("seq", "dp", None),
        P("seq", None, "dp"),
    )
    return jax.shard_map(
        local,
        mesh=mesh,
        in_specs=placed,
        out_specs=(
            P("dp", "seq", None),
            P("dp", "seq", None),
            P("dp"),
            P("dp", None),
            P("dp", None),
            P("dp"),
            P("dp", None),
            P("dp", None),
            P("dp"),
            P("dp", None),
            P("dp", None),
            P("dp", None),
            P("dp", None),
            P("seq", "dp", None),
            P("seq", "dp", None),
            P("seq", None, "dp"),
        ),
        check_vma=False,
    )
```

time: 1640 us -> 1210 us (0.74)
  waiting for transfers between devices: 929 us -> 35.6 us
  Pallas kernels: 0 us -> 710 us
  blocking collectives: 135 us -> 0 us
  starting transfers between devices: 91.8 us -> 0.36 us
  other arithmetic: 100 us -> 76.6 us
    pallas_call x0 -> x10, Pallas kernels: none -> 710 us  [communicate(): pl.pallas_call(kernel, out_shape=[shape for shape, _ in results], in_spec...]
    reduce_scatter x7 -> x3, waiting for transfers between devices: 329 us -> 0.01 us  [the longest x1 0.01 us: local(): lax.psum_scatter(grad_egate.astype(BF16), 'dp', scatter_dimension=1, tile...]
    all_gather x14 -> x6, waiting for transfers between devices: 332 us -> 33.9 us  [the longest x1 33.9 us: local(): w_edown = lax.all_gather(expert_down, 'dp', axis=2, tiled=True)]
    psum x2 -> x0, waiting for transfers between devices: 138 us -> none  [the longest x1 70.7 us: local(): lax.psum(jnp.concatenate([grad_ffn_gain, grad_router.reshape(-1)]), ('seq...]
    ppermute x55 -> x0, waiting for transfers between devices: 126 us -> none  [swap(): return lax.ppermute(value, axis, [(i, i ^ mask) for i in range(count)])]
    ppermute x55 -> x0, starting transfers between devices: 90 us -> none  [swap(): return lax.ppermute(value, axis, [(i, i ^ mask) for i in range(count)])]
    all_gather x4 -> x0, blocking collectives: 84.8 us -> none  [the longest x1 44.9 us: local(): routes_abs = lax.all_gather(routes[0], 'seq', axis=0, tiled=True)]
    psum x1 -> x0, blocking collectives: 50.6 us -> none  [local(): lax.psum(jnp.concatenate([grad_attn_gain, grad_latent_gain]), ('seq', 'dp'))]
  transfers between devices with their start and end apart: 79 -> 9, of which waited for: 29 -> 1; matrix products, arithmetic and copies ran while one was open for 26% -> 31% of each run, Pallas kernels for 0% -> 59%
where the time goes in v2:
time: 1210 us; the launch traced here: 1200 us
  Pallas kernels  710 us (59%)
  matrix products  248 us (20%)
  local copies, waits for them, and re-layouts  113 us (9%)
  other arithmetic  76.6 us (6%)
  waiting for transfers between devices  35.6 us (3%)
  between operations  16.4 us (1%)
    pallas_call x10, Pallas kernels, communicate(): pl.pallas_call(kernel, out_shape=[shape for shape, _ in results], in_spec...  710 us
    dot_general x9, matrix products, dot(): return jnp.dot(left, right, preferred_element_type=F32)  45.8 us
    unnamed x272, local copies, waits for them, and re-layouts  43.3 us
    dot_general x8, matrix products, t_dot(): lax.dot_general(left, right, (((0,), (0,)), ((), ())), preferred_element_...  35.5 us
    all_gather x1, waiting for transfers between devices, local(): w_edown = lax.all_gather(expert_down, 'dp', axis=2, tiled=True)  33.9 us
  transfers between devices with their start and end apart: 9, of which 1 were waited for; matrix products, arithmetic and copies ran while one was open for 31% of the time, Pallas kernels for 59%

profile of v2, /device:TPU:0, one launch (start us, length us, event | category | flops | bytes accessed | tf_op | source)
XLA Modules:
  0.0 1199.6 jit_solution(13698814537935691213)
XLA Ops:
  33.3 61.6 %shard_map.297 = (bf16[4,2,128,2048]{3,2,1,0:T(8,128)(2,1)}, bf16[4,2,128,128]{3,2,1,0:T(8,128)(2,1)S(1)}, bf16[4,544,512]{2,1,0:T(8,128)(2,1)S(1)}, bf16[4,2,256,576]{3,2,1,0:T(8,128)(2,1)}) custom-call(bf16[128,2048]{1,0:T(8,128)(2,1)S(1)} %bitcast.247, bf16[128,128]{1,0:T(8,128)(2,1)S(1)} %pad.25.refs_1_, bf16[544,512]{1,0:T(8,128)(2,1)S(1)} %pad_maximum_fusion.8.refs_2_, ...), custom_call_target="tpu_custom_call" | custom-call | tf_op jit(solution)/shard_map/pallas_call | solution.py:597
  146.4 13.1 %shard_map.298 = (bf16[8,128,256]{2,1,0:T(8,128)(2,1)S(1)}, bf16[4,2,256,2048]{3,2,1,0:T(8,128)(2,1)}) custom-call(bf16[8,128,256]{2,1,0:T(8,128)(2,1)S(1)} %copy.279.refs_0_, bf16[4,256,2048]{2,1,0:T(8,128)(2,1)S(1)} %bitcast.249), custom_call_target="tpu_custom_call" | custom-call | tf_op jit(solution)/shard_map/pallas_call | solution.py:597
  165.5 44.0 %shard_map.299 = bf16[4,2,128,2048]{3,2,1,0:T(8,128)(2,1)S(1)} custom-call(bf16[128,2048]{1,0:T(8,128)(2,1)S(1)} %multiply_convert_fusion.13.refs_0_), custom_call_target="tpu_custom_call" | custom-call | tf_op jit(solution)/shard_map/pallas_call | solution.py:597
  211.6 42.4 %shard_map.300 = bf16[4,2,128,2048]{3,2,1,0:T(8,128)(2,1)S(1)} custom-call(bf16[128,2048]{1,0:T(8,128)(2,1)S(1)} %bitcast.248), custom_call_target="tpu_custom_call" | custom-call | tf_op jit(solution)/shard_map/pallas_call | solution.py:597
  288.1 9.2 convolution_convert_fusion.5
  297.3 201.8 %shard_map.301 = (bf16[2,480,2048]{2,1,0:T(8,128)(2,1)}, bf16[4,2,512,704]{3,2,1,0:T(8,128)(2,1)}, bf16[4,2,96,2048]{3,2,1,0:T(8,128)(2,1)S(1)}) custom-call(bf16[2,480,2048]{2,1,0:T(8,128)(2,1)} %bitcast.286, bf16[4,512,704]{2,1,0:T(8,128)(2,1)} %bitcast.273, bf16[4,96,2048]{2,1,0:T(8,128)(2,1)S(1)} %copy-done.9), custom_call_target="tpu_custom_call" | custom-call | tf_op jit(solution)/shard_map/pallas_call | solution.py:597
  500.7 13.4 %fusion.108 = f32[2,480,1408]{2,1,0:T(8,128)} fusion(bf16[2,480,2048]{2,1,0:T(8,128)(2,1)} %bitcast.287, bf16[2,2048,1408]{2,1,0:T(8,128)(2,1)} %all-gather.12.cloned.1.call-done), kind=kOutput, calls=%fused_computation.241 | convolution fusion | flops 5536481280 | bytes 20873216 | tf_op jit(solution)/shard_map/nmh,nhq->nmq/dot_general | solution.py:797
  514.1 13.8 %multiply_convert_fusion.4 = (bf16[2,480,1408]{2,1,0:T(8,128)(2,1)S(1)}, f32[2,480,1408]{2,1,0:T(8,128)}) fusion(f32[2,480,1408]{2,1,0:T(8,128)} %fusion.108, bf16[2,480,2048]{2,1,0:T(8,128)(2,1)} %get-tuple-element.48, bf16[2,2048,1408]{2,1,0:T(8,128)(2,1)} %all-gather.14.cloned.1.call-done), kind=kOutput, calls=%fused_computation.27 | convolution fusion | flops 5544591360 | bytes 28983296 | tf_op jit(solution)/shard_map/nmh,nhq->nmq/dot_general | solution.py:813
  528.0 33.9 %all-gather.16.cloned.1.call-done = bf16[2,1408,2048]{2,1,0:T(8,128)(2,1)} async-done(((bf16[2,1408,512]{2,1,0:T(8,128)(2,1)}), bf16[2,1408,2048]{2,1,0:T(8,128)(2,1)}) %all-gather.16.cloned.1.call-update) | async-done | bytes 11534352 | tf_op jit(solution)/shard_map/all_gather | solution.py:696
  561.9 9.3 convolution_convert_fusion.4
  579.5 14.7 %multiply_convert_fusion.3 = (bf16[2,480,1408]{2,1,0:T(8,128)(2,1)}, bf16[2,480,1408]{2,1,0:T(8,128)(2,1)S(1)}) fusion(f32[2,480,1408]{2,1,0:T(8,128)} %fusion.108, f32[2,480,1408]{2,1,0:T(8,128)} %get-tuple-element.175, bf16[2,1408,2048]{2,1,0:T(8,128)(2,1)} %all-gather.16.cloned.1.call-done, f32[2,480,2048]{2,1,0:T(8,128)} %get-tuple-element.177, ...), kind=kOutput, calls=%fused_computation.26 | convolution fusion | flops 5559336960 | bytes 35622656 | tf_op jit(solution)/shard_map/kcd,kfd->kcf/dot_general | solution.py:823
  594.3 12.6 %convolution_convert_fusion.2 = bf16[2,2048,1408]{2,1,0:T(8,128)(2,1)} fusion(bf16[2,480,2048]{2,1,0:T(8,128)(2,1)} %get-tuple-element.48, bf16[2,480,1408]{2,1,0:T(8,128)(2,1)S(1)} %get-tuple-element.147), kind=kOutput, calls=%fused_computation.3 | convolution fusion | flops 5542248448 | bytes 18169856 | tf_op jit(solution)/shard_map/kcd,kcf->kdf/dot_general | solution.py:828
  608.6 11.6 convolution_convert_fusion.1
  627.3 13.2 %convolution_convert_fusion = bf16[2,1408,2048]{2,1,0:T(8,128)(2,1)} fusion(bf16[2,480,1408]{2,1,0:T(8,128)(2,1)S(1)} %copy-done.117, f32[2,480,2048]{2,1,0:T(8,128)} %get-tuple-element.177, f32[2,480]{1,0:T(2,128)S(1)} %get-tuple-element.137), kind=kOutput, calls=%fused_computation.1 | convolution fusion | flops 5546180608 | bytes 22105856 | tf_op jit(solution)/shard_map/kcf,kcd->kfd/dot_general | solution.py:815
  648.8 9.5 copy.264
  658.3 8.8 fusion.99
  706.9 12.1 %fusion.109 = f32[2,480,2048]{2,1,0:T(8,128)} fusion(bf16[2,480,1408]{2,1,0:T(8,128)(2,1)} %copy-done.42, bf16[2,2048,1408]{2,1,0:T(8,128)(2,1)} %all-gather.12.cloned.1.call-done), kind=kOutput, calls=%fused_computation.242 | convolution fusion | flops 5536481280 | bytes 22102016 | tf_op jit(solution)/shard_map/sta,sra->str/dot_general | solution.py:840
  719.0 13.9 %add_convert_fusion = bf16[2,480,2048]{2,1,0:T(8,128)(2,1)} fusion(f32[2,480,2048]{2,1,0:T(8,128)} %fusion.109, bf16[2,480,1408]{2,1,0:T(8,128)(2,1)S(1)} %copy-done.123, bf16[2,2048,1408]{2,1,0:T(8,128)(2,1)} %all-gather.14.cloned.1.call-done), kind=kOutput, calls=%fused_computation.19 | convolution fusion | flops 5540413440 | bytes 26034176 | tf_op jit(solution)/shard_map/sta,sra->str/dot_general | solution.py:841
  741.3 60.3 %shard_map.302 = (f32[128,2048]{1,0:T(8,128)S(1)}, f32[128,128]{1,0:T(8,128)S(1)}) custom-call(bf16[4,2,128,2048]{3,2,1,0:T(8,128)(2,1)S(1)} %bitcast.253, bf16[4,2,128,128]{3,2,1,0:T(8,128)(2,1)S(1)} %maximum_maximum_fusion.1.refs_1_), custom_call_target="tpu_custom_call" | custom-call | tf_op jit(solution)/shard_map/pallas_call | solution.py:597
  810.3 17.8 %shard_map.303 = bf16[8,128,256]{2,1,0:T(8,128)(2,1)S(1)} custom-call(bf16[8,128,256]{2,1,0:T(8,128)(2,1)S(1)} %bitcast.259), custom_call_target="tpu_custom_call" | custom-call | tf_op jit(solution)/shard_map/pallas_call | solution.py:597
  863.0 121.8 %shard_map.304 = (f32[128,640]{1,0:T(8,128)S(1)}, f32[128,2048]{1,0:T(8,128)S(1)}, bf16[512,384]{1,0:T(8,128)(2,1)S(1)}, bf16[128,512]{1,0:T(8,128)(2,1)S(1)}, b...) custom-call(bf16[4,2,128,640]{3,2,1,0:T(8,128)(2,1)} %maximum_maximum_fusion.refs_0_, ...), custom_call_target="tpu_custom_call" | custom-call | tf_op jit(solution)/shard_map/pallas_call | solution.py:597
  1002.8 8.7 fusion.2
  1011.5 118.0 %shard_map.305 = (f32[128,2048]{1,0:T(8,128)S(1)}, bf16[4,2,512,384]{3,2,1,0:T(8,128)(2,1)}, bf16[4,2,128,512]{3,2,1,0:T(8,128)(2,1)S(1)}, bf16[4,2,64,2048]{3,2...) custom-call(bf16[4,2,128,2048]{3,2,1,0:T(8,128)(2,1)} %bitcast.280, ...), custom_call_target="tpu_custom_call" | custom-call | tf_op jit(solution)/shard_map/pallas_call | solution.py:597
  1137.9 28.9 %shard_map.306 = bf16[4,2,64,640]{3,2,1,0:T(8,128)(2,1)S(1)} custom-call(bf16[4,2,64,640]{3,2,1,0:T(8,128)(2,1)S(1)} %bitcast.255), custom_call_target="tpu_custom_call" | custom-call | tf_op jit(solution)/shard_map/pallas_call | solution.py:597
  (466 shorter events, 288.8 us)
Async XLA Ops:
  7.2 137.1 %all-gather.18.cloned.1.call-start = ((), (), s32[]{:S(2)}) async-start(), calls=%async_computation.11 | async-start | bytes 5242880 | tf_op jit(solution)/shard_map/all_gather | solution.py:684
  9.7 246.3 %all-gather.8.cloned.1.call-start = ((), (), s32[]{:S(2)}) async-start(), calls=%async_computation.3 | async-start | bytes 3604480 | tf_op jit(solution)/shard_map/all_gather | solution.py:685
  21.0 242.9 %all-gather.10.cloned.1.call-start = ((), (), s32[]{:S(2)}) async-start(), calls=%async_computation.4 | async-start | bytes 1802240 | tf_op jit(solution)/shard_map/all_gather | solution.py:691
  22.9 477.8 %all-gather.12.cloned.1.call-start = ((), (), s32[]{:S(2)}) async-start(), calls=%async_computation.5 | async-start | bytes 14417920 | tf_op jit(solution)/shard_map/all_gather | solution.py:694
  23.5 490.6 %all-gather.14.cloned.1.call-start = ((), (), s32[]{:S(2)}) async-start(), calls=%async_computation.6 | async-start | bytes 14417920 | tf_op jit(solution)/shard_map/all_gather | solution.py:695
  24.1 537.8 %all-gather.16.cloned.1.call-start = ((), (), s32[]{:S(2)}) async-start(), calls=%async_computation.7 | async-start | bytes 14417920 | tf_op jit(solution)/shard_map/all_gather | solution.py:696
  24.7 1153.2 %reduce-scatter.4.cloned.1.call-start = ((), (), s32[]{:S(2)}) async-start(), calls=%async_computation.8 | async-start | bytes 14417920 | tf_op jit(solution)/shard_map/reduce_scatter | solution.py:833
  142.1 145.0 %copy-start.71 = (pred[1024,16]{1,0:T(8,128)(4,1)}, pred[1024,16]{1,0:T(8,128)(4,1)S(1)}, u32[]{:S(2)}) copy-start(pred[1024,16]{1,0:T(8,128)(4,1)S(1)} %copy.238) | copy-start | bytes 49156
  142.5 142.2 %copy-start.50 = (bf16[2048,16]{1,0:T(8,128)(2,1)}, bf16[2048,16]{1,0:T(8,128)(2,1)S(1)}, u32[]{:S(2)}) copy-start(bf16[2048,16]{1,0:T(8,128)(2,1)S(1)} %reshape.625) | copy-start | bytes 196612
  164.8 89.2 %copy-start.39 = (f32[128,2048]{1,0:T(8,128)}, f32[128,2048]{1,0:T(8,128)S(1)}, u32[]{:S(2)}) copy-start(f32[128,2048]{1,0:T(8,128)S(1)} %get-tuple-element.173) | copy-start | bytes 3145732
  164.8 46.8 %copy-start.12 = (bf16[1,128,2048]{2,1,0:T(8,128)(2,1)S(1)}, bf16[1,128,2048]{2,1,0:T(8,128)(2,1)}, u32[]{:S(2)}) copy-start(bf16[1,128,2048]{2,1,0:T(8,128)(2,1)} %param.21) | copy-start | bytes 1572868
  165.3 88.7 %copy-start.100 = (f32[128]{0:T(128)}, f32[128]{0:T(128)S(1)}, u32[]{:S(2)}) copy-start(f32[128]{0:T(128)S(1)} %get-tuple-element.189) | copy-start | bytes 1540
  165.5 44.1 %copy-start.10 = (bf16[128,2048]{1,0:T(8,128)(2,1)}, bf16[128,2048]{1,0:T(8,128)(2,1)S(1)}, u32[]{:S(2)}) copy-start(bf16[128,2048]{1,0:T(8,128)(2,1)S(1)} %multiply_convert_fusion.13.refs_0_) | copy-start | bytes 1572868
  528.0 43.3 %copy-start.116 = (bf16[2,480,1408]{2,1,0:T(8,128)(2,1)}, bf16[2,480,1408]{2,1,0:T(8,128)(2,1)S(1)}, u32[]{:S(2)}) copy-start(bf16[2,480,1408]{2,1,0:T(8,128)(2,1)S(1)} %get-tuple-element.174) | copy-start | bytes 8110084
  606.9 575.7 %reduce-scatter.6.cloned.1.call-start = ((), (), s32[]{:S(2)}) async-start(), calls=%async_computation.9 | async-start | bytes 14417920 | tf_op jit(solution)/shard_map/reduce_scatter | solution.py:836
  620.2 567.2 %reduce-scatter.8.cloned.1.call-start = ((), (), s32[]{:S(2)}) async-start(), calls=%async_computation.10 | async-start | bytes 14417920 | tf_op jit(solution)/shard_map/reduce_scatter | solution.py:830
  719.0 87.9 %slice-start = ((s8[8388608]{0:T(1024)(128)(4,1)}), s8[4194304]{0:T(1024)(128)(4,1)S(1)}, s32[]{:S(2)}) async-start(s8[8388608]{0:T(1024)(128)(4,1)} %bitcast.267), calls=%async_computation.12 | async-start | bytes 8388608
  732.9 74.0 %slice-start.1 = ((s8[8388608]{0:T(1024)(128)(4,1)}), s8[4194304]{0:T(1024)(128)(4,1)S(1)}, s32[]{:S(2)}) async-start(s8[8388608]{0:T(1024)(128)(4,1)} %bitcast.267), calls=%async_computation.13 | async-start | bytes 8388608
  741.3 62.4 %copy-start.40 = (f32[128,2048]{1,0:T(8,128)S(1)}, f32[128,2048]{1,0:T(8,128)}, u32[]{:S(2)}) copy-start(f32[128,2048]{1,0:T(8,128)} %copy-done.39) | copy-start | bytes 3145732
  741.3 62.4 %copy-start.51 = (bf16[2048,16]{1,0:T(8,128)(2,1)S(1)}, bf16[2048,16]{1,0:T(8,128)(2,1)}, u32[]{:S(2)}) copy-start(bf16[2048,16]{1,0:T(8,128)(2,1)} %copy-done.50) | copy-start | bytes 196612
  741.3 62.4 %copy-start.90 = (f32[1,4,4,128]{3,1,2,0:T(4,128)S(1)}, f32[1,4,4,128]{3,1,2,0:T(4,128)}, u32[]{:S(2)}) copy-start(f32[1,4,4,128]{3,1,2,0:T(4,128)} %copy-done.89) | copy-start | bytes 24580
  741.3 62.4 %copy-start.101 = (f32[128]{0:T(128)S(1)}, f32[128]{0:T(128)}, u32[]{:S(2)}) copy-start(f32[128]{0:T(128)} %copy-done.100) | copy-start | bytes 1540
  741.3 65.2 %copy-start.13 = (bf16[1,128,2048]{2,1,0:T(8,128)(2,1)S(1)}, bf16[1,128,2048]{2,1,0:T(8,128)(2,1)}, u32[]{:S(2)}) copy-start(bf16[1,128,2048]{2,1,0:T(8,128)(2,1)} %param.21) | copy-start | bytes 1572868
  863.0 127.1 %copy-start.11 = (bf16[128,2048]{1,0:T(8,128)(2,1)S(1)}, bf16[128,2048]{1,0:T(8,128)(2,1)}, u32[]{:S(2)}) copy-start(bf16[128,2048]{1,0:T(8,128)(2,1)} %copy-done.10) | copy-start | bytes 1572868
  (111 other events, 552.6 us)
Sparse Core Ops, SparseCore 0:
  10.4 77.9 all-gather.17
  90.9 41.6 all-gather.7
  135.0 29.9 all-gather.9
  166.7 113.7 all-gather.11
  282.1 164.3 all-gather.13
  448.2 113.6 all-gather.15
  607.0 112.1 reduce-scatter.3
  722.3 112.0 reduce-scatter.5
  837.5 158.9 reduce-scatter.7

commit v3 on v2

--- a/solution.py
+++ b/solution.py
@@ -170,6 +170,7 @@
 
 class Part:
     axes = ("near", "far")
+    alias = False
 
     def __init__(self, value):
         self.value = value
@@ -302,73 +303,18 @@
     cores = True
 
 
-class PairCores(Part):
-    axes = ("near",)
-
-    def result(self):
-        shape = (self.value.shape[0], 2) + self.value.shape[1:]
-        return jax.ShapeDtypeStruct(shape, self.value.dtype), pl.ANY
-
-    def scratch(self):
-        return [pltpu.SemaphoreType.DMA((3,))]
-
-    def steps(self, block, out, scratch, place):
-        chip, core, group = place
-        (sems,) = scratch
-        local_copy = pltpu.make_async_copy(block, out.at[:, core], sems.at[0])
-        local_copy.start()
-        copy = flip_copy(
-            block, out.at[:, core], sems.at[1], sems.at[2], {"seq": 2 * chip + 1 - core}
-        )
-        yield
-        copy.wait()
-        local_copy.wait()
-
-    def finish(self, out):
-        return out
-
-
 class Pass(Part):
     axes = ()
+    alias = True
 
     def result(self):
         return jax.ShapeDtypeStruct(self.value.shape, self.value.dtype), pl.ANY
 
     def scratch(self):
-        return [pltpu.SemaphoreType.DMA((1,))]
+        return []
 
     def steps(self, block, out, scratch, place):
-        local_copy = pltpu.make_async_copy(block, out, scratch[0].at[0])
-        local_copy.start()
         yield
-        local_copy.wait()
-
-    def finish(self, out):
-        return out
-
-
-class ExchangeDp(Part):
-    axes = ("dp",)
-
-    def result(self):
-        return jax.ShapeDtypeStruct(self.value.shape, self.value.dtype), pl.ANY
-
-    def scratch(self):
-        return [pltpu.SemaphoreType.DMA((self.groups,)) for _ in range(2)]
-
-    def steps(self, block, out, scratch, place):
-        chip, core, group = place
-        send, recv = scratch
-        local_copy = pltpu.make_async_copy(block.at[group], out.at[group], send.at[0])
-        local_copy.start()
-        copies = [
-            flip_copy(block.at[group ^ p], out.at[group], send.at[p], recv.at[p], {"dp": group ^ p})
-            for p in range(1, self.groups)
-        ]
-        yield
-        for copy in copies:
-            copy.wait()
-        local_copy.wait()
 
     def finish(self, out):
         return out
@@ -404,7 +350,7 @@
             pltpu.VMEM((2, self.chips) + block, BF16),
             pltpu.SemaphoreType.DMA((2, self.chips)),
             pltpu.SemaphoreType.DMA((2, self.chips)),
-            pltpu.SemaphoreType.DMA((2,)),
+            pltpu.SemaphoreType.DMA((2, self.chips)),
             pltpu.SemaphoreType.DMA((1,)),
         ]
 
@@ -414,20 +360,32 @@
         mine, peer, arrived, send, recv, near, own_sem = scratch
         local_copy = pltpu.make_async_copy(partial.at[:, core], mine, own_sem.at[0])
         local_copy.start()
-        beside = flip_copy(
-            partial.at[:, 1 - core], peer, near.at[0], near.at[1], {"seq": 2 * chip + 1 - core}
-        )
+        order = [k for i in range(chips // 2) for k in (chips - 1 - i, i)]
+        beside = {
+            k: flip_copy(
+                partial.at[k, 1 - core],
+                peer.at[k],
+                near.at[0, k],
+                near.at[1, k],
+                {"seq": 2 * chip + 1 - core},
+            )
+            for k in order
+        }
         yield
         local_copy.wait()
-        beside.wait()
-        for k in range(chips):
+
+        def pair(k):
+            beside[k].wait()
             add_rows(mine.at[k], [mine.at[k], peer.at[k]])
+
         more = [chip + 1 < chips, chip > 0]
         onward = [{"seq": 2 * (chip + 1) + core}, {"seq": 2 * (chip - 1) + core}]
         for step in range(chips - 1):
             for way in range(2):
                 to = chips - 1 - step if way == 0 else step
                 ahead = chip < to if way == 0 else chip > to
+                if 2 * step < chips:
+                    pair(to)
 
                 @pl.when(ahead)
                 def _(way=way, to=to):
@@ -561,7 +519,7 @@
         return out.reshape((2 * self.chips,) + self.value.shape[1:])
 
 
-def communicate(number, parts):
+def communicate(number, parts, micros=50):
     values = [part.prepare() if isinstance(part, ScatterSeq) else part.value for part in parts]
     results = [part.result() for part in parts]
     scratches = [part.scratch() for part in parts]
@@ -600,11 +558,84 @@
         in_specs=[pl.BlockSpec(memory_space=pl.ANY)] * len(parts),
         out_specs=[pl.BlockSpec(memory_space=space) for _, space in results],
         scratch_shapes=[item for scratch in scratches for item in scratch],
+        input_output_aliases={i: i for i, part in enumerate(parts) if part.alias},
+        cost_estimate=pl.CostEstimate(
+            flops=0, bytes_accessed=micros * 3_000_000, transcendentals=0
+        ),
         compiler_params=pltpu.CompilerParams(
             collective_id=number, has_side_effects=True, vmem_limit_bytes=48 * 1024 * 1024
         ),
     )(*values)
     return [part.finish(out) for part, out in zip(parts, outs)]
+
+
+def swap_dp(value, mask):
+    return lax.ppermute(value, "dp", [(i, i ^ mask) for i in range(lax.axis_size("dp"))])
+
+
+def background_reduce(value):
+    me = lax.axis_index("dp")
+    total = lax.dynamic_index_in_dim(value, me, 0, keepdims=False).astype(F32)
+    for p in range(1, lax.axis_size("dp")):
+        piece = lax.dynamic_index_in_dim(value, me ^ p, 0, keepdims=False)
+        total = total + swap_dp(piece, p).astype(F32)
+    return total.astype(BF16)
+
+
+def background_gather(value):
+    return jnp.stack([value] + [swap_dp(value, p) for p in range(1, lax.axis_size("dp"))])
+
+
+def background_exchange(value):
+    me = lax.axis_index("dp")
+    pieces = [
+        lax.dynamic_index_in_dim(value, me ^ p, 0, keepdims=False)
+        for p in range(lax.axis_size("dp"))
+    ]
+    return jnp.stack([pieces[0]] + [swap_dp(pieces[p], p) for p in range(1, len(pieces))])
+
+
+def after(values, others):
+    def kernel(*refs):
+        del refs
+
+    count = len(values)
+    return pl.pallas_call(
+        kernel,
+        out_shape=[jax.ShapeDtypeStruct(v.shape, v.dtype) for v in values],
+        in_specs=[pl.BlockSpec(memory_space=pl.ANY)] * (count + len(others)),
+        out_specs=[pl.BlockSpec(memory_space=pl.ANY)] * count,
+        input_output_aliases={i: i for i in range(count)},
+        compiler_params=pltpu.CompilerParams(has_side_effects=True),
+    )(*values, *others)
+
+
+def joined_columns(pieces, groups, unit):
+    count, rows, columns = pieces.shape
+    half = columns // 2
+    block = 64
+
+    def kernel(pieces_ref, *out_refs):
+        parts = [pieces_ref[rank].astype(F32) for rank in range(count)]
+        for side, out_ref in enumerate(out_refs):
+            out_ref[...] = jnp.concatenate(
+                [
+                    parts[rank][:, side * half + p * unit : side * half + (p + 1) * unit]
+                    for p in range(groups)
+                    for rank in range(count)
+                ],
+                axis=1,
+            )
+
+    shape = jax.ShapeDtypeStruct((rows, count * half), F32)
+    return pl.pallas_call(
+        kernel,
+        grid=(rows // block,),
+        out_shape=[shape, shape],
+        in_specs=[pl.BlockSpec((count, block, columns), lambda i: (0, i, 0))],
+        out_specs=[pl.BlockSpec((block, count * half), lambda i: (i, 0))] * 2,
+        compiler_params=pltpu.CompilerParams(vmem_limit_bytes=48 * 1024 * 1024),
+    )(pieces)
 
 
 def padded_rows(value):
@@ -677,33 +708,31 @@
     side = dp_count * unit
 
     def columns_of(weight):
-        split = weight.reshape(weight.shape[0], dp_count, seq_count, unit)
-        mine = lax.dynamic_index_in_dim(split, me, 2, keepdims=False)
-        return mine.reshape(weight.shape[0], side)
-
-    w_output = lax.all_gather(half_of(output_weight), "dp", axis=0, tiled=False)
-    w_sin = lax.all_gather(
-        jnp.concatenate([columns_of(shared_gate), columns_of(shared_up)], axis=1),
-        "dp",
-        axis=0,
-        tiled=True,
-    )
-    w_sdown = lax.all_gather(
-        lax.dynamic_slice_in_dim(shared_down, me * unit, unit, 0), "dp", axis=0, tiled=True
-    )
-    w_egate = lax.all_gather(expert_gate, "dp", axis=1, tiled=True)
-    w_eup = lax.all_gather(expert_up, "dp", axis=1, tiled=True)
-    w_edown = lax.all_gather(expert_down, "dp", axis=2, tiled=True)
-
-    x_all, routes_all, pack, w_latent = communicate(
+        return [
+            lax.dynamic_slice_in_dim(weight, (p * seq_count + me) * unit, unit, 1)
+            for p in range(dp_count)
+        ]
+
+    x_all, routes_all, pack, w_latent, w_output, w_sin, w_sdown, g_all = communicate(
         1,
         [
             GatherSeq(inputs[0]),
             GatherSeq(routes_pad),
             GatherDp(pack),
             GatherDpCores(half_of(latent_weight)),
+            GatherDpCores(half_of(output_weight)),
+            GatherDp(jnp.concatenate(columns_of(shared_gate) + columns_of(shared_up), axis=1)),
+            GatherDp(padded_rows(lax.dynamic_slice_in_dim(shared_down, me * unit, unit, 0))),
+            GatherSeq(cotangent[0]),
         ],
     )
+    expert_gate, expert_up, expert_down = after([expert_gate, expert_up, expert_down], [x_all])
+    w_egate = lax.all_gather(expert_gate, "dp", axis=1, tiled=True)
+    w_eup = lax.all_gather(expert_up, "dp", axis=1, tiled=True)
+    w_edown = lax.all_gather(expert_down, "dp", axis=2, tiled=True)
+    w_sin = w_sin.reshape(width, 2 * side)
+    w_sdown = w_sdown[:, :unit].reshape(side, width)
+    g_all = g_all.reshape(group, width)
     x_all = x_all.reshape(group, width)
     w_query = pack[:, :shard, :hq].reshape(width, hq)
     w_latent = w_latent.reshape(width, latent_width)
@@ -762,7 +791,7 @@
     head_out = jnp.einsum("hqk,khd->qhd", soft, values, preferred_element_type=F32)
     head_out = head_out.astype(BF16).reshape(seq_count, tokens, heads_dev * VDIM)
 
-    head_out, w_output = communicate(2, [ExchangeSeq(head_out), PairCores(w_output)])
+    (head_out,) = communicate(2, [ExchangeSeq(head_out)])
     w_output = w_output.reshape(width, width)
     flat_out = jnp.swapaxes(head_out, 0, 1).reshape(tokens, HEADS * VDIM)
     x_float = inputs[0].astype(F32)
@@ -778,10 +807,6 @@
     gates = chosen / chosen_sum
     my_gates = lax.dynamic_slice_in_dim(gates.T, me * EXP_DEV, EXP_DEV, 0)
     gate_rows = jnp.sum(jnp.where(placed, my_gates[:, None, :], 0.0), axis=-1)
-
-    g_own = lax.optimization_barrier((cotangent[0], ffn_all))[0]
-    (g_all,) = communicate(4, [GatherSeq(g_own)])
-    g_all = g_all.reshape(group, width)
 
     side_in = dot(ffn_all, w_sin)
     side_gate, side_up = side_in[:, :side], side_in[:, side:]
@@ -792,50 +817,42 @@
     d_side_gate, d_side_up = side_pull(d_side_act)
     d_side = jnp.concatenate([d_side_gate, d_side_up], axis=1).astype(BF16)
     grad_sin = t_dot(ffn_all, d_side)
+    dispatch, all_sin, all_sdown = communicate(
+        5,
+        [
+            Pass(dispatch),
+            ReduceDpGatherSeq(grad_sin.astype(BF16).reshape(dp_count, shard, 2 * side)),
+            ReduceDpGatherSeq(padded_rows(grad_sdown.astype(BF16).reshape(dp_count, unit, width))),
+        ],
+    )
+
+    out_sgate, out_sup = joined_columns(all_sin, dp_count, unit)
+    out_sdown = all_sdown[:, :unit].reshape(hidden // dp_count, width).astype(F32)
+
     rows_shape = (EXP_DEV, CAP, width)
     expert_in = dot(dispatch, ffn_all).astype(BF16).reshape(rows_shape)
     hidden_gate = jnp.einsum("nmh,nhq->nmq", expert_in, w_egate, preferred_element_type=F32)
-    expert_in, all_sin, all_sdown = communicate(
-        5,
-        [
-            Pass(expert_in),
-            ReduceDpGatherSeq(grad_sin.astype(BF16).reshape(dp_count, shard, 2 * side)),
-            ReduceDpGatherSeq(padded_rows(grad_sdown.astype(BF16).reshape(dp_count, unit, width))),
-        ],
-    )
-    all_side = all_sin.reshape(seq_count, shard, 2, dp_count, unit)
-    all_side = all_side.transpose(2, 1, 3, 0, 4).reshape(2, shard, hidden).astype(F32)
-    out_sgate, out_sup = all_side[0], all_side[1]
-    out_sdown = all_sdown[:, :unit].reshape(hidden // dp_count, width).astype(F32)
-
-    grad_rows = dot(dispatch, g_all).reshape(rows_shape)
-    expert_grad = (gate_rows[:, :, None] * grad_rows).astype(BF16)
+    g_rows = dot(dispatch, g_all).astype(BF16).reshape(rows_shape)
+    expert_grad = (gate_rows[:, :, None] * g_rows.astype(F32)).astype(BF16)
     hidden_up = jnp.einsum("nmh,nhq->nmq", expert_in, w_eup, preferred_element_type=F32)
     expert_act = swiglu(hidden_gate, hidden_up).astype(BF16)
     grad_edown = jnp.einsum("kcf,kcd->kfd", expert_act, expert_grad, preferred_element_type=F32)
-    expert_out = jnp.einsum(
-        "kcf,kfd->kcd", expert_act, w_edown, preferred_element_type=F32
-    ).astype(BF16).astype(F32)
-    d_gate_rows = jnp.sum(expert_out * grad_rows, axis=-1)
-    moe_rows = (gate_rows[:, :, None] * expert_out).astype(BF16).reshape(EXP_DEV * CAP, width)
-    ffn_out = (dot(side_act, w_sdown) + t_dot(dispatch, moe_rows)).astype(BF16)
-
-    d_act = jnp.einsum("kcd,kfd->kcf", expert_grad, w_edown, preferred_element_type=F32)
+    grad_edown = grad_edown.astype(BF16)
+    (g_rows,) = after([g_rows], [grad_edown, out_sgate, out_sup, out_sdown])
+
+    d_act_plain = jnp.einsum("kcd,kfd->kcf", g_rows, w_edown, preferred_element_type=F32)
+    d_gate_rows = jnp.sum(expert_act.astype(F32) * d_act_plain, axis=-1)
     _, expert_pull = jax.vjp(swiglu, hidden_gate, hidden_up)
-    d_hidden_gate, d_hidden_up = expert_pull(d_act)
+    d_hidden_gate, d_hidden_up = expert_pull(gate_rows[:, :, None] * d_act_plain)
     d_hidden_gate = d_hidden_gate.astype(BF16)
     d_hidden_up = d_hidden_up.astype(BF16)
     grad_egate = jnp.einsum("kcd,kcf->kdf", expert_in, d_hidden_gate, preferred_element_type=F32)
     grad_eup = jnp.einsum("kcd,kcf->kdf", expert_in, d_hidden_up, preferred_element_type=F32)
-    shard_edown = lax.psum_scatter(
-        grad_edown.astype(BF16), "dp", scatter_dimension=2, tiled=True
-    ).astype(F32)
-    shard_egate = lax.psum_scatter(
-        grad_egate.astype(BF16), "dp", scatter_dimension=1, tiled=True
-    ).astype(F32)
-    shard_eup = lax.psum_scatter(
-        grad_eup.astype(BF16), "dp", scatter_dimension=1, tiled=True
-    ).astype(F32)
+    grad_egate, grad_eup = grad_egate.astype(BF16), grad_eup.astype(BF16)
+    shard_edown = lax.psum_scatter(grad_edown, "dp", scatter_dimension=2, tiled=True).astype(F32)
+    shard_egate = lax.psum_scatter(grad_egate, "dp", scatter_dimension=1, tiled=True).astype(F32)
+    shard_eup = lax.psum_scatter(grad_eup, "dp", scatter_dimension=1, tiled=True).astype(F32)
+    d_hidden_gate, d_hidden_up = after([d_hidden_gate, d_hidden_up], [grad_egate, grad_eup])
     d_expert_in = (
         jnp.einsum("sta,sra->str", d_hidden_gate, w_egate, preferred_element_type=F32)
         + jnp.einsum("sta,sra->str", d_hidden_up, w_eup, preferred_element_type=F32)
@@ -859,6 +876,12 @@
         ],
     )
     d_gate = d_gate[:, :experts] + d_gate[:, experts : 2 * experts]
+
+    (expert_act,) = after([expert_act], [d_ffn])
+    expert_out = jnp.einsum("kcf,kfd->kcd", expert_act, w_edown, preferred_element_type=F32)
+    expert_out = expert_out.astype(BF16).astype(F32)
+    moe_rows = (gate_rows[:, :, None] * expert_out).astype(BF16).reshape(EXP_DEV * CAP, width)
+    ffn_out = (dot(side_act, w_sdown) + t_dot(dispatch, moe_rows)).astype(BF16)
 
     own_hot = own(route_hot)
     own_probs = own(router_probs)
@@ -905,18 +928,20 @@
     def by_group(rows):
         return jnp.swapaxes(rows.reshape(tokens, dp_count, -1), 0, 1)
 
-    own_attn_in = own(attn_in)
-    d_latent_sum, d_attn_in, sum_query, sum_expand, left_out, right_out, left_latent = communicate(
+    left_out = background_exchange(by_group(flat_out))
+    right_out = background_gather(d_attn)
+    (right_out,) = after([right_out], [d_attn_part])
+    left_latent = background_exchange(by_group(own(attn_in)))
+    sum_query = background_reduce(grad_query.reshape(dp_count, shard, hq))
+    sum_expand = background_reduce(grad_expand.reshape(dp_count, rank_shard, hkv))
+    d_latent_sum, d_attn_in, moe = communicate(
         8,
         [
             ScatterSeq(d_latent_part.reshape(seq_count, tokens, latent_width + latent_pad)),
             ScatterSeq(d_attn_part.reshape(seq_count, tokens, width)),
-            ReduceDp(grad_query.reshape(dp_count, shard, hq)),
-            ReduceDp(grad_expand.reshape(dp_count, rank_shard, hkv)),
-            ExchangeDp(by_group(flat_out)),
-            GatherDp(d_attn),
-            ExchangeDp(by_group(own_attn_in)),
+            ScatterSeq(ffn_out.reshape(seq_count, tokens, width)),
         ],
+        micros=90,
     )
     d_k_pe = rotate(d_latent_sum[:, KV_RANK:latent_width], own(cosine), -own(sine))
     d_latent, grad_latent_gain = norm_backward(
@@ -945,23 +970,7 @@
     gain_rows = -(-gain_width // (16 * 128)) * 16
     gains = jnp.pad(gains, ((0, 0), (0, gain_rows * 128 - gain_width)))
 
-    moe, all_query, all_expand, out_output, right_latent, all_gains = communicate(
-        9,
-        [
-            ScatterSeq(ffn_out.reshape(seq_count, tokens, width)),
-            GatherSeq(sum_query),
-            GatherSeq(sum_expand),
-            SumSeq(grad_output),
-            GatherDp(latent_rows),
-            ReduceDpGatherSeq(gains.reshape(dp_count, gain_rows, 128)),
-        ],
-    )
-    layer_out = (residual + moe).astype(BF16)
-    out_query = jnp.swapaxes(all_query, 0, 1).reshape(shard, HEADS * QK).astype(F32)
-    out_expand = (
-        jnp.swapaxes(all_expand, 0, 1).reshape(rank_shard, HEADS * (NOPE + VDIM)).astype(F32)
-    )
-    out_output = out_output.reshape(shard, width).astype(F32)
+    right_latent = background_gather(latent_rows)
     grad_latent = t_dot(
         left_latent.reshape(all_tokens, shard),
         right_latent.reshape(all_tokens, -1)[:, :latent_width],
@@ -970,7 +979,22 @@
         grad_latent.reshape(seq_count, shard // seq_count, latent_width),
         ((0, 0), (0, 0), (0, latent_pad)),
     )
-    (out_latent,) = communicate(10, [SumSeq(latent_blocks)])
+    out_output, all_query, all_expand, out_latent, all_gains = communicate(
+        9,
+        [
+            SumSeq(grad_output),
+            GatherSeq(sum_query),
+            GatherSeq(sum_expand),
+            SumSeq(latent_blocks),
+            ReduceDpGatherSeq(gains.reshape(dp_count, gain_rows, 128)),
+        ],
+    )
+    layer_out = (residual + moe).astype(BF16)
+    out_query = jnp.swapaxes(all_query, 0, 1).reshape(shard, HEADS * QK).astype(F32)
+    out_expand = (
+        jnp.swapaxes(all_expand, 0, 1).reshape(rank_shard, HEADS * (NOPE + VDIM)).astype(F32)
+    )
+    out_output = out_output.reshape(shard, width).astype(F32)
     out_latent = out_latent.reshape(shard, -1)[:, :latent_width].astype(F32)
 
     sums = jnp.sum(all_gains, axis=0).reshape(-1)

time: 1210 us -> 1100 us (0.909)
  Pallas kernels: 710 us -> 599 us
  local copies, waits for them, and re-layouts: 113 us -> 85.6 us
  matrix products: 248 us -> 225 us
  waiting for transfers between devices: 35.6 us -> 58.2 us
  starting transfers between devices: 0.36 us -> 22.9 us
    pallas_call x10 -> x8, Pallas kernels: 710 us -> 589 us  [communicate(): pl.pallas_call(kernel, out_shape=[shape for shape, _ in results], in_spec...]
    ppermute x0 -> x18, waiting for transfers between devices: none -> 46.1 us  [swap_dp(): lax.ppermute(value, 'dp', [(i, i ^ mask) for i in range(lax.axis_size('dp...]
    all_gather x1, waiting for transfers between devices: 33.9 us -> 10.7 us  [local(): w_edown = lax.all_gather(expert_down, 'dp', axis=2, tiled=True)]
    ppermute x0 -> x18, starting transfers between devices: none -> 22.7 us  [swap_dp(): lax.ppermute(value, 'dp', [(i, i ^ mask) for i in range(lax.axis_size('dp...]
    slice x4 -> x2, local copies, waits for them, and re-layouts: 18.3 us -> 1.49 us  [the longest x1 1.28 us: local(): w_sdown = w_sdown[:, :unit].reshape(side, width)]
    unnamed x272 -> x305, local copies, waits for them, and re-layouts: 43.3 us -> 34.8 us
  transfers between devices with their start and end apart: 9 -> 24, of which waited for: 1 -> 7; matrix products, arithmetic and copies ran while one was open for 31% -> 32% of each run, Pallas kernels for 59% -> 44%
where the time goes in v3:
time: 1100 us; the launch traced here: 1090 us
  Pallas kernels  599 us (54%)
  matrix products  225 us (20%)
  local copies, waits for them, and re-layouts  85.6 us (8%)
  other arithmetic  82.8 us (8%)
  waiting for transfers between devices  58.2 us (5%)
  starting transfers between devices  22.9 us (2%)
  between operations  16.5 us (2%)
    pallas_call x8, Pallas kernels, communicate(): pl.pallas_call(kernel, out_shape=[shape for shape, _ in results], in_spec...  589 us
    ppermute x18, waiting for transfers between devices, swap_dp(): lax.ppermute(value, 'dp', [(i, i ^ mask) for i in range(lax.axis_size('dp...  46.1 us
    dot_general x9, matrix products, dot(): return jnp.dot(left, right, preferred_element_type=F32)  36.8 us
    unnamed x305, local copies, waits for them, and re-layouts  34.8 us
    dot_general x8, matrix products, t_dot(): lax.dot_general(left, right, (((0,), (0,)), ((), ())), preferred_element_...  28.3 us
    dot_general x6, matrix products, dot_t(): lax.dot_general(left, right, (((1,), (1,)), ((), ())), preferred_element_...  25 us
    ppermute x18, starting transfers between devices, swap_dp(): lax.ppermute(value, 'dp', [(i, i ^ mask) for i in range(lax.axis_size('dp...  22.7 us
  transfers between devices with their start and end apart: 24, of which 7 were waited for; matrix products, arithmetic and copies ran while one was open for 32% of the time, Pallas kernels for 44%

profile of v3, /device:TPU:0, one launch (start us, length us, event | category | flops | bytes accessed | tf_op | source)
XLA Modules:
  0.0 1090.2 jit_solution(3848453310453392263)
XLA Ops:
  34.5 122.7 %shard_map.297 = (bf16[4,2,128,2048]{3,2,1,0:T(8,128)(2,1)}, bf16[4,2,128,128]{3,2,1,0:T(8,128)(2,1)S(1)}, bf16[4,544,512]{2,1,0:T(8,128)(2,1)}, bf16[4,2,256,57...) custom-call(bf16[128,2048]{1,0:T(8,128)(2,1)S(1)} %bitcast.279, ...), custom_call_target="tpu_custom_call" | custom-call | bytes 150000000 | tf_op jit(solution)/shard_map/pallas_call | solution.py:555
  221.9 13.1 %shard_map.298 = bf16[8,128,256]{2,1,0:T(8,128)(2,1)S(1)} custom-call(bf16[8,128,256]{2,1,0:T(8,128)(2,1)S(1)} %copy.297.refs_0_), custom_call_target="tpu_custom_call" | custom-call | bytes 150000000 | tf_op jit(solution)/shard_map/pallas_call | solution.py:555
  240.5 44.0 %shard_map.299 = bf16[4,2,128,2048]{3,2,1,0:T(8,128)(2,1)S(1)} custom-call(bf16[128,2048]{1,0:T(8,128)(2,1)S(1)} %multiply_convert_fusion.13.refs_0_), custom_call_target="tpu_custom_call" | custom-call | bytes 150000000 | tf_op jit(solution)/shard_map/pallas_call | solution.py:555
  309.4 159.8 %shard_map.300 = (bf16[960,1024]{1,0:T(8,128)(2,1)S(1)}, bf16[4,2,512,704]{3,2,1,0:T(8,128)(2,1)}, bf16[4,2,96,2048]{3,2,1,0:T(8,128)(2,1)}) custom-call(bf16[960,1024]{1,0:T(8,128)(2,1)S(1)} %fusion.12.refs_0_, bf16[4,512,704]{2,1,0:T(8,128)(2,1)} %bitcast.293, bf16[4,96,2048]{2,1,0:T(8,128)(2,1)S(1)} %copy-done.11), custom_call_target="tpu_custom_call", output_to_operand_aliasing={{0}: (0, {})} | custom-call | bytes 150000000 | tf_op jit(solution)/shard_map/pallas_call | solution.py:555
  481.2 13.6 %fusion.107 = f32[2,480,1408]{2,1,0:T(8,128)} fusion(bf16[2,480,2048]{2,1,0:T(8,128)(2,1)} %bitcast.370, bf16[2,2048,1408]{2,1,0:T(8,128)(2,1)} %all-gather.4.cloned.1.call-done), kind=kOutput, calls=%fused_computation.267 | convolution fusion | flops 5536481280 | bytes 20873216 | tf_op jit(solution)/shard_map/nmh,nhq->nmq/dot_general | solution.py:834
  494.8 14.0 %multiply_convert_fusion.5 = (bf16[2,480,1408]{2,1,0:T(8,128)(2,1)S(1)}, f32[2,480,1408]{2,1,0:T(8,128)}) fusion(f32[2,480,1408]{2,1,0:T(8,128)} %fusion.107, bf16[2,480,2048]{2,1,0:T(8,128)(2,1)} %bitcast.371, bf16[2,2048,1408]{2,1,0:T(8,128)(2,1)} %all-gather.6.cloned.1.call-done), kind=kOutput, calls=%fused_computation.23 | convolution fusion | flops 5544591360 | bytes 28983296 | tf_op jit(solution)/shard_map/nmh,nhq->nmq/dot_general | solution.py:837
  508.8 9.1 convolution_convert_fusion.2.refs_1_
  520.1 10.5 shard_map.302
  534.1 10.7 all-gather.8.cloned.1.call-done
  544.8 14.6 %multiply_convert_fusion.4 = (bf16[2,480,1408]{2,1,0:T(8,128)(2,1)S(1)}, bf16[2,480,1408]{2,1,0:T(8,128)(2,1)}, f32[2,480]{1,0:T(2,128)S(1)}) fusion(f32[2,480]{1,0:T(2,128)S(1)} %select_reduce_fusion.1, f32[2,480,1408]{2,1,0:T(8,128)} %fusion.107, f32[2,480,1408]{2,1,0:T(8,128)} %get-tuple-element.218, bf16[2,480,1408]{2,1,0:T(8,128)(2,1)S(1)} %copy-done.57, ...), kind=kOutput, calls=%fused_computation.22 | convolution fusion | flops 5560810496 | bytes 34397696 | tf_op jit(solution)/shard_map/kcd,kfd->kcf/dot_general | solution.py:843
  560.9 12.0 %convolution_convert_fusion.refs_3_ = bf16[2,2048,1408]{2,1,0:T(8,128)(2,1)} fusion(bf16[2,480,2048]{2,1,0:T(8,128)(2,1)} %bitcast.372, bf16[2,480,1408]{2,1,0:T(8,128)(2,1)S(1)} %get-tuple-element.164.refs_1_), kind=kOutput, calls=%fused_computation.1 | convolution fusion | flops 5542248448 | bytes 18169856 | tf_op jit(solution)/shard_map/kcd,kcf->kdf/dot_general | solution.py:850
  584.1 9.2 fusion.44
  593.2 9.8 convolution_convert_fusion.1.refs_2_
  610.9 10.0 fusion.108
  620.9 11.5 %add_convert_fusion.2 = bf16[2,480,2048]{2,1,0:T(8,128)(2,1)} fusion(f32[2,480,2048]{2,1,0:T(8,128)S(1)} %fusion.108, bf16[2,480,1408]{2,1,0:T(8,128)(2,1)} %get-tuple-element.61, bf16[2,2048,1408]{2,1,0:T(8,128)(2,1)} %all-gather.6.cloned.1.call-done), kind=kOutput, calls=%fused_computation.14 | convolution fusion | flops 5540413440 | bytes 26034176 | tf_op jit(solution)/shard_map/sta,sra->str/dot_general | solution.py:858
  632.5 8.2 add_convert_fusion.1
  640.7 57.8 %shard_map.305 = (f32[128,2048]{1,0:T(8,128)S(1)}, f32[128,128]{1,0:T(8,128)S(1)}) custom-call(bf16[4,2,128,2048]{3,2,1,0:T(8,128)(2,1)S(1)} %bitcast.281, bf16[4,2,128,128]{3,2,1,0:T(8,128)(2,1)S(1)} %maximum_maximum_fusion.1.refs_1_), custom_call_target="tpu_custom_call" | custom-call | bytes 150000000 | tf_op jit(solution)/shard_map/pallas_call | solution.py:555
  714.7 17.8 %shard_map.306 = bf16[8,128,256]{2,1,0:T(8,128)(2,1)S(1)} custom-call(bf16[8,128,256]{2,1,0:T(8,128)(2,1)S(1)} %bitcast.284), custom_call_target="tpu_custom_call" | custom-call | bytes 150000000 | tf_op jit(solution)/shard_map/pallas_call | solution.py:555
  766.7 9.9 multiply_convert_fusion.2
  785.9 84.3 %shard_map.308 = (f32[128,640]{1,0:T(8,128)S(1)}, f32[128,2048]{1,0:T(8,128)S(1)}, f32[128,2048]{1,0:T(8,128)S(1)}) custom-call(bf16[4,2,128,640]{3,2,1,0:T(8,128)(2,1)S(1)} %maximum_maximum_fusion.refs_0_, bf16[4,2,128,2048]{3,2,1,0:T(8,128)(2,1)} %bitcast.292, bf16[4,2,128,2048]{3,2,1,0:T(8,128)(2,1)} %bitcast.291), custom_call_target="tpu_custom_call" | custom-call | bytes 270000000 | tf_op jit(solution)/shard_map/pallas_call | solution.py:555
  899.4 15.1 %collective-permute-done.15 = bf16[128,640]{1,0:T(8,128)(2,1)S(1)} collective-permute-done((bf16[128,640]{1,0:T(8,128)(2,1)S(1)}, bf16[128,640]{1,0:T(8,128)(2,1)S(1)}, u32[]{:S(2)}, u32[]{:S(2)}) %collective-permute-start.15) | collective-permute-done | bytes 163872 | tf_op jit(solution)/shard_map/ppermute | solution.py:573
  925.9 10.0 collective-permute-done.8
  936.3 9.6 collective-permute-done.7
  960.3 89.5 %shard_map.310 = (bf16[4,2,64,2048]{3,2,1,0:T(8,128)(2,1)S(1)}, bf16[4,2,512,384]{3,2,1,0:T(8,128)(2,1)}, bf16[4,2,128,512]{3,2,1,0:T(8,128)(2,1)S(1)}, bf16[4,2...) custom-call(bf16[4,2,64,2048]{3,2,1,0:T(8,128)(2,1)} %bitcast.314, bf16[512,384]{1,0:T(8,128)(2,1)S(1)} %fusion.47.refs_1_, ...), custom_call_target="tpu_custom_call" | custom-call | bytes 150000000 | tf_op jit(solution)/shard_map/pallas_call | solution.py:555
  (542 shorter events, 306.9 us)
Async XLA Ops:
  7.2 474.0 %all-gather.4.cloned.1.call-start = ((), (), s32[]{:S(2)}) async-start(), calls=%async_computation.3 | async-start | bytes 14417920 | tf_op jit(solution)/shard_map/all_gather | solution.py:730
  157.9 336.8 %all-gather.6.cloned.1.call-start = ((), (), s32[]{:S(2)}) async-start(), calls=%async_computation.4 | async-start | bytes 14417920 | tf_op jit(solution)/shard_map/all_gather | solution.py:731
  158.7 386.1 %all-gather.8.cloned.1.call-start = ((), (), s32[]{:S(2)}) async-start(), calls=%async_computation.5 | async-start | bytes 14417920 | tf_op jit(solution)/shard_map/all_gather | solution.py:732
  159.4 908.9 %reduce-scatter.8.cloned.1.call-start = ((), (), s32[]{:S(2)}) async-start(), calls=%async_computation.8 | async-start | bytes 14417920 | tf_op jit(solution)/shard_map/reduce_scatter | solution.py:852
  517.9 555.6 %reduce-scatter.6.cloned.1.call-start = ((), (), s32[]{:S(2)}) async-start(), calls=%async_computation.7 | async-start | bytes 14417920 | tf_op jit(solution)/shard_map/reduce_scatter | solution.py:854
  572.9 505.5 %reduce-scatter.4.cloned.1.call-start = ((), (), s32[]{:S(2)}) async-start(), calls=%async_computation.6 | async-start | bytes 14417920 | tf_op jit(solution)/shard_map/reduce_scatter | solution.py:853
  578.3 28.8 %collective-permute-start.12 = (bf16[128,512]{1,0:T(8,128)(2,1)S(1)}, bf16[128,512]{1,0:T(8,128)(2,1)}, u32[]{:S(2)}, u32[]{:S(2)}) collective-permute-start(bf16[128,512]{1,0:T(8,128)(2,1)S(1)} %bitcast.353), channel_id=1, source_target_pairs={{0,1},{1,0},{2,3},{3,2},{4,5},{5,4},{6,7},{7,6},{8,9},{9,8},{10,11... | collective-permute-start | bytes 393224 | tf_op jit(solution)/shard_map/ppermute | solution.py:573
  579.9 27.2 %collective-permute-start.13 = (bf16[128,512]{1,0:T(8,128)(2,1)S(1)}, bf16[128,512]{1,0:T(8,128)(2,1)}, u32[]{:S(2)}, u32[]{:S(2)}) collective-permute-start(bf16[128,512]{1,0:T(8,128)(2,1)S(1)} %bitcast.354), channel_id=1, source_target_pairs={{0,2},{1,3},{2,0},{3,1},{4,6},{5,7},{6,4},{7,5},{8,10},{9,11},{10,... | collective-permute-start | bytes 393224 | tf_op jit(solution)/shard_map/ppermute | solution.py:573
  580.7 26.4 %collective-permute-start.14 = (bf16[128,512]{1,0:T(8,128)(2,1)S(1)}, bf16[128,512]{1,0:T(8,128)(2,1)}, u32[]{:S(2)}, u32[]{:S(2)}) collective-permute-start(bf16[128,512]{1,0:T(8,128)(2,1)S(1)} %bitcast.355), channel_id=1, source_target_pairs={{0,3},{1,2},{2,1},{3,0},{4,7},{5,6},{6,5},{7,4},{8,11},{9,10},{10,... | collective-permute-start | bytes 393224 | tf_op jit(solution)/shard_map/ppermute | solution.py:573
  705.7 242.0 %collective-permute-start.5 = (bf16[128,2048]{1,0:T(8,128)(2,1)}, bf16[128,2048]{1,0:T(8,128)(2,1)}, u32[]{:S(2)}, u32[]{:S(2)}) collective-permute-start(bf16[128,2048]{1,0:T(8,128)(2,1)} %fusion.98), channel_id=1, source_target_pairs={{0,3},{1,2},{2,1},{3,0},{4,7},{5,6},{6,5},{7,4},{8,11},{9,10},{10,... | collective-permute-start | bytes 1572872 | tf_op jit(solution)/shard_map/ppermute | solution.py:573
  756.1 132.6 %collective-permute-start.9 = (bf16[128,512]{1,0:T(8,128)(2,1)}, bf16[128,512]{1,0:T(8,128)(2,1)}, u32[]{:S(2)}, u32[]{:S(2)}) collective-permute-start(bf16[128,512]{1,0:T(8,128)(2,1)} %get-tuple-element.197), channel_id=1, source_target_pairs={{0,1},{1,0},{2,3},{3,2},{4,5},{5,4},{6,7},{7,6},{8,9},{9,8},{10,11... | collective-permute-start | bytes 393224 | tf_op jit(solution)/shard_map/ppermute | solution.py:573
  757.2 132.1 %collective-permute-start.11 = (bf16[128,512]{1,0:T(8,128)(2,1)}, bf16[128,512]{1,0:T(8,128)(2,1)}, u32[]{:S(2)}, u32[]{:S(2)}) collective-permute-start(bf16[128,512]{1,0:T(8,128)(2,1)} %get-tuple-element.198), channel_id=1, source_target_pairs={{0,3},{1,2},{2,1},{3,0},{4,7},{5,6},{6,5},{7,4},{8,11},{9,10},{10,... | collective-permute-start | bytes 393224 | tf_op jit(solution)/shard_map/ppermute | solution.py:573
  758.5 132.2 %collective-permute-start.10 = (bf16[128,512]{1,0:T(8,128)(2,1)}, bf16[128,512]{1,0:T(8,128)(2,1)}, u32[]{:S(2)}, u32[]{:S(2)}) collective-permute-start(bf16[128,512]{1,0:T(8,128)(2,1)} %get-tuple-element.199), channel_id=1, source_target_pairs={{0,2},{1,3},{2,0},{3,1},{4,6},{5,7},{6,4},{7,5},{8,10},{9,11},{10,... | collective-permute-start | bytes 393224 | tf_op jit(solution)/shard_map/ppermute | solution.py:573
  886.8 36.3 %collective-permute-start.6 = (bf16[512,384]{1,0:T(8,128)(2,1)}, bf16[512,384]{1,0:T(8,128)(2,1)S(1)}, u32[]{:S(2)}, u32[]{:S(2)}) collective-permute-start(bf16[512,384]{1,0:T(8,128)(2,1)} %get-tuple-element.186), channel_id=1, source_target_pairs={{0,1},{1,0},{2,3},{3,2},{4,5},{5,4},{6,7},{7,6},{8,9},{9,8},{10,11... | collective-permute-start | bytes 1179656 | tf_op jit(solution)/shard_map/ppermute | solution.py:573
  888.7 10.1 collective-permute-start.16
  889.3 25.1 %collective-permute-start.15 = (bf16[128,640]{1,0:T(8,128)(2,1)S(1)}, bf16[128,640]{1,0:T(8,128)(2,1)S(1)}, u32[]{:S(2)}, u32[]{:S(2)}) collective-permute-start(bf16[128,640]{1,0:T(8,128)(2,1)S(1)} %get-tuple-element.205), channel_id=1, source_target_pairs={{0,1},{1,0},{2,3},{3,2},{4,5},{5,4},{6,7},{7,6},{8,9},{9,8},{10,11... | collective-permute-start | bytes 491528 | tf_op jit(solution)/shard_map/ppermute | solution.py:573
  890.7 31.3 %collective-permute-start.17 = (bf16[128,640]{1,0:T(8,128)(2,1)S(1)}, bf16[128,640]{1,0:T(8,128)(2,1)S(1)}, u32[]{:S(2)}, u32[]{:S(2)}) collective-permute-start(bf16[128,640]{1,0:T(8,128)(2,1)S(1)} %get-tuple-element.205), channel_id=1, source_target_pairs={{0,3},{1,2},{2,1},{3,0},{4,7},{5,6},{6,5},{7,4},{8,11},{9,10},{10,... | collective-permute-start | bytes 491528 | tf_op jit(solution)/shard_map/ppermute | solution.py:573
  898.8 53.7 %collective-permute-start.4 = (bf16[128,2048]{1,0:T(8,128)(2,1)}, bf16[128,2048]{1,0:T(8,128)(2,1)S(1)}, u32[]{:S(2)}, u32[]{:S(2)}) collective-permute-start(bf16[128,2048]{1,0:T(8,128)(2,1)} %fusion.98), channel_id=1, source_target_pairs={{0,2},{1,3},{2,0},{3,1},{4,6},{5,7},{6,4},{7,5},{8,10},{9,11},{10,... | collective-permute-start | bytes 1572872 | tf_op jit(solution)/shard_map/ppermute | solution.py:573
  914.4 21.5 %collective-permute-start.8 = (bf16[512,384]{1,0:T(8,128)(2,1)}, bf16[512,384]{1,0:T(8,128)(2,1)}, u32[]{:S(2)}, u32[]{:S(2)}) collective-permute-start(bf16[512,384]{1,0:T(8,128)(2,1)} %get-tuple-element.187), channel_id=1, source_target_pairs={{0,3},{1,2},{2,1},{3,0},{4,7},{5,6},{6,5},{7,4},{8,11},{9,10},{10,... | collective-permute-start | bytes 1179656 | tf_op jit(solution)/shard_map/ppermute | solution.py:573
  922.0 23.9 %collective-permute-start.7 = (bf16[512,384]{1,0:T(8,128)(2,1)S(1)}, bf16[512,384]{1,0:T(8,128)(2,1)}, u32[]{:S(2)}, u32[]{:S(2)}) collective-permute-start(bf16[512,384]{1,0:T(8,128)(2,1)S(1)} %get-tuple-element.188), channel_id=1, source_target_pairs={{0,2},{1,3},{2,0},{3,1},{4,6},{5,7},{6,4},{7,5},{8,10},{9,11},{10,... | collective-permute-start | bytes 1179656 | tf_op jit(solution)/shard_map/ppermute | solution.py:573
  923.0 29.4 %collective-permute-start.3 = (bf16[128,2048]{1,0:T(8,128)(2,1)}, bf16[128,2048]{1,0:T(8,128)(2,1)S(1)}, u32[]{:S(2)}, u32[]{:S(2)}) collective-permute-start(bf16[128,2048]{1,0:T(8,128)(2,1)} %fusion.98), channel_id=1, source_target_pairs={{0,1},{1,0},{2,3},{3,2},{4,5},{5,4},{6,7},{7,6},{8,9},{9,8},{10,11... | collective-permute-start | bytes 1572872 | tf_op jit(solution)/shard_map/ppermute | solution.py:573
  936.0 19.3 %collective-permute-start.2 = (bf16[128,512]{0,1:T(8,128)(2,1)}, bf16[128,512]{0,1:T(8,128)(2,1)S(1)}, u32[]{:S(2)}, u32[]{:S(2)}) collective-permute-start(bf16[128,512]{0,1:T(8,128)(2,1)} %get-tuple-element.201), channel_id=1, source_target_pairs={{0,3},{1,2},{2,1},{3,0},{4,7},{5,6},{6,5},{7,4},{8,11},{9,10},{10,... | collective-permute-start | bytes 393224 | tf_op jit(solution)/shard_map/ppermute | solution.py:573
  945.9 9.4 collective-permute-start.1
  947.8 7.6 collective-permute-start
  (143 other events, 2020.3 us)
Sparse Core Ops, SparseCore 0:
  158.1 111.9 all-gather.3
  272.5 156.7 all-gather.5
  431.1 113.6 all-gather.7
  547.7 117.7 reduce-scatter.7
  668.5 128.9 reduce-scatter.5
  800.4 140.6 reduce-scatter.3

commit v4 on v3

--- a/solution.py
+++ b/solution.py
@@ -573,13 +573,17 @@
     return lax.ppermute(value, "dp", [(i, i ^ mask) for i in range(lax.axis_size("dp"))])
 
 
-def background_reduce(value):
+def background_pieces(value):
     me = lax.axis_index("dp")
-    total = lax.dynamic_index_in_dim(value, me, 0, keepdims=False).astype(F32)
-    for p in range(1, lax.axis_size("dp")):
-        piece = lax.dynamic_index_in_dim(value, me ^ p, 0, keepdims=False)
-        total = total + swap_dp(piece, p).astype(F32)
-    return total.astype(BF16)
+    groups = lax.axis_size("dp")
+    pieces = [
+        lax.dynamic_index_in_dim(value, me ^ p, 0, keepdims=False) for p in range(groups)
+    ]
+    return [pieces[0]] + [swap_dp(pieces[p], p) for p in range(1, groups)]
+
+
+def sum_pieces(pieces):
+    return sum([piece.astype(F32) for piece in pieces[1:]], pieces[0].astype(F32)).astype(BF16)
 
 
 def background_gather(value):
@@ -713,7 +717,7 @@
             for p in range(dp_count)
         ]
 
-    x_all, routes_all, pack, w_latent, w_output, w_sin, w_sdown, g_all = communicate(
+    x_all, routes_all, pack, w_latent, w_output, g_all = communicate(
         1,
         [
             GatherSeq(inputs[0]),
@@ -721,17 +725,17 @@
             GatherDp(pack),
             GatherDpCores(half_of(latent_weight)),
             GatherDpCores(half_of(output_weight)),
-            GatherDp(jnp.concatenate(columns_of(shared_gate) + columns_of(shared_up), axis=1)),
-            GatherDp(padded_rows(lax.dynamic_slice_in_dim(shared_down, me * unit, unit, 0))),
             GatherSeq(cotangent[0]),
         ],
     )
-    expert_gate, expert_up, expert_down = after([expert_gate, expert_up, expert_down], [x_all])
+    arrived = routes_all[0, 0, 0] >= 0
+    expert_gate, expert_up, expert_down = (
+        jnp.where(arrived, weight, jnp.zeros_like(weight))
+        for weight in (expert_gate, expert_up, expert_down)
+    )
     w_egate = lax.all_gather(expert_gate, "dp", axis=1, tiled=True)
     w_eup = lax.all_gather(expert_up, "dp", axis=1, tiled=True)
     w_edown = lax.all_gather(expert_down, "dp", axis=2, tiled=True)
-    w_sin = w_sin.reshape(width, 2 * side)
-    w_sdown = w_sdown[:, :unit].reshape(side, width)
     g_all = g_all.reshape(group, width)
     x_all = x_all.reshape(group, width)
     w_query = pack[:, :shard, :hq].reshape(width, hq)
@@ -798,7 +802,16 @@
     residual = x_float + dot(flat_out, w_output)
     ffn_in = normalized_rows(residual, g_ffn).astype(BF16)
 
-    (ffn_all,) = communicate(3, [GatherSeq(ffn_in)])
+    ffn_all, w_sin, w_sdown = communicate(
+        3,
+        [
+            GatherSeq(ffn_in),
+            GatherDp(jnp.concatenate(columns_of(shared_gate) + columns_of(shared_up), axis=1)),
+            GatherDp(padded_rows(lax.dynamic_slice_in_dim(shared_down, me * unit, unit, 0))),
+        ],
+    )
+    w_sin = w_sin.reshape(width, 2 * side)
+    w_sdown = w_sdown[:, :unit].reshape(side, width)
     ffn_all = ffn_all.reshape(group, width)
 
     router_probs = jax.nn.softmax(dot(ffn_all, w_router), axis=-1)
@@ -841,6 +854,7 @@
     (g_rows,) = after([g_rows], [grad_edown, out_sgate, out_sup, out_sdown])
 
     d_act_plain = jnp.einsum("kcd,kfd->kcf", g_rows, w_edown, preferred_element_type=F32)
+    d_act_plain = lax.optimization_barrier(d_act_plain)
     d_gate_rows = jnp.sum(expert_act.astype(F32) * d_act_plain, axis=-1)
     _, expert_pull = jax.vjp(swiglu, hidden_gate, hidden_up)
     d_hidden_gate, d_hidden_up = expert_pull(gate_rows[:, :, None] * d_act_plain)
@@ -930,10 +944,10 @@
 
     left_out = background_exchange(by_group(flat_out))
     right_out = background_gather(d_attn)
-    (right_out,) = after([right_out], [d_attn_part])
+    right_out, d_attn_part = after([right_out, d_attn_part], [left_out])
     left_latent = background_exchange(by_group(own(attn_in)))
-    sum_query = background_reduce(grad_query.reshape(dp_count, shard, hq))
-    sum_expand = background_reduce(grad_expand.reshape(dp_count, rank_shard, hkv))
+    query_pieces = background_pieces(grad_query.reshape(dp_count, shard, hq))
+    expand_pieces = background_pieces(grad_expand.reshape(dp_count, rank_shard, hkv))
     d_latent_sum, d_attn_in, moe = communicate(
         8,
         [
@@ -943,6 +957,8 @@
         ],
         micros=90,
     )
+    query_pieces[0], expand_pieces[0] = after([query_pieces[0], expand_pieces[0]], [d_attn_in])
+    sum_query, sum_expand = sum_pieces(query_pieces), sum_pieces(expand_pieces)
     d_k_pe = rotate(d_latent_sum[:, KV_RANK:latent_width], own(cosine), -own(sine))
     d_latent, grad_latent_gain = norm_backward(
         own(latent), g_latent, d_latent_sum[:, :KV_RANK]

time: 1100 us -> 1070 us (0.973)
  waiting for transfers between devices: 58.2 us -> 16 us
  other arithmetic: 82.8 us -> 100 us
    ppermute x18, waiting for transfers between devices: 46.1 us -> 15.9 us  [swap_dp(): lax.ppermute(value, 'dp', [(i, i ^ mask) for i in range(lax.axis_size('dp...]
    unnamed x305 -> x296, local copies, waits for them, and re-layouts: 34.8 us -> 26.6 us
  transfers between devices with their start and end apart: 24 -> 24, of which waited for: 7 -> 3; matrix products, arithmetic and copies ran while one was open for 32% -> 35% of each run, Pallas kernels for 44% -> 48%
where the time goes in v4:
time: 1070 us
  Pallas kernels  598 us (56%)
  matrix products  224 us (21%)
  other arithmetic  100 us (9%)
  local copies, waits for them, and re-layouts  90.8 us (8%)
  starting transfers between devices  22.4 us (2%)
  between operations  17.2 us (2%)
  waiting for transfers between devices  16 us (1%)
    pallas_call x8, Pallas kernels, communicate(): pl.pallas_call(kernel, out_shape=[shape for shape, _ in results], in_spec...  588 us
    dot_general x9, matrix products, dot(): return jnp.dot(left, right, preferred_element_type=F32)  39.3 us
    dot_general x8, matrix products, t_dot(): lax.dot_general(left, right, (((0,), (0,)), ((), ())), preferred_element_...  28.4 us
    dot_general x6, matrix products, dot_t(): lax.dot_general(left, right, (((1,), (1,)), ((), ())), preferred_element_...  27.1 us
    unnamed x296, local copies, waits for them, and re-layouts  26.6 us
    ppermute x18, starting transfers between devices, swap_dp(): lax.ppermute(value, 'dp', [(i, i ^ mask) for i in range(lax.axis_size('dp...  22.1 us
  transfers between devices with their start and end apart: 24, of which 3 were waited for; matrix products, arithmetic and copies ran while one was open for 35% of the time, Pallas kernels for 48%

profile of v4, /device:TPU:0, one launch (start us, length us, event | category | flops | bytes accessed | tf_op | source)
XLA Modules:
  0.0 1068.4 jit_solution(16396353541616454127)
XLA Ops:
  21.3 87.2 %shard_map.297 = (bf16[4,2,128,2048]{3,2,1,0:T(8,128)(2,1)}, bf16[4,2,128,128]{3,2,1,0:T(8,128)(2,1)S(1)}, bf16[4,544,512]{2,1,0:T(8,128)(2,1)S(1)}, bf16[4,2,25...) custom-call(bf16[128,2048]{1,0:T(8,128)(2,1)S(1)} %bitcast.270, ...), custom_call_target="tpu_custom_call" | custom-call | bytes 150000000 | tf_op jit(solution)/shard_map/pallas_call | solution.py:555
  169.2 8.4 fusion.87
  182.2 13.1 %shard_map.298 = bf16[8,128,256]{2,1,0:T(8,128)(2,1)S(1)} custom-call(bf16[8,128,256]{2,1,0:T(8,128)(2,1)S(1)} %copy.324.refs_0_), custom_call_target="tpu_custom_call" | custom-call | bytes 150000000 | tf_op jit(solution)/shard_map/pallas_call | solution.py:555
  204.3 65.8 %shard_map.299 = (bf16[4,2,128,2048]{3,2,1,0:T(8,128)(2,1)}, bf16[4,512,704]{2,1,0:T(8,128)(2,1)}, bf16[4,96,2048]{2,1,0:T(8,128)(2,1)S(1)}) custom-call(bf16[128,2048]{1,0:T(8,128)(2,1)S(1)} %multiply_convert_fusion.13.refs_0_, bf16[512,704]{1,0:T(8,128)(2,1)S(1)} %concatenate.58.refs_1_, bf16[96,2048]{1,0:T(8,128)(2,1)S(1)} %pad.31.refs_2_), custom_call_target="tpu_custom_call" | custom-call | bytes 150000000 | tf_op jit(solution)/shard_map/pallas_call | solution.py:555
  298.9 170.1 %shard_map.300 = (bf16[960,1024]{1,0:T(8,128)(2,1)S(1)}, bf16[4,2,512,704]{3,2,1,0:T(8,128)(2,1)}, bf16[4,2,96,2048]{3,2,1,0:T(8,128)(2,1)}) custom-call(bf16[960,1024]{1,0:T(8,128)(2,1)S(1)} %fusion.12.refs_0_, bf16[4,512,704]{2,1,0:T(8,128)(2,1)} %bitcast.288, bf16[4,96,2048]{2,1,0:T(8,128)(2,1)S(1)} %pad.32.refs_2_), custom_call_target="tpu_custom_call", output_to_operand_aliasing={{0}: (0, {})} | custom-call | bytes 150000000 | tf_op jit(solution)/shard_map/pallas_call | solution.py:555
  481.0 13.2 %fusion.93 = f32[2,480,1408]{2,1,0:T(8,128)} fusion(bf16[2,480,2048]{2,1,0:T(8,128)(2,1)} %bitcast.372, bf16[2,2048,1408]{2,1,0:T(8,128)(2,1)} %all-gather.4.cloned.1.call-done), kind=kOutput, calls=%fused_computation.259 | convolution fusion | flops 5536481280 | bytes 20873216 | tf_op jit(solution)/shard_map/nmh,nhq->nmq/dot_general | solution.py:847
  494.3 14.0 %multiply_convert_fusion.5 = (bf16[2,480,1408]{2,1,0:T(8,128)(2,1)S(1)}, f32[2,480,1408]{2,1,0:T(8,128)}) fusion(f32[2,480,1408]{2,1,0:T(8,128)} %fusion.93, bf16[2,480,2048]{2,1,0:T(8,128)(2,1)} %bitcast.373, bf16[2,2048,1408]{2,1,0:T(8,128)(2,1)} %all-gather.6.cloned.1.call-done), kind=kOutput, calls=%fused_computation.23 | convolution fusion | flops 5544591360 | bytes 28983296 | tf_op jit(solution)/shard_map/nmh,nhq->nmq/dot_general | solution.py:850
  508.2 9.2 convolution_convert_fusion.2.refs_1_
  519.7 10.2 shard_map.301
  533.4 10.3 fusion.94
  543.8 7.5 multiply_convert_fusion.4
  552.8 9.5 convolution_convert_fusion.refs_3_
  576.3 9.2 fusion.44
  585.5 10.0 convolution_convert_fusion.1.refs_2_
  608.7 10.1 fusion.95
  618.8 12.3 %add_convert_fusion.2 = bf16[2,480,2048]{2,1,0:T(8,128)(2,1)} fusion(f32[2,480,2048]{2,1,0:T(8,128)S(1)} %fusion.95, bf16[2,480,1408]{2,1,0:T(8,128)(2,1)} %get-tuple-element.61, bf16[2,2048,1408]{2,1,0:T(8,128)(2,1)} %all-gather.6.cloned.1.call-done), kind=kOutput, calls=%fused_computation.14 | convolution fusion | flops 5540413440 | bytes 26034176 | tf_op jit(solution)/shard_map/sta,sra->str/dot_general | solution.py:872
  631.1 8.3 add_convert_fusion.1
  639.4 54.3 %shard_map.304 = (f32[128,2048]{1,0:T(8,128)S(1)}, f32[128,128]{1,0:T(8,128)S(1)}) custom-call(bf16[4,2,128,2048]{3,2,1,0:T(8,128)(2,1)S(1)} %bitcast.272, bf16[4,2,128,128]{3,2,1,0:T(8,128)(2,1)S(1)} %maximum_maximum_fusion.1.refs_1_), custom_call_target="tpu_custom_call" | custom-call | bytes 150000000 | tf_op jit(solution)/shard_map/pallas_call | solution.py:555
  709.5 7.6 convolution_convert_fusion.9
  722.3 17.9 %shard_map.305 = bf16[8,128,256]{2,1,0:T(8,128)(2,1)S(1)} custom-call(bf16[8,128,256]{2,1,0:T(8,128)(2,1)S(1)} %bitcast.275), custom_call_target="tpu_custom_call" | custom-call | bytes 150000000 | tf_op jit(solution)/shard_map/pallas_call | solution.py:555
  781.2 9.7 multiply_convert_fusion.2
  813.7 83.7 %shard_map.308 = (f32[128,640]{1,0:T(8,128)S(1)}, f32[128,2048]{1,0:T(8,128)S(1)}, f32[128,2048]{1,0:T(8,128)S(1)}) custom-call(bf16[4,2,128,640]{3,2,1,0:T(8,128)(2,1)S(1)} %copy-done.7, bf16[4,2,128,2048]{3,2,1,0:T(8,128)(2,1)} %bitcast.283, bf16[4,2,128,2048]{3,2,1,0:T(8,128)(2,1)} %bitcast.282), custom_call_target="tpu_custom_call" | custom-call | bytes 270000000 | tf_op jit(solution)/shard_map/pallas_call | solution.py:555
  921.3 9.1 collective-permute-done.16
  931.5 95.6 %shard_map.310 = (bf16[4,2,64,2048]{3,2,1,0:T(8,128)(2,1)S(1)}, bf16[4,2,512,384]{3,2,1,0:T(8,128)(2,1)}, bf16[4,2,128,512]{3,2,1,0:T(8,128)(2,1)S(1)}, bf16[4,2...) custom-call(bf16[4,2,64,2048]{3,2,1,0:T(8,128)(2,1)} %bitcast.309, bf16[512,384]{1,0:T(8,128)(2,1)S(1)} %add_convert_fusion.4.refs_1_, ...), custom_call_target="tpu_custom_call" | custom-call | bytes 150000000 | tf_op jit(solution)/shard_map/pallas_call | solution.py:555
  (543 shorter events, 304.8 us)
Async XLA Ops:
  7.2 473.8 %all-gather.4.cloned.1.call-start = ((), (), s32[]{:S(2)}) async-start(), calls=%async_computation.3 | async-start | bytes 14417920 | tf_op jit(solution)/shard_map/all_gather | solution.py:736
  111.5 382.8 %all-gather.6.cloned.1.call-start = ((), (), s32[]{:S(2)}) async-start(), calls=%async_computation.4 | async-start | bytes 14417920 | tf_op jit(solution)/shard_map/all_gather | solution.py:737
  115.2 418.2 %all-gather.8.cloned.1.call-start = ((), (), s32[]{:S(2)}) async-start(), calls=%async_computation.5 | async-start | bytes 14417920 | tf_op jit(solution)/shard_map/all_gather | solution.py:738
  119.5 927.2 %reduce-scatter.8.cloned.1.call-start = ((), (), s32[]{:S(2)}) async-start(), calls=%async_computation.8 | async-start | bytes 14417920 | tf_op jit(solution)/shard_map/reduce_scatter | solution.py:866
  517.5 534.3 %reduce-scatter.6.cloned.1.call-start = ((), (), s32[]{:S(2)}) async-start(), calls=%async_computation.7 | async-start | bytes 14417920 | tf_op jit(solution)/shard_map/reduce_scatter | solution.py:868
  562.3 494.3 %reduce-scatter.4.cloned.1.call-start = ((), (), s32[]{:S(2)}) async-start(), calls=%async_computation.6 | async-start | bytes 14417920 | tf_op jit(solution)/shard_map/reduce_scatter | solution.py:867
  568.0 37.8 %collective-permute-start.5 = (bf16[128,512]{1,0:T(8,128)(2,1)S(1)}, bf16[128,512]{1,0:T(8,128)(2,1)S(1)}, u32[]{:S(2)}, u32[]{:S(2)}) collective-permute-start(bf16[128,512]{1,0:T(8,128)(2,1)S(1)} %bitcast.346), channel_id=1, source_target_pairs={{0,3},{1,2},{2,1},{3,0},{4,7},{5,6},{6,5},{7,4},{8,11},{9,10},{10,... | collective-permute-start | bytes 393224 | tf_op jit(solution)/shard_map/ppermute | solution.py:573
  569.7 36.2 %collective-permute-start.4 = (bf16[128,512]{1,0:T(8,128)(2,1)S(1)}, bf16[128,512]{1,0:T(8,128)(2,1)S(1)}, u32[]{:S(2)}, u32[]{:S(2)}) collective-permute-start(bf16[128,512]{1,0:T(8,128)(2,1)S(1)} %bitcast.347), channel_id=1, source_target_pairs={{0,2},{1,3},{2,0},{3,1},{4,6},{5,7},{6,4},{7,5},{8,10},{9,11},{10,... | collective-permute-start | bytes 393224 | tf_op jit(solution)/shard_map/ppermute | solution.py:573
  571.4 34.5 %collective-permute-start.3 = (bf16[128,512]{1,0:T(8,128)(2,1)S(1)}, bf16[128,512]{1,0:T(8,128)(2,1)S(1)}, u32[]{:S(2)}, u32[]{:S(2)}) collective-permute-start(bf16[128,512]{1,0:T(8,128)(2,1)S(1)} %bitcast.348), channel_id=1, source_target_pairs={{0,1},{1,0},{2,3},{3,2},{4,5},{5,4},{6,7},{7,6},{8,9},{9,8},{10,11... | collective-permute-start | bytes 393224 | tf_op jit(solution)/shard_map/ppermute | solution.py:573
  572.1 23.5 %collective-permute-start.12 = (bf16[128,512]{1,0:T(8,128)(2,1)S(1)}, bf16[128,512]{1,0:T(8,128)(2,1)S(1)}, u32[]{:S(2)}, u32[]{:S(2)}) collective-permute-start(bf16[128,512]{1,0:T(8,128)(2,1)S(1)} %bitcast.351), channel_id=1, source_target_pairs={{0,1},{1,0},{2,3},{3,2},{4,5},{5,4},{6,7},{7,6},{8,9},{9,8},{10,11... | collective-permute-start | bytes 393224 | tf_op jit(solution)/shard_map/ppermute | solution.py:573
  573.8 27.9 %collective-permute-start.13 = (bf16[128,512]{1,0:T(8,128)(2,1)S(1)}, bf16[128,512]{1,0:T(8,128)(2,1)S(1)}, u32[]{:S(2)}, u32[]{:S(2)}) collective-permute-start(bf16[128,512]{1,0:T(8,128)(2,1)S(1)} %bitcast.349), channel_id=1, source_target_pairs={{0,2},{1,3},{2,0},{3,1},{4,6},{5,7},{6,4},{7,5},{8,10},{9,11},{10,... | collective-permute-start | bytes 393224 | tf_op jit(solution)/shard_map/ppermute | solution.py:573
  595.6 9.4 collective-permute-start.14
  700.9 104.9 %collective-permute-start.2 = (bf16[128,2048]{1,0:T(8,128)(2,1)}, bf16[128,2048]{1,0:T(8,128)(2,1)}, u32[]{:S(2)}, u32[]{:S(2)}) collective-permute-start(bf16[128,2048]{1,0:T(8,128)(2,1)} %fusion.84), channel_id=1, source_target_pairs={{0,3},{1,2},{2,1},{3,0},{4,7},{5,6},{6,5},{7,4},{8,11},{9,10},{10,... | collective-permute-start | bytes 1572872 | tf_op jit(solution)/shard_map/ppermute | solution.py:573
  701.9 104.5 %collective-permute-start.1 = (bf16[128,2048]{1,0:T(8,128)(2,1)}, bf16[128,2048]{1,0:T(8,128)(2,1)}, u32[]{:S(2)}, u32[]{:S(2)}) collective-permute-start(bf16[128,2048]{1,0:T(8,128)(2,1)} %fusion.84), channel_id=1, source_target_pairs={{0,2},{1,3},{2,0},{3,1},{4,6},{5,7},{6,4},{7,5},{8,10},{9,11},{10,... | collective-permute-start | bytes 1572872 | tf_op jit(solution)/shard_map/ppermute | solution.py:573
  703.6 104.5 %collective-permute-start = (bf16[128,2048]{1,0:T(8,128)(2,1)}, bf16[128,2048]{1,0:T(8,128)(2,1)}, u32[]{:S(2)}, u32[]{:S(2)}) collective-permute-start(bf16[128,2048]{1,0:T(8,128)(2,1)} %fusion.84), channel_id=1, source_target_pairs={{0,1},{1,0},{2,3},{3,2},{4,5},{5,4},{6,7},{7,6},{8,9},{9,8},{10,11... | collective-permute-start | bytes 1572872 | tf_op jit(solution)/shard_map/ppermute | solution.py:573
  771.2 144.0 %collective-permute-start.9 = (bf16[128,512]{1,0:T(8,128)(2,1)}, bf16[128,512]{1,0:T(8,128)(2,1)}, u32[]{:S(2)}, u32[]{:S(2)}) collective-permute-start(bf16[128,512]{1,0:T(8,128)(2,1)} %get-tuple-element.202), channel_id=1, source_target_pairs={{0,1},{1,0},{2,3},{3,2},{4,5},{5,4},{6,7},{7,6},{8,9},{9,8},{10,11... | collective-permute-start | bytes 393224 | tf_op jit(solution)/shard_map/ppermute | solution.py:573
  772.2 144.7 %collective-permute-start.11 = (bf16[128,512]{1,0:T(8,128)(2,1)}, bf16[128,512]{1,0:T(8,128)(2,1)}, u32[]{:S(2)}, u32[]{:S(2)}) collective-permute-start(bf16[128,512]{1,0:T(8,128)(2,1)} %get-tuple-element.203), channel_id=1, source_target_pairs={{0,3},{1,2},{2,1},{3,0},{4,7},{5,6},{6,5},{7,4},{8,11},{9,10},{10,... | collective-permute-start | bytes 393224 | tf_op jit(solution)/shard_map/ppermute | solution.py:573
  805.7 105.2 %collective-permute-start.8 = (bf16[512,384]{1,0:T(8,128)(2,1)}, bf16[512,384]{1,0:T(8,128)(2,1)}, u32[]{:S(2)}, u32[]{:S(2)}) collective-permute-start(bf16[512,384]{1,0:T(8,128)(2,1)} %get-tuple-element.191), channel_id=1, source_target_pairs={{0,3},{1,2},{2,1},{3,0},{4,7},{5,6},{6,5},{7,4},{8,11},{9,10},{10,... | collective-permute-start | bytes 1179656 | tf_op jit(solution)/shard_map/ppermute | solution.py:573
  806.3 105.4 %collective-permute-start.7 = (bf16[512,384]{1,0:T(8,128)(2,1)}, bf16[512,384]{1,0:T(8,128)(2,1)}, u32[]{:S(2)}, u32[]{:S(2)}) collective-permute-start(bf16[512,384]{1,0:T(8,128)(2,1)} %get-tuple-element.192), channel_id=1, source_target_pairs={{0,2},{1,3},{2,0},{3,1},{4,6},{5,7},{6,4},{7,5},{8,10},{9,11},{10,... | collective-permute-start | bytes 1179656 | tf_op jit(solution)/shard_map/ppermute | solution.py:573
  808.1 104.9 %collective-permute-start.6 = (bf16[512,384]{1,0:T(8,128)(2,1)}, bf16[512,384]{1,0:T(8,128)(2,1)}, u32[]{:S(2)}, u32[]{:S(2)}) collective-permute-start(bf16[512,384]{1,0:T(8,128)(2,1)} %get-tuple-element.193), channel_id=1, source_target_pairs={{0,1},{1,0},{2,3},{3,2},{4,5},{5,4},{6,7},{7,6},{8,9},{9,8},{10,11... | collective-permute-start | bytes 1179656 | tf_op jit(solution)/shard_map/ppermute | solution.py:573
  911.0 9.3 collective-permute-start.10
  911.8 18.7 %collective-permute-start.16 = (bf16[128,640]{1,0:T(8,128)(2,1)}, bf16[128,640]{1,0:T(8,128)(2,1)S(1)}, u32[]{:S(2)}, u32[]{:S(2)}) collective-permute-start(bf16[128,640]{1,0:T(8,128)(2,1)} %get-tuple-element.211), channel_id=1, source_target_pairs={{0,2},{1,3},{2,0},{3,1},{4,6},{5,7},{6,4},{7,5},{8,10},{9,11},{10,... | collective-permute-start | bytes 491528 | tf_op jit(solution)/shard_map/ppermute | solution.py:573
  913.0 17.5 %collective-permute-start.15 = (bf16[128,640]{1,0:T(8,128)(2,1)}, bf16[128,640]{1,0:T(8,128)(2,1)S(1)}, u32[]{:S(2)}, u32[]{:S(2)}) collective-permute-start(bf16[128,640]{1,0:T(8,128)(2,1)} %get-tuple-element.211), channel_id=1, source_target_pairs={{0,1},{1,0},{2,3},{3,2},{4,5},{5,4},{6,7},{7,6},{8,9},{9,8},{10,11... | collective-permute-start | bytes 491528 | tf_op jit(solution)/shard_map/ppermute | solution.py:573
  915.2 15.3 %collective-permute-start.17 = (bf16[128,640]{1,0:T(8,128)(2,1)}, bf16[128,640]{1,0:T(8,128)(2,1)S(1)}, u32[]{:S(2)}, u32[]{:S(2)}) collective-permute-start(bf16[128,640]{1,0:T(8,128)(2,1)} %get-tuple-element.211), channel_id=1, source_target_pairs={{0,3},{1,2},{2,1},{3,0},{4,7},{5,6},{6,5},{7,4},{8,11},{9,10},{10,... | collective-permute-start | bytes 491528 | tf_op jit(solution)/shard_map/ppermute | solution.py:573
  (141 other events, 1678.6 us)
Sparse Core Ops, SparseCore 0:
  111.6 125.9 all-gather.3
  240.1 172.3 all-gather.5
  414.3 113.6 all-gather.7
  530.9 123.3 reduce-scatter.7
  657.3 140.1 reduce-scatter.5
  800.4 137.6 reduce-scatter.3

commit v5 on v4

--- a/solution.py
+++ b/solution.py
@@ -320,6 +320,33 @@
         return out
 
 
+class ExchangeDp(Part):
+    axes = ("dp",)
+
+    def result(self):
+        return jax.ShapeDtypeStruct(self.value.shape, self.value.dtype), pl.ANY
+
+    def scratch(self):
+        return [pltpu.SemaphoreType.DMA((self.groups,)) for _ in range(2)]
+
+    def steps(self, block, out, scratch, place):
+        chip, core, group = place
+        send, recv = scratch
+        local_copy = pltpu.make_async_copy(block.at[group], out.at[group], send.at[0])
+        local_copy.start()
+        copies = [
+            flip_copy(block.at[group ^ p], out.at[group], send.at[p], recv.at[p], {"dp": group ^ p})
+            for p in range(1, self.groups)
+        ]
+        yield
+        for copy in copies:
+            copy.wait()
+        local_copy.wait()
+
+    def finish(self, out):
+        return out
+
+
 def add_rows(target, sources):
     rows = target.shape[0]
 
@@ -590,13 +617,14 @@
     return jnp.stack([value] + [swap_dp(value, p) for p in range(1, lax.axis_size("dp"))])
 
 
-def background_exchange(value):
+def own_first(value):
     me = lax.axis_index("dp")
-    pieces = [
-        lax.dynamic_index_in_dim(value, me ^ p, 0, keepdims=False)
-        for p in range(lax.axis_size("dp"))
-    ]
-    return jnp.stack([pieces[0]] + [swap_dp(pieces[p], p) for p in range(1, len(pieces))])
+    return jnp.stack(
+        [
+            lax.dynamic_index_in_dim(value, me ^ p, 0, keepdims=False)
+            for p in range(lax.axis_size("dp"))
+        ]
+    )
 
 
 def after(values, others):
@@ -882,11 +910,16 @@
     d_gate_pack = jnp.concatenate(
         [d_gate_high, d_gate_low, jnp.zeros((group, 128 - 2 * experts), BF16)], axis=1
     )
-    d_ffn, d_gate = communicate(
+    def by_group(rows):
+        return jnp.swapaxes(rows.reshape(tokens, dp_count, -1), 0, 1)
+
+    d_ffn, d_gate, left_out, left_latent = communicate(
         6,
         [
             ScatterSeq(d_ffn_partial.astype(BF16).reshape(seq_count, tokens, width)),
             ScatterSeq(d_gate_pack.reshape(seq_count, tokens, 128)),
+            ExchangeDp(by_group(flat_out)),
+            ExchangeDp(by_group(own(attn_in))),
         ],
     )
     d_gate = d_gate[:, :experts] + d_gate[:, experts : 2 * experts]
@@ -939,13 +972,9 @@
     grad_expand = t_dot(latent_normed, d_key_value).astype(BF16)
     grad_query = t_dot(attn_in, d_q_raw).astype(BF16)
 
-    def by_group(rows):
-        return jnp.swapaxes(rows.reshape(tokens, dp_count, -1), 0, 1)
-
-    left_out = background_exchange(by_group(flat_out))
+    left_out, left_latent = own_first(left_out), own_first(left_latent)
     right_out = background_gather(d_attn)
     right_out, d_attn_part = after([right_out, d_attn_part], [left_out])
-    left_latent = background_exchange(by_group(own(attn_in)))
     query_pieces = background_pieces(grad_query.reshape(dp_count, shard, hq))
     expand_pieces = background_pieces(grad_expand.reshape(dp_count, rank_shard, hkv))
     d_latent_sum, d_attn_in, moe = communicate(

time: 1070 us -> 1070 us (level)
    ppermute x18 -> x12, starting transfers between devices: 22.1 us -> 14.2 us  [swap_dp(): lax.ppermute(value, 'dp', [(i, i ^ mask) for i in range(lax.axis_size('dp...]
    unnamed x296 -> x304, local copies, waits for them, and re-layouts: 26.6 us -> 31.6 us
  transfers between devices with their start and end apart: 24 -> 18, of which waited for: 3 -> 3; matrix products, arithmetic and copies ran while one was open for 35% -> 36% of each run, Pallas kernels for 48% -> 48%
where the time goes in v5:
time: 1070 us; the launch traced here: 1060 us
  Pallas kernels  597 us (56%)
  matrix products  223 us (21%)
  other arithmetic  103 us (10%)
  local copies, waits for them, and re-layouts  94.9 us (9%)
  between operations  17 us (2%)
  starting transfers between devices  14.5 us (1%)
  waiting for transfers between devices  12 us (1%)
    pallas_call x8, Pallas kernels, communicate(): pl.pallas_call(kernel, out_shape=[shape for shape, _ in results], in_spec...  587 us
    dot_general x9, matrix products, dot(): return jnp.dot(left, right, preferred_element_type=F32)  39.3 us
    unnamed x304, local copies, waits for them, and re-layouts  31.6 us
    dot_general x8, matrix products, t_dot(): lax.dot_general(left, right, (((0,), (0,)), ((), ())), preferred_element_...  29.6 us
    dot_general x6, matrix products, dot_t(): lax.dot_general(left, right, (((1,), (1,)), ((), ())), preferred_element_...  27.4 us
  transfers between devices with their start and end apart: 18, of which 3 were waited for; matrix products, arithmetic and copies ran while one was open for 36% of the time, Pallas kernels for 48%

profile of v5, /device:TPU:0, one launch (start us, length us, event | category | flops | bytes accessed | tf_op | source)
XLA Modules:
  0.0 1061.8 jit_solution(3815493316506572626)
XLA Ops:
  21.3 87.2 %shard_map.297 = (bf16[4,2,128,2048]{3,2,1,0:T(8,128)(2,1)}, bf16[4,2,128,128]{3,2,1,0:T(8,128)(2,1)S(1)}, bf16[4,544,512]{2,1,0:T(8,128)(2,1)S(1)}, bf16[4,2,25...) custom-call(bf16[128,2048]{1,0:T(8,128)(2,1)S(1)} %bitcast.258, ...), custom_call_target="tpu_custom_call" | custom-call | bytes 150000000 | tf_op jit(solution)/shard_map/pallas_call | solution.py:582
  169.1 8.4 fusion.87
  182.2 13.2 %shard_map.298 = bf16[8,128,256]{2,1,0:T(8,128)(2,1)S(1)} custom-call(bf16[8,128,256]{2,1,0:T(8,128)(2,1)S(1)} %copy.258.refs_0_), custom_call_target="tpu_custom_call" | custom-call | bytes 150000000 | tf_op jit(solution)/shard_map/pallas_call | solution.py:582
  204.3 65.9 %shard_map.299 = (bf16[4,2,128,2048]{3,2,1,0:T(8,128)(2,1)}, bf16[4,512,704]{2,1,0:T(8,128)(2,1)}, bf16[4,96,2048]{2,1,0:T(8,128)(2,1)S(1)}) custom-call(bf16[128,2048]{1,0:T(8,128)(2,1)S(1)} %multiply_convert_fusion.13.refs_0_, bf16[512,704]{1,0:T(8,128)(2,1)S(1)} %concatenate.58.refs_1_, bf16[96,2048]{1,0:T(8,128)(2,1)S(1)} %pad.31.refs_2_), custom_call_target="tpu_custom_call" | custom-call | bytes 150000000 | tf_op jit(solution)/shard_map/pallas_call | solution.py:582
  298.9 170.2 %shard_map.300 = (bf16[960,1024]{1,0:T(8,128)(2,1)S(1)}, bf16[4,2,512,704]{3,2,1,0:T(8,128)(2,1)}, bf16[4,2,96,2048]{3,2,1,0:T(8,128)(2,1)}) custom-call(bf16[960,1024]{1,0:T(8,128)(2,1)S(1)} %fusion.12.refs_0_, bf16[4,512,704]{2,1,0:T(8,128)(2,1)} %bitcast.277, bf16[4,96,2048]{2,1,0:T(8,128)(2,1)S(1)} %pad.32.refs_2_), custom_call_target="tpu_custom_call", output_to_operand_aliasing={{0}: (0, {})} | custom-call | bytes 150000000 | tf_op jit(solution)/shard_map/pallas_call | solution.py:582
  481.0 13.2 %fusion.93 = f32[2,480,1408]{2,1,0:T(8,128)} fusion(bf16[2,480,2048]{2,1,0:T(8,128)(2,1)} %bitcast.346, bf16[2,2048,1408]{2,1,0:T(8,128)(2,1)} %all-gather.4.cloned.1.call-done), kind=kOutput, calls=%fused_computation.259 | convolution fusion | flops 5536481280 | bytes 20873216 | tf_op jit(solution)/shard_map/nmh,nhq->nmq/dot_general | solution.py:875
  494.3 14.0 %multiply_convert_fusion.5 = (bf16[2,480,1408]{2,1,0:T(8,128)(2,1)S(1)}, f32[2,480,1408]{2,1,0:T(8,128)}) fusion(f32[2,480,1408]{2,1,0:T(8,128)} %fusion.93, bf16[2,480,2048]{2,1,0:T(8,128)(2,1)} %bitcast.347, bf16[2,2048,1408]{2,1,0:T(8,128)(2,1)} %all-gather.6.cloned.1.call-done), kind=kOutput, calls=%fused_computation.23 | convolution fusion | flops 5544591360 | bytes 28983296 | tf_op jit(solution)/shard_map/nmh,nhq->nmq/dot_general | solution.py:878
  508.2 9.2 convolution_convert_fusion.2.refs_1_
  519.7 10.2 shard_map.301
  533.4 10.3 fusion.94
  543.8 7.5 multiply_convert_fusion.4
  552.9 9.5 convolution_convert_fusion.refs_3_
  577.2 9.2 fusion.44
  586.3 10.0 convolution_convert_fusion.1.refs_2_
  598.2 10.1 fusion.95
  608.4 11.7 %add_convert_fusion.2 = bf16[2,480,2048]{2,1,0:T(8,128)(2,1)} fusion(f32[2,480,2048]{2,1,0:T(8,128)S(1)} %fusion.95, bf16[2,480,1408]{2,1,0:T(8,128)(2,1)} %get-tuple-element.63, bf16[2,2048,1408]{2,1,0:T(8,128)(2,1)} %all-gather.6.cloned.1.call-done), kind=kOutput, calls=%fused_computation.14 | convolution fusion | flops 5540413440 | bytes 26034176 | tf_op jit(solution)/shard_map/sta,sra->str/dot_general | solution.py:900
  620.0 9.6 add_convert_fusion.1
  629.7 57.1 %shard_map.304 = (f32[128,2048]{1,0:T(8,128)S(1)}, f32[128,128]{1,0:T(8,128)S(1)}, bf16[4,128,512]{2,1,0:T(8,128)(2,1)S(1)}, bf16[4,128,512]{2,1,0:T(8,128)(2,1)S(1)}) custom-call(bf16[4,2,128,2048]{3,2,1,0:T(8,128)(2,1)} %bitcast.290, bf16[4,2,128,128]{3,2,1,0:T(8,128)(2,1)S(1)} %maximum_maximum_fusion.1.refs_1_, bf16[4,128,512]{2,1,0:T(8,128)(2,1)S(1)} %bitcast.264, ...), custom_call_target="tpu_custom_call" | custom-call | bytes 150000000 | tf_op jit(solution)/shard_map/pallas_call | solution.py:582
  704.3 7.3 convolution_convert_fusion.9
  716.7 17.5 %shard_map.305 = bf16[8,128,256]{2,1,0:T(8,128)(2,1)S(1)} custom-call(bf16[8,128,256]{2,1,0:T(8,128)(2,1)S(1)} %bitcast.262), custom_call_target="tpu_custom_call" | custom-call | bytes 150000000 | tf_op jit(solution)/shard_map/pallas_call | solution.py:582
  778.5 7.0 multiply_convert_fusion.2
  809.0 83.8 %shard_map.308 = (f32[128,640]{1,0:T(8,128)S(1)}, f32[128,2048]{1,0:T(8,128)S(1)}, f32[128,2048]{1,0:T(8,128)S(1)}) custom-call(bf16[4,2,128,640]{3,2,1,0:T(8,128)(2,1)S(1)} %copy-done.7, bf16[4,2,128,2048]{3,2,1,0:T(8,128)(2,1)} %bitcast.272, bf16[4,2,128,2048]{3,2,1,0:T(8,128)(2,1)} %bitcast.271), custom_call_target="tpu_custom_call" | custom-call | bytes 270000000 | tf_op jit(solution)/shard_map/pallas_call | solution.py:582
  917.9 8.9 collective-permute-done.10
  928.3 92.1 %shard_map.310 = (bf16[4,2,64,2048]{3,2,1,0:T(8,128)(2,1)S(1)}, bf16[4,2,512,384]{3,2,1,0:T(8,128)(2,1)}, bf16[4,2,128,512]{3,2,1,0:T(8,128)(2,1)S(1)}, bf16[4,2...) custom-call(bf16[4,2,64,2048]{3,2,1,0:T(8,128)(2,1)} %bitcast.298, bf16[512,384]{1,0:T(8,128)(2,1)S(1)} %add_convert_fusion.4.refs_1_, ...), custom_call_target="tpu_custom_call" | custom-call | bytes 150000000 | tf_op jit(solution)/shard_map/pallas_call | solution.py:582
  (535 shorter events, 301.7 us)
Async XLA Ops:
  7.2 473.8 %all-gather.4.cloned.1.call-start = ((), (), s32[]{:S(2)}) async-start(), calls=%async_computation.3 | async-start | bytes 14417920 | tf_op jit(solution)/shard_map/all_gather | solution.py:764
  21.3 88.3 %copy-start.60 = (bf16[2,512,1408]{2,1,0:T(8,128)(2,1)S(1)}, bf16[2,512,1408]{2,1,0:T(8,128)(2,1)}, u32[]{:S(2)}) copy-start(bf16[2,512,1408]{2,1,0:T(8,128)(2,1)} %param.33) | copy-start | bytes 8650756
  111.5 382.8 %all-gather.6.cloned.1.call-start = ((), (), s32[]{:S(2)}) async-start(), calls=%async_computation.4 | async-start | bytes 14417920 | tf_op jit(solution)/shard_map/all_gather | solution.py:765
  115.2 418.2 %all-gather.8.cloned.1.call-start = ((), (), s32[]{:S(2)}) async-start(), calls=%async_computation.5 | async-start | bytes 14417920 | tf_op jit(solution)/shard_map/all_gather | solution.py:766
  119.4 920.5 %reduce-scatter.8.cloned.1.call-start = ((), (), s32[]{:S(2)}) async-start(), calls=%async_computation.8 | async-start | bytes 14417920 | tf_op jit(solution)/shard_map/reduce_scatter | solution.py:894
  298.5 170.6 %copy-start.97 = (s32[2,1024]{1,0:T(2,128)}, s32[2,1024]{1,0:T(2,128)S(1)}, u32[]{:S(2)}) copy-start(s32[2,1024]{1,0:T(2,128)S(1)} %compare_select_fusion) | copy-start | bytes 24580
  298.5 171.1 %copy-start.36 = (bf16[4,2,128,2048]{3,2,1,0:T(8,128)(2,1)S(1)}, bf16[4,2,128,2048]{3,2,1,0:T(8,128)(2,1)}, u32[]{:S(2)}) copy-start(bf16[4,2,128,2048]{3,2,1,0:T(8,128)(2,1)} %get-tuple-element.54) | copy-start | bytes 12582916
  517.5 527.7 %reduce-scatter.6.cloned.1.call-start = ((), (), s32[]{:S(2)}) async-start(), calls=%async_computation.7 | async-start | bytes 14417920 | tf_op jit(solution)/shard_map/reduce_scatter | solution.py:896
  562.4 487.7 %reduce-scatter.4.cloned.1.call-start = ((), (), s32[]{:S(2)}) async-start(), calls=%async_computation.6 | async-start | bytes 14417920 | tf_op jit(solution)/shard_map/reduce_scatter | solution.py:895
  695.8 105.1 %collective-permute-start.2 = (bf16[128,2048]{1,0:T(8,128)(2,1)}, bf16[128,2048]{1,0:T(8,128)(2,1)}, u32[]{:S(2)}, u32[]{:S(2)}) collective-permute-start(bf16[128,2048]{1,0:T(8,128)(2,1)} %fusion.84), channel_id=1, source_target_pairs={{0,3},{1,2},{2,1},{3,0},{4,7},{5,6},{6,5},{7,4},{8,11},{9,10},{10,... | collective-permute-start | bytes 1572872 | tf_op jit(solution)/shard_map/ppermute | solution.py:600
  696.4 106.4 %collective-permute-start.1 = (bf16[128,2048]{1,0:T(8,128)(2,1)}, bf16[128,2048]{1,0:T(8,128)(2,1)}, u32[]{:S(2)}, u32[]{:S(2)}) collective-permute-start(bf16[128,2048]{1,0:T(8,128)(2,1)} %fusion.84), channel_id=1, source_target_pairs={{0,2},{1,3},{2,0},{3,1},{4,6},{5,7},{6,4},{7,5},{8,10},{9,11},{10,... | collective-permute-start | bytes 1572872 | tf_op jit(solution)/shard_map/ppermute | solution.py:600
  698.7 104.2 %collective-permute-start = (bf16[128,2048]{1,0:T(8,128)(2,1)}, bf16[128,2048]{1,0:T(8,128)(2,1)}, u32[]{:S(2)}, u32[]{:S(2)}) collective-permute-start(bf16[128,2048]{1,0:T(8,128)(2,1)} %fusion.84), channel_id=1, source_target_pairs={{0,1},{1,0},{2,3},{3,2},{4,5},{5,4},{6,7},{7,6},{8,9},{9,8},{10,11... | collective-permute-start | bytes 1572872 | tf_op jit(solution)/shard_map/ppermute | solution.py:600
  766.1 146.4 %collective-permute-start.6 = (bf16[128,512]{1,0:T(8,128)(2,1)}, bf16[128,512]{1,0:T(8,128)(2,1)}, u32[]{:S(2)}, u32[]{:S(2)}) collective-permute-start(bf16[128,512]{1,0:T(8,128)(2,1)} %get-tuple-element.190), channel_id=1, source_target_pairs={{0,1},{1,0},{2,3},{3,2},{4,5},{5,4},{6,7},{7,6},{8,9},{9,8},{10,11... | collective-permute-start | bytes 393224 | tf_op jit(solution)/shard_map/ppermute | solution.py:600
  767.6 146.9 %collective-permute-start.8 = (bf16[128,512]{1,0:T(8,128)(2,1)}, bf16[128,512]{1,0:T(8,128)(2,1)}, u32[]{:S(2)}, u32[]{:S(2)}) collective-permute-start(bf16[128,512]{1,0:T(8,128)(2,1)} %get-tuple-element.191), channel_id=1, source_target_pairs={{0,3},{1,2},{2,1},{3,0},{4,7},{5,6},{6,5},{7,4},{8,11},{9,10},{10,... | collective-permute-start | bytes 393224 | tf_op jit(solution)/shard_map/ppermute | solution.py:600
  800.9 106.6 %collective-permute-start.5 = (bf16[512,384]{1,0:T(8,128)(2,1)}, bf16[512,384]{1,0:T(8,128)(2,1)}, u32[]{:S(2)}, u32[]{:S(2)}) collective-permute-start(bf16[512,384]{1,0:T(8,128)(2,1)} %get-tuple-element.179), channel_id=1, source_target_pairs={{0,3},{1,2},{2,1},{3,0},{4,7},{5,6},{6,5},{7,4},{8,11},{9,10},{10,... | collective-permute-start | bytes 1179656 | tf_op jit(solution)/shard_map/ppermute | solution.py:600
  802.9 105.8 %collective-permute-start.4 = (bf16[512,384]{1,0:T(8,128)(2,1)}, bf16[512,384]{1,0:T(8,128)(2,1)}, u32[]{:S(2)}, u32[]{:S(2)}) collective-permute-start(bf16[512,384]{1,0:T(8,128)(2,1)} %get-tuple-element.180), channel_id=1, source_target_pairs={{0,2},{1,3},{2,0},{3,1},{4,6},{5,7},{6,4},{7,5},{8,10},{9,11},{10,... | collective-permute-start | bytes 1179656 | tf_op jit(solution)/shard_map/ppermute | solution.py:600
  802.9 106.7 %collective-permute-start.3 = (bf16[512,384]{1,0:T(8,128)(2,1)}, bf16[512,384]{1,0:T(8,128)(2,1)}, u32[]{:S(2)}, u32[]{:S(2)}) collective-permute-start(bf16[512,384]{1,0:T(8,128)(2,1)} %get-tuple-element.181), channel_id=1, source_target_pairs={{0,1},{1,0},{2,3},{3,2},{4,5},{5,4},{6,7},{7,6},{8,9},{9,8},{10,11... | collective-permute-start | bytes 1179656 | tf_op jit(solution)/shard_map/ppermute | solution.py:600
  809.0 85.8 %copy-start.113 = (f32[512]{0:T(512)S(1)}, f32[512]{0:T(512)}, u32[]{:S(2)}) copy-start(f32[512]{0:T(512)} %copy-done.111) | copy-start | bytes 6148
  809.0 85.8 %copy-start.132 = (f32[128]{0:T(128)S(1)}, f32[128]{0:T(128)}, u32[]{:S(2)}) copy-start(f32[128]{0:T(128)} %add_rsqrt_fusion.2) | copy-start | bytes 1540
  809.0 89.9 %copy-start.126 = (f32[128]{0:T(128)S(1)}, f32[128]{0:T(128)}, u32[]{:S(2)}) copy-start(f32[128]{0:T(128)} %add_rsqrt_fusion.3) | copy-start | bytes 1540
  907.5 9.3 collective-permute-start.7
  908.7 18.1 %collective-permute-start.10 = (bf16[128,640]{1,0:T(8,128)(2,1)}, bf16[128,640]{1,0:T(8,128)(2,1)S(1)}, u32[]{:S(2)}, u32[]{:S(2)}) collective-permute-start(bf16[128,640]{1,0:T(8,128)(2,1)} %get-tuple-element.199), channel_id=1, source_target_pairs={{0,2},{1,3},{2,0},{3,1},{4,6},{5,7},{6,4},{7,5},{8,10},{9,11},{10,... | collective-permute-start | bytes 491528 | tf_op jit(solution)/shard_map/ppermute | solution.py:600
  909.5 17.3 %collective-permute-start.9 = (bf16[128,640]{1,0:T(8,128)(2,1)}, bf16[128,640]{1,0:T(8,128)(2,1)S(1)}, u32[]{:S(2)}, u32[]{:S(2)}) collective-permute-start(bf16[128,640]{1,0:T(8,128)(2,1)} %get-tuple-element.199), channel_id=1, source_target_pairs={{0,1},{1,0},{2,3},{3,2},{4,5},{5,4},{6,7},{7,6},{8,9},{9,8},{10,11... | collective-permute-start | bytes 491528 | tf_op jit(solution)/shard_map/ppermute | solution.py:600
  912.6 14.7 %collective-permute-start.11 = (bf16[128,640]{1,0:T(8,128)(2,1)}, bf16[128,640]{1,0:T(8,128)(2,1)S(1)}, u32[]{:S(2)}, u32[]{:S(2)}) collective-permute-start(bf16[128,640]{1,0:T(8,128)(2,1)} %get-tuple-element.199), channel_id=1, source_target_pairs={{0,3},{1,2},{2,1},{3,0},{4,7},{5,6},{6,5},{7,4},{8,11},{9,10},{10,... | collective-permute-start | bytes 491528 | tf_op jit(solution)/shard_map/ppermute | solution.py:600
  (139 other events, 1072.0 us)
Sparse Core Ops, SparseCore 0:
  111.6 125.9 all-gather.3
  240.1 172.3 all-gather.5
  414.3 113.6 all-gather.7
  530.9 120.4 reduce-scatter.7
  654.4 140.4 reduce-scatter.5
  797.8 136.7 reduce-scatter.3

commit v6 on v5

--- a/solution.py
+++ b/solution.py
@@ -226,6 +226,8 @@
 class GatherDp(Part):
     axes = ("dp",)
     cores = False
+    relay = True
+    late = 0
 
     def result(self):
         lead = (self.groups, 2) if self.cores else (self.groups,)
@@ -241,7 +243,7 @@
         send, recv, relay_send, relay_recv = scratch
         count = self.groups
         beside = {"seq": 2 * chip + 1 - core}
-        relayed = count == 4
+        relayed = self.relay and count == 4
 
         def at(rank):
             return out.at[rank, core] if self.cores else out.at[rank]
@@ -263,7 +265,8 @@
             cores.append(
                 flip_copy(block, at(group), send.at[1, 0], recv.at[1, 0], beside)
             )
-        yield
+        for _ in range(1 + self.late):
+            yield
         relays = []
         for p, copy in copies.items():
             copy.wait_recv()
@@ -296,6 +299,11 @@
 
     def finish(self, out):
         return out
+
+
+class GatherDpLate(GatherDp):
+    relay = False
+    late = 4
 
 
 class GatherDpCores(GatherDp):
@@ -972,17 +980,16 @@
     grad_expand = t_dot(latent_normed, d_key_value).astype(BF16)
     grad_query = t_dot(attn_in, d_q_raw).astype(BF16)
 
-    left_out, left_latent = own_first(left_out), own_first(left_latent)
-    right_out = background_gather(d_attn)
-    right_out, d_attn_part = after([right_out, d_attn_part], [left_out])
+    left_latent = own_first(left_latent)
     query_pieces = background_pieces(grad_query.reshape(dp_count, shard, hq))
     expand_pieces = background_pieces(grad_expand.reshape(dp_count, rank_shard, hkv))
-    d_latent_sum, d_attn_in, moe = communicate(
+    d_latent_sum, d_attn_in, moe, right_out = communicate(
         8,
         [
             ScatterSeq(d_latent_part.reshape(seq_count, tokens, latent_width + latent_pad)),
             ScatterSeq(d_attn_part.reshape(seq_count, tokens, width)),
             ScatterSeq(ffn_out.reshape(seq_count, tokens, width)),
+            GatherDpLate(d_attn),
         ],
         micros=90,
     )

time: 1070 us -> 1070 us (level)
  waiting for transfers between devices: 12 us -> 31.1 us
    ppermute x12 -> x9, waiting for transfers between devices: 11.9 us -> 27.4 us  [swap_dp(): lax.ppermute(value, 'dp', [(i, i ^ mask) for i in range(lax.axis_size('dp...]
    unnamed x304 -> x260, local copies, waits for them, and re-layouts: 31.6 us -> 27.8 us
  transfers between devices with their start and end apart: 18 -> 15, of which waited for: 3 -> 5; matrix products, arithmetic and copies ran while one was open for 36% -> 35% of each run, Pallas kernels for 48% -> 47%
where the time goes in v6:
time: 1070 us
  Pallas kernels  593 us (55%)
  matrix products  229 us (21%)
  other arithmetic  94.5 us (9%)
  local copies, waits for them, and re-layouts  90 us (8%)
  waiting for transfers between devices  31.1 us (3%)
  between operations  16.9 us (2%)
  starting transfers between devices  11.1 us (1%)
    pallas_call x8, Pallas kernels, communicate(): pl.pallas_call(kernel, out_shape=[shape for shape, _ in results], in_spec...  582 us
    dot_general x9, matrix products, dot(): return jnp.dot(left, right, preferred_element_type=F32)  36.6 us
    dot_general x8, matrix products, t_dot(): lax.dot_general(left, right, (((0,), (0,)), ((), ())), preferred_element_...  32.4 us
    dot_general x6, matrix products, dot_t(): lax.dot_general(left, right, (((1,), (1,)), ((), ())), preferred_element_...  27.9 us
    unnamed x260, local copies, waits for them, and re-layouts  27.8 us
    ppermute x9, waiting for transfers between devices, swap_dp(): lax.ppermute(value, 'dp', [(i, i ^ mask) for i in range(lax.axis_size('dp...  27.4 us
  transfers between devices with their start and end apart: 15, of which 5 were waited for; matrix products, arithmetic and copies ran while one was open for 35% of the time, Pallas kernels for 47%

profile of v6, /device:TPU:0, one launch (start us, length us, event | category | flops | bytes accessed | tf_op | source)
XLA Modules:
  0.0 1065.2 jit_solution(11521502385658630990)
XLA Ops:
  21.3 87.2 %shard_map.297 = (bf16[4,2,128,2048]{3,2,1,0:T(8,128)(2,1)}, bf16[4,2,128,128]{3,2,1,0:T(8,128)(2,1)S(1)}, bf16[4,544,512]{2,1,0:T(8,128)(2,1)S(1)}, bf16[4,2,25...) custom-call(bf16[128,2048]{1,0:T(8,128)(2,1)S(1)} %bitcast.255, ...), custom_call_target="tpu_custom_call" | custom-call | bytes 150000000 | tf_op jit(solution)/shard_map/pallas_call | solution.py:590
  160.6 8.4 fusion.87
  173.6 13.1 %shard_map.298 = bf16[8,128,256]{2,1,0:T(8,128)(2,1)S(1)} custom-call(bf16[8,128,256]{2,1,0:T(8,128)(2,1)S(1)} %copy.256.refs_0_), custom_call_target="tpu_custom_call" | custom-call | bytes 150000000 | tf_op jit(solution)/shard_map/pallas_call | solution.py:590
  196.2 68.9 %shard_map.299 = (bf16[4,2,128,2048]{3,2,1,0:T(8,128)(2,1)}, bf16[4,512,704]{2,1,0:T(8,128)(2,1)}, bf16[4,96,2048]{2,1,0:T(8,128)(2,1)S(1)}) custom-call(bf16[128,2048]{1,0:T(8,128)(2,1)S(1)} %multiply_convert_fusion.13.refs_0_, bf16[512,704]{1,0:T(8,128)(2,1)S(1)} %concatenate.58.refs_1_, bf16[96,2048]{1,0:T(8,128)(2,1)S(1)} %pad.31.refs_2_), custom_call_target="tpu_custom_call" | custom-call | bytes 150000000 | tf_op jit(solution)/shard_map/pallas_call | solution.py:590
  272.0 6.3 fusion.92
  293.8 163.0 %shard_map.300 = (bf16[960,1024]{1,0:T(8,128)(2,1)S(1)}, bf16[4,2,512,704]{3,2,1,0:T(8,128)(2,1)}, bf16[4,2,96,2048]{3,2,1,0:T(8,128)(2,1)}) custom-call(bf16[960,1024]{1,0:T(8,128)(2,1)S(1)} %fusion.12.refs_0_, bf16[4,512,704]{2,1,0:T(8,128)(2,1)} %bitcast.273, bf16[4,96,2048]{2,1,0:T(8,128)(2,1)S(1)} %pad.32.refs_2_), custom_call_target="tpu_custom_call", output_to_operand_aliasing={{0}: (0, {})} | custom-call | bytes 150000000 | tf_op jit(solution)/shard_map/pallas_call | solution.py:590
  468.7 13.6 %fusion.93 = f32[2,480,1408]{2,1,0:T(8,128)} fusion(bf16[2,480,2048]{2,1,0:T(8,128)(2,1)} %bitcast.339, bf16[2,2048,1408]{2,1,0:T(8,128)(2,1)} %all-gather.4.cloned.1.call-done), kind=kOutput, calls=%fused_computation.253 | convolution fusion | flops 5536481280 | bytes 20873216 | tf_op jit(solution)/shard_map/nmh,nhq->nmq/dot_general | solution.py:883
  482.3 14.0 %multiply_convert_fusion.5 = (bf16[2,480,1408]{2,1,0:T(8,128)(2,1)S(1)}, f32[2,480,1408]{2,1,0:T(8,128)}) fusion(f32[2,480,1408]{2,1,0:T(8,128)} %fusion.93, bf16[2,480,2048]{2,1,0:T(8,128)(2,1)} %bitcast.340, bf16[2,2048,1408]{2,1,0:T(8,128)(2,1)} %all-gather.6.cloned.1.call-done), kind=kOutput, calls=%fused_computation.23 | convolution fusion | flops 5544591360 | bytes 28983296 | tf_op jit(solution)/shard_map/nmh,nhq->nmq/dot_general | solution.py:886
  496.3 9.1 convolution_convert_fusion.2.refs_1_
  507.7 10.5 shard_map.301
  525.3 10.3 fusion.94
  543.3 9.5 convolution_convert_fusion.refs_3_
  564.3 9.6 fusion.44
  573.8 9.6 convolution_convert_fusion.1.refs_2_
  589.7 10.1 fusion.95
  599.8 11.5 %add_convert_fusion.2 = bf16[2,480,2048]{2,1,0:T(8,128)(2,1)} fusion(f32[2,480,2048]{2,1,0:T(8,128)S(1)} %fusion.95, bf16[2,480,1408]{2,1,0:T(8,128)(2,1)} %get-tuple-element.62, bf16[2,2048,1408]{2,1,0:T(8,128)(2,1)} %all-gather.6.cloned.1.call-done), kind=kOutput, calls=%fused_computation.14 | convolution fusion | flops 5540413440 | bytes 26034176 | tf_op jit(solution)/shard_map/sta,sra->str/dot_general | solution.py:908
  611.3 9.9 add_convert_fusion.1
  621.2 57.8 %shard_map.304 = (f32[128,2048]{1,0:T(8,128)S(1)}, f32[128,128]{1,0:T(8,128)S(1)}, bf16[4,128,512]{2,1,0:T(8,128)(2,1)S(1)}, bf16[4,128,512]{2,1,0:T(8,128)(2,1)S(1)}) custom-call(bf16[4,2,128,2048]{3,2,1,0:T(8,128)(2,1)} %bitcast.287, bf16[4,2,128,128]{3,2,1,0:T(8,128)(2,1)S(1)} %maximum_maximum_fusion.1.refs_1_, bf16[4,128,512]{2,1,0:T(8,128)(2,1)S(1)} %bitcast.261, ...), custom_call_target="tpu_custom_call" | custom-call | bytes 150000000 | tf_op jit(solution)/shard_map/pallas_call | solution.py:590
  688.0 7.2 convolution_convert_fusion.9
  700.5 17.3 %shard_map.305 = bf16[8,128,256]{2,1,0:T(8,128)(2,1)S(1)} custom-call(bf16[8,128,256]{2,1,0:T(8,128)(2,1)S(1)} %bitcast.259), custom_call_target="tpu_custom_call" | custom-call | bytes 150000000 | tf_op jit(solution)/shard_map/pallas_call | solution.py:590
  759.8 9.6 multiply_convert_fusion.2
  778.7 84.9 %shard_map.307 = (f32[128,640]{1,0:T(8,128)S(1)}, f32[128,2048]{1,0:T(8,128)S(1)}, f32[128,2048]{1,0:T(8,128)S(1)}, bf16[4,128,2048]{2,1,0:T(8,128)(2,1)}) custom-call(bf16[4,2,128,640]{3,2,1,0:T(8,128)(2,1)S(1)} %maximum_maximum_fusion.refs_0_, bf16[4,2,128,2048]{3,2,1,0:T(8,128)(2,1)} %bitcast.286, bf16[4,2,128,2048]{3,2,1,0:T(8,128)(2,1)} %bitcast.268, ...), custom_call_target="tpu_custom_call" | custom-call | bytes 270000000 | tf_op jit(solution)/shard_map/pallas_call | solution.py:590
  910.4 14.4 %collective-permute-done.2 = bf16[512,384]{1,0:T(8,128)(2,1)} collective-permute-done((bf16[512,384]{1,0:T(8,128)(2,1)}, bf16[512,384]{1,0:T(8,128)(2,1)}, u32[]{:S(2)}, u32[]{:S(2)}) %collective-permute-start.2) | collective-permute-done | bytes 393248 | tf_op jit(solution)/shard_map/ppermute | solution.py:608
  933.6 90.1 %shard_map.309 = (bf16[4,2,64,2048]{3,2,1,0:T(8,128)(2,1)S(1)}, bf16[4,2,512,384]{3,2,1,0:T(8,128)(2,1)}, bf16[4,2,128,512]{3,2,1,0:T(8,128)(2,1)S(1)}, bf16[4,2...) custom-call(bf16[4,2,64,2048]{3,2,1,0:T(8,128)(2,1)} %bitcast.295, bf16[512,384]{1,0:T(8,128)(2,1)S(1)} %add_convert_fusion.4.refs_1_, ...), custom_call_target="tpu_custom_call" | custom-call | bytes 150000000 | tf_op jit(solution)/shard_map/pallas_call | solution.py:590
  (479 shorter events, 302.3 us)
Async XLA Ops:
  7.2 461.5 %all-gather.4.cloned.1.call-start = ((), (), s32[]{:S(2)}) async-start(), calls=%async_computation.3 | async-start | bytes 14417920 | tf_op jit(solution)/shard_map/all_gather | solution.py:772
  21.3 88.3 %copy-start.57 = (bf16[2,512,1408]{2,1,0:T(8,128)(2,1)S(1)}, bf16[2,512,1408]{2,1,0:T(8,128)(2,1)}, u32[]{:S(2)}) copy-start(bf16[2,512,1408]{2,1,0:T(8,128)(2,1)} %param.33) | copy-start | bytes 8650756
  111.5 370.8 %all-gather.6.cloned.1.call-start = ((), (), s32[]{:S(2)}) async-start(), calls=%async_computation.4 | async-start | bytes 14417920 | tf_op jit(solution)/shard_map/all_gather | solution.py:773
  115.2 410.1 %all-gather.8.cloned.1.call-start = ((), (), s32[]{:S(2)}) async-start(), calls=%async_computation.5 | async-start | bytes 14417920 | tf_op jit(solution)/shard_map/all_gather | solution.py:774
  119.5 923.9 %reduce-scatter.8.cloned.1.call-start = ((), (), s32[]{:S(2)}) async-start(), calls=%async_computation.8 | async-start | bytes 14417920 | tf_op jit(solution)/shard_map/reduce_scatter | solution.py:902
  133.5 137.5 %copy-start.67 = (pred[1024,16]{1,0:T(8,128)(4,1)}, pred[1024,16]{1,0:T(8,128)(4,1)S(1)}, u32[]{:S(2)}) copy-start(pred[1024,16]{1,0:T(8,128)(4,1)S(1)} %copy.221) | copy-start | bytes 49156
  195.5 74.3 %copy-start.28 = (f32[128,2048]{1,0:T(8,128)}, f32[128,2048]{1,0:T(8,128)S(1)}, u32[]{:S(2)}) copy-start(f32[128,2048]{1,0:T(8,128)S(1)} %get-tuple-element.204) | copy-start | bytes 3145732
  195.5 70.9 %copy-start.45 = (bf16[2048,16]{1,0:T(8,128)(2,1)S(1)}, bf16[2048,16]{1,0:T(8,128)(2,1)}, u32[]{:S(2)}) copy-start(bf16[2048,16]{1,0:T(8,128)(2,1)} %reshape.575) | copy-start | bytes 196612
  196.2 73.6 %copy-start.7 = (bf16[128,2048]{1,0:T(8,128)(2,1)}, bf16[128,2048]{1,0:T(8,128)(2,1)S(1)}, u32[]{:S(2)}) copy-start(bf16[128,2048]{1,0:T(8,128)(2,1)S(1)} %multiply_convert_fusion.13.refs_0_) | copy-start | bytes 1572868
  293.4 163.4 %copy-start.91 = (s32[2,1024]{1,0:T(2,128)}, s32[2,1024]{1,0:T(2,128)S(1)}, u32[]{:S(2)}) copy-start(s32[2,1024]{1,0:T(2,128)S(1)} %compare_select_fusion) | copy-start | bytes 24580
  293.4 164.0 %copy-start.33 = (bf16[4,2,128,2048]{3,2,1,0:T(8,128)(2,1)S(1)}, bf16[4,2,128,2048]{3,2,1,0:T(8,128)(2,1)}, u32[]{:S(2)}) copy-start(bf16[4,2,128,2048]{3,2,1,0:T(8,128)(2,1)} %get-tuple-element.53) | copy-start | bytes 12582916
  505.5 543.1 %reduce-scatter.6.cloned.1.call-start = ((), (), s32[]{:S(2)}) async-start(), calls=%async_computation.7 | async-start | bytes 14417920 | tf_op jit(solution)/shard_map/reduce_scatter | solution.py:904
  552.9 500.5 %reduce-scatter.4.cloned.1.call-start = ((), (), s32[]{:S(2)}) async-start(), calls=%async_computation.6 | async-start | bytes 14417920 | tf_op jit(solution)/shard_map/reduce_scatter | solution.py:903
  778.7 85.0 %copy-start.101 = (f32[512]{0:T(512)S(1)}, f32[512]{0:T(512)}, u32[]{:S(2)}) copy-start(f32[512]{0:T(512)} %copy-done.100) | copy-start | bytes 6148
  778.7 91.7 %copy-start.8 = (bf16[128,2048]{1,0:T(8,128)(2,1)S(1)}, bf16[128,2048]{1,0:T(8,128)(2,1)}, u32[]{:S(2)}) copy-start(bf16[128,2048]{1,0:T(8,128)(2,1)} %copy-done.7) | copy-start | bytes 1572868
  868.1 34.0 %collective-permute-start.7 = (bf16[128,640]{1,0:T(8,128)(2,1)}, bf16[128,640]{1,0:T(8,128)(2,1)}, u32[]{:S(2)}, u32[]{:S(2)}) collective-permute-start(bf16[128,640]{1,0:T(8,128)(2,1)} %get-tuple-element.193), channel_id=1, source_target_pairs={{0,2},{1,3},{2,0},{3,1},{4,6},{5,7},{6,4},{7,5},{8,10},{9,11},{10,... | collective-permute-start | bytes 491528 | tf_op jit(solution)/shard_map/ppermute | solution.py:608
  869.6 33.2 %collective-permute-start.6 = (bf16[128,640]{1,0:T(8,128)(2,1)}, bf16[128,640]{1,0:T(8,128)(2,1)}, u32[]{:S(2)}, u32[]{:S(2)}) collective-permute-start(bf16[128,640]{1,0:T(8,128)(2,1)} %get-tuple-element.193), channel_id=1, source_target_pairs={{0,1},{1,0},{2,3},{3,2},{4,5},{5,4},{6,7},{7,6},{8,9},{9,8},{10,11... | collective-permute-start | bytes 491528 | tf_op jit(solution)/shard_map/ppermute | solution.py:608
  878.4 18.4 %collective-permute-start.3 = (bf16[128,512]{1,0:T(8,128)(2,1)}, bf16[128,512]{1,0:T(8,128)(2,1)}, u32[]{:S(2)}, u32[]{:S(2)}) collective-permute-start(bf16[128,512]{1,0:T(8,128)(2,1)} %get-tuple-element.188), channel_id=1, source_target_pairs={{0,1},{1,0},{2,3},{3,2},{4,5},{5,4},{6,7},{7,6},{8,9},{9,8},{10,11... | collective-permute-start | bytes 393224 | tf_op jit(solution)/shard_map/ppermute | solution.py:608
  879.7 18.4 %collective-permute-start.5 = (bf16[128,512]{1,0:T(8,128)(2,1)}, bf16[128,512]{1,0:T(8,128)(2,1)}, u32[]{:S(2)}, u32[]{:S(2)}) collective-permute-start(bf16[128,512]{1,0:T(8,128)(2,1)} %get-tuple-element.189), channel_id=1, source_target_pairs={{0,3},{1,2},{2,1},{3,0},{4,7},{5,6},{6,5},{7,4},{8,11},{9,10},{10,... | collective-permute-start | bytes 393224 | tf_op jit(solution)/shard_map/ppermute | solution.py:608
  881.1 18.6 %collective-permute-start.4 = (bf16[128,512]{1,0:T(8,128)(2,1)}, bf16[128,512]{1,0:T(8,128)(2,1)}, u32[]{:S(2)}, u32[]{:S(2)}) collective-permute-start(bf16[128,512]{1,0:T(8,128)(2,1)} %get-tuple-element.190), channel_id=1, source_target_pairs={{0,2},{1,3},{2,0},{3,1},{4,6},{5,7},{6,4},{7,5},{8,10},{9,11},{10,... | collective-permute-start | bytes 393224 | tf_op jit(solution)/shard_map/ppermute | solution.py:608
  896.7 11.7 %collective-permute-start.8 = (bf16[128,640]{1,0:T(8,128)(2,1)}, bf16[128,640]{1,0:T(8,128)(2,1)S(1)}, u32[]{:S(2)}, u32[]{:S(2)}) collective-permute-start(bf16[128,640]{1,0:T(8,128)(2,1)} %get-tuple-element.193), channel_id=1, source_target_pairs={{0,3},{1,2},{2,1},{3,0},{4,7},{5,6},{6,5},{7,4},{8,11},{9,10},{10,... | collective-permute-start | bytes 491528 | tf_op jit(solution)/shard_map/ppermute | solution.py:608
  898.0 26.8 %collective-permute-start.2 = (bf16[512,384]{1,0:T(8,128)(2,1)}, bf16[512,384]{1,0:T(8,128)(2,1)}, u32[]{:S(2)}, u32[]{:S(2)}) collective-permute-start(bf16[512,384]{1,0:T(8,128)(2,1)} %get-tuple-element.177), channel_id=1, source_target_pairs={{0,3},{1,2},{2,1},{3,0},{4,7},{5,6},{6,5},{7,4},{8,11},{9,10},{10,... | collective-permute-start | bytes 1179656 | tf_op jit(solution)/shard_map/ppermute | solution.py:608
  899.7 30.0 %collective-permute-start.1 = (bf16[512,384]{1,0:T(8,128)(2,1)}, bf16[512,384]{1,0:T(8,128)(2,1)}, u32[]{:S(2)}, u32[]{:S(2)}) collective-permute-start(bf16[512,384]{1,0:T(8,128)(2,1)} %get-tuple-element.178), channel_id=1, source_target_pairs={{0,2},{1,3},{2,0},{3,1},{4,6},{5,7},{6,4},{7,5},{8,10},{9,11},{10,... | collective-permute-start | bytes 1179656 | tf_op jit(solution)/shard_map/ppermute | solution.py:608
  902.1 30.0 %collective-permute-start = (bf16[512,384]{1,0:T(8,128)(2,1)S(1)}, bf16[512,384]{1,0:T(8,128)(2,1)}, u32[]{:S(2)}, u32[]{:S(2)}) collective-permute-start(bf16[512,384]{1,0:T(8,128)(2,1)S(1)} %copy-done.83), channel_id=1, source_target_pairs={{0,1},{1,0},{2,3},{3,2},{4,5},{5,4},{6,7},{7,6},{8,9},{9,8},{10,11... | collective-permute-start | bytes 1179656 | tf_op jit(solution)/shard_map/ppermute | solution.py:608
  (114 other events, 828.7 us)
Sparse Core Ops, SparseCore 0:
  111.6 134.1 all-gather.3
  248.2 163.3 all-gather.5
  413.4 111.7 all-gather.7
  528.2 123.2 reduce-scatter.7
  654.5 112.2 reduce-scatter.5
  769.7 162.8 reduce-scatter.3

commit v7 on v5

--- a/solution.py
+++ b/solution.py
@@ -858,12 +858,12 @@
     d_side_gate, d_side_up = side_pull(d_side_act)
     d_side = jnp.concatenate([d_side_gate, d_side_up], axis=1).astype(BF16)
     grad_sin = t_dot(ffn_all, d_side)
-    dispatch, all_sin, all_sdown = communicate(
+    dispatch, all_sdown, all_sin = communicate(
         5,
         [
             Pass(dispatch),
+            ReduceDpGatherSeq(padded_rows(grad_sdown.astype(BF16).reshape(dp_count, unit, width))),
             ReduceDpGatherSeq(grad_sin.astype(BF16).reshape(dp_count, shard, 2 * side)),
-            ReduceDpGatherSeq(padded_rows(grad_sdown.astype(BF16).reshape(dp_count, unit, width))),
         ],
     )
 

time: 1070 us -> 1070 us (level)
  Pallas kernels: 597 us -> 612 us
    pallas_call x8, Pallas kernels: 587 us -> 602 us  [communicate(): pl.pallas_call(kernel, out_shape=[shape for shape, _ in results], in_spec...]
  transfers between devices with their start and end apart: 18 -> 18, of which waited for: 3 -> 2; matrix products, arithmetic and copies ran while one was open for 36% -> 35% of each run, Pallas kernels for 48% -> 49%
where the time goes in v7:
time: 1070 us
  Pallas kernels  612 us (57%)
  matrix products  223 us (21%)
  other arithmetic  102 us (10%)
  local copies, waits for them, and re-layouts  94.7 us (9%)
  between operations  17 us (2%)
  starting transfers between devices  14.5 us (1%)
    pallas_call x8, Pallas kernels, communicate(): pl.pallas_call(kernel, out_shape=[shape for shape, _ in results], in_spec...  602 us
    dot_general x9, matrix products, dot(): return jnp.dot(left, right, preferred_element_type=F32)  39.3 us
    unnamed x304, local copies, waits for them, and re-layouts  31.3 us
    dot_general x8, matrix products, t_dot(): lax.dot_general(left, right, (((0,), (0,)), ((), ())), preferred_element_...  29.7 us
    dot_general x6, matrix products, dot_t(): lax.dot_general(left, right, (((1,), (1,)), ((), ())), preferred_element_...  27.9 us
  transfers between devices with their start and end apart: 18, of which 2 were waited for; matrix products, arithmetic and copies ran while one was open for 35% of the time, Pallas kernels for 49%

profile of v7, /device:TPU:0, one launch (start us, length us, event | category | flops | bytes accessed | tf_op | source)
XLA Modules:
  0.0 1068.7 jit_solution(15925221735862712995)
XLA Ops:
  21.3 87.2 %shard_map.297 = (bf16[4,2,128,2048]{3,2,1,0:T(8,128)(2,1)}, bf16[4,2,128,128]{3,2,1,0:T(8,128)(2,1)S(1)}, bf16[4,544,512]{2,1,0:T(8,128)(2,1)S(1)}, bf16[4,2,25...) custom-call(bf16[128,2048]{1,0:T(8,128)(2,1)S(1)} %bitcast.258, ...), custom_call_target="tpu_custom_call" | custom-call | bytes 150000000 | tf_op jit(solution)/shard_map/pallas_call | solution.py:582
  169.1 8.4 fusion.87
  182.2 13.2 %shard_map.298 = bf16[8,128,256]{2,1,0:T(8,128)(2,1)S(1)} custom-call(bf16[8,128,256]{2,1,0:T(8,128)(2,1)S(1)} %copy.258.refs_0_), custom_call_target="tpu_custom_call" | custom-call | bytes 150000000 | tf_op jit(solution)/shard_map/pallas_call | solution.py:582
  204.3 65.9 %shard_map.299 = (bf16[4,2,128,2048]{3,2,1,0:T(8,128)(2,1)}, bf16[4,512,704]{2,1,0:T(8,128)(2,1)}, bf16[4,96,2048]{2,1,0:T(8,128)(2,1)S(1)}) custom-call(bf16[128,2048]{1,0:T(8,128)(2,1)S(1)} %multiply_convert_fusion.13.refs_0_, bf16[512,704]{1,0:T(8,128)(2,1)S(1)} %concatenate.58.refs_1_, bf16[96,2048]{1,0:T(8,128)(2,1)S(1)} %pad.31.refs_2_), custom_call_target="tpu_custom_call" | custom-call | bytes 150000000 | tf_op jit(solution)/shard_map/pallas_call | solution.py:582
  277.1 6.3 fusion.92
  298.9 179.5 %shard_map.300 = (bf16[960,1024]{1,0:T(8,128)(2,1)S(1)}, bf16[4,2,96,2048]{3,2,1,0:T(8,128)(2,1)}, bf16[4,2,512,704]{3,2,1,0:T(8,128)(2,1)}) custom-call(bf16[960,1024]{1,0:T(8,128)(2,1)S(1)} %fusion.12.refs_0_, bf16[4,96,2048]{2,1,0:T(8,128)(2,1)S(1)} %pad.32.refs_1_, bf16[4,512,704]{2,1,0:T(8,128)(2,1)} %bitcast.277), custom_call_target="tpu_custom_call", output_to_operand_aliasing={{0}: (0, {})} | custom-call | bytes 150000000 | tf_op jit(solution)/shard_map/pallas_call | solution.py:582
  490.4 13.2 %fusion.93 = f32[2,480,1408]{2,1,0:T(8,128)} fusion(bf16[2,480,2048]{2,1,0:T(8,128)(2,1)} %bitcast.346, bf16[2,2048,1408]{2,1,0:T(8,128)(2,1)} %all-gather.4.cloned.1.call-done), kind=kOutput, calls=%fused_computation.259 | convolution fusion | flops 5536481280 | bytes 20873216 | tf_op jit(solution)/shard_map/nmh,nhq->nmq/dot_general | solution.py:875
  503.6 14.0 %multiply_convert_fusion.5 = (bf16[2,480,1408]{2,1,0:T(8,128)(2,1)S(1)}, f32[2,480,1408]{2,1,0:T(8,128)}) fusion(f32[2,480,1408]{2,1,0:T(8,128)} %fusion.93, bf16[2,480,2048]{2,1,0:T(8,128)(2,1)} %bitcast.347, bf16[2,2048,1408]{2,1,0:T(8,128)(2,1)} %all-gather.6.cloned.1.call-done), kind=kOutput, calls=%fused_computation.23 | convolution fusion | flops 5544591360 | bytes 28983296 | tf_op jit(solution)/shard_map/nmh,nhq->nmq/dot_general | solution.py:878
  517.6 9.2 convolution_convert_fusion.2.refs_1_
  529.1 10.4 shard_map.301
  543.0 10.7 %fusion.94 = f32[2,480,1408]{2,1,0:T(8,128)S(1)} fusion(bf16[2,480,2048]{2,1,0:T(8,128)(2,1)} %shard_map.302, bf16[2,1408,2048]{2,1,0:T(8,128)(2,1)} %all-gather.8.cloned.1.call-done), kind=kOutput, calls=%fused_computation.260 | convolution fusion | flops 5536481280 | bytes 20873216 | tf_op jit(solution)/shard_map/kcd,kfd->kcf/dot_general | solution.py:884
  553.7 7.4 multiply_convert_fusion.4
  562.6 9.5 convolution_convert_fusion.refs_3_
  586.5 9.5 fusion.44
  596.1 10.0 convolution_convert_fusion.1.refs_2_
  608.0 10.5 fusion.95
  618.5 11.8 %add_convert_fusion.2 = bf16[2,480,2048]{2,1,0:T(8,128)(2,1)} fusion(f32[2,480,2048]{2,1,0:T(8,128)S(1)} %fusion.95, bf16[2,480,1408]{2,1,0:T(8,128)(2,1)} %get-tuple-element.63, bf16[2,2048,1408]{2,1,0:T(8,128)(2,1)} %all-gather.6.cloned.1.call-done), kind=kOutput, calls=%fused_computation.14 | convolution fusion | flops 5540413440 | bytes 26034176 | tf_op jit(solution)/shard_map/sta,sra->str/dot_general | solution.py:900
  630.4 9.7 add_convert_fusion.1
  640.1 56.5 %shard_map.304 = (f32[128,2048]{1,0:T(8,128)S(1)}, f32[128,128]{1,0:T(8,128)S(1)}, bf16[4,128,512]{2,1,0:T(8,128)(2,1)S(1)}, bf16[4,128,512]{2,1,0:T(8,128)(2,1)S(1)}) custom-call(bf16[4,2,128,2048]{3,2,1,0:T(8,128)(2,1)} %bitcast.290, bf16[4,2,128,128]{3,2,1,0:T(8,128)(2,1)S(1)} %maximum_maximum_fusion.1.refs_1_, bf16[4,128,512]{2,1,0:T(8,128)(2,1)S(1)} %bitcast.264, ...), custom_call_target="tpu_custom_call" | custom-call | bytes 150000000 | tf_op jit(solution)/shard_map/pallas_call | solution.py:582
  713.8 7.4 convolution_convert_fusion.9
  726.3 17.7 %shard_map.305 = bf16[8,128,256]{2,1,0:T(8,128)(2,1)S(1)} custom-call(bf16[8,128,256]{2,1,0:T(8,128)(2,1)S(1)} %bitcast.262), custom_call_target="tpu_custom_call" | custom-call | bytes 150000000 | tf_op jit(solution)/shard_map/pallas_call | solution.py:582
  787.2 7.0 multiply_convert_fusion.2
  817.5 85.1 %shard_map.308 = (f32[128,640]{1,0:T(8,128)S(1)}, f32[128,2048]{1,0:T(8,128)S(1)}, f32[128,2048]{1,0:T(8,128)S(1)}) custom-call(bf16[4,2,128,640]{3,2,1,0:T(8,128)(2,1)S(1)} %copy-done.7, bf16[4,2,128,2048]{3,2,1,0:T(8,128)(2,1)} %bitcast.272, bf16[4,2,128,2048]{3,2,1,0:T(8,128)(2,1)} %bitcast.271), custom_call_target="tpu_custom_call" | custom-call | bytes 270000000 | tf_op jit(solution)/shard_map/pallas_call | solution.py:582
  930.7 96.7 %shard_map.310 = (bf16[4,2,64,2048]{3,2,1,0:T(8,128)(2,1)S(1)}, bf16[4,2,512,384]{3,2,1,0:T(8,128)(2,1)}, bf16[4,2,128,512]{3,2,1,0:T(8,128)(2,1)S(1)}, bf16[4,2...) custom-call(bf16[4,2,64,2048]{3,2,1,0:T(8,128)(2,1)} %bitcast.298, bf16[512,384]{1,0:T(8,128)(2,1)S(1)} %add_convert_fusion.4.refs_1_, ...), custom_call_target="tpu_custom_call" | custom-call | bytes 150000000 | tf_op jit(solution)/shard_map/pallas_call | solution.py:582
  (535 shorter events, 295.0 us)
Async XLA Ops:
  7.2 483.2 %all-gather.4.cloned.1.call-start = ((), (), s32[]{:S(2)}) async-start(), calls=%async_computation.3 | async-start | bytes 14417920 | tf_op jit(solution)/shard_map/all_gather | solution.py:764
  21.3 88.3 %copy-start.60 = (bf16[2,512,1408]{2,1,0:T(8,128)(2,1)S(1)}, bf16[2,512,1408]{2,1,0:T(8,128)(2,1)}, u32[]{:S(2)}) copy-start(bf16[2,512,1408]{2,1,0:T(8,128)(2,1)} %param.33) | copy-start | bytes 8650756
  111.5 392.1 %all-gather.6.cloned.1.call-start = ((), (), s32[]{:S(2)}) async-start(), calls=%async_computation.4 | async-start | bytes 14417920 | tf_op jit(solution)/shard_map/all_gather | solution.py:765
  115.2 427.8 %all-gather.8.cloned.1.call-start = ((), (), s32[]{:S(2)}) async-start(), calls=%async_computation.5 | async-start | bytes 14417920 | tf_op jit(solution)/shard_map/all_gather | solution.py:766
  119.4 927.5 %reduce-scatter.8.cloned.1.call-start = ((), (), s32[]{:S(2)}) async-start(), calls=%async_computation.8 | async-start | bytes 14417920 | tf_op jit(solution)/shard_map/reduce_scatter | solution.py:894
  298.5 179.9 %copy-start.97 = (s32[2,1024]{1,0:T(2,128)}, s32[2,1024]{1,0:T(2,128)S(1)}, u32[]{:S(2)}) copy-start(s32[2,1024]{1,0:T(2,128)S(1)} %compare_select_fusion) | copy-start | bytes 24580
  298.5 180.4 %copy-start.36 = (bf16[4,2,128,2048]{3,2,1,0:T(8,128)(2,1)S(1)}, bf16[4,2,128,2048]{3,2,1,0:T(8,128)(2,1)}, u32[]{:S(2)}) copy-start(bf16[4,2,128,2048]{3,2,1,0:T(8,128)(2,1)} %get-tuple-element.54) | copy-start | bytes 12582916
  526.8 525.3 %reduce-scatter.6.cloned.1.call-start = ((), (), s32[]{:S(2)}) async-start(), calls=%async_computation.7 | async-start | bytes 14417920 | tf_op jit(solution)/shard_map/reduce_scatter | solution.py:896
  572.2 484.8 %reduce-scatter.4.cloned.1.call-start = ((), (), s32[]{:S(2)}) async-start(), calls=%async_computation.6 | async-start | bytes 14417920 | tf_op jit(solution)/shard_map/reduce_scatter | solution.py:895
  705.3 104.3 %collective-permute-start.2 = (bf16[128,2048]{1,0:T(8,128)(2,1)}, bf16[128,2048]{1,0:T(8,128)(2,1)}, u32[]{:S(2)}, u32[]{:S(2)}) collective-permute-start(bf16[128,2048]{1,0:T(8,128)(2,1)} %fusion.84), channel_id=1, source_target_pairs={{0,3},{1,2},{2,1},{3,0},{4,7},{5,6},{6,5},{7,4},{8,11},{9,10},{10,... | collective-permute-start | bytes 1572872 | tf_op jit(solution)/shard_map/ppermute | solution.py:600
  706.7 104.1 %collective-permute-start.1 = (bf16[128,2048]{1,0:T(8,128)(2,1)}, bf16[128,2048]{1,0:T(8,128)(2,1)}, u32[]{:S(2)}, u32[]{:S(2)}) collective-permute-start(bf16[128,2048]{1,0:T(8,128)(2,1)} %fusion.84), channel_id=1, source_target_pairs={{0,2},{1,3},{2,0},{3,1},{4,6},{5,7},{6,4},{7,5},{8,10},{9,11},{10,... | collective-permute-start | bytes 1572872 | tf_op jit(solution)/shard_map/ppermute | solution.py:600
  707.9 103.8 %collective-permute-start = (bf16[128,2048]{1,0:T(8,128)(2,1)}, bf16[128,2048]{1,0:T(8,128)(2,1)}, u32[]{:S(2)}, u32[]{:S(2)}) collective-permute-start(bf16[128,2048]{1,0:T(8,128)(2,1)} %fusion.84), channel_id=1, source_target_pairs={{0,1},{1,0},{2,3},{3,2},{4,5},{5,4},{6,7},{7,6},{8,9},{9,8},{10,11... | collective-permute-start | bytes 1572872 | tf_op jit(solution)/shard_map/ppermute | solution.py:600
  774.7 147.2 %collective-permute-start.6 = (bf16[128,512]{1,0:T(8,128)(2,1)}, bf16[128,512]{1,0:T(8,128)(2,1)}, u32[]{:S(2)}, u32[]{:S(2)}) collective-permute-start(bf16[128,512]{1,0:T(8,128)(2,1)} %get-tuple-element.190), channel_id=1, source_target_pairs={{0,1},{1,0},{2,3},{3,2},{4,5},{5,4},{6,7},{7,6},{8,9},{9,8},{10,11... | collective-permute-start | bytes 393224 | tf_op jit(solution)/shard_map/ppermute | solution.py:600
  775.8 147.9 %collective-permute-start.8 = (bf16[128,512]{1,0:T(8,128)(2,1)}, bf16[128,512]{1,0:T(8,128)(2,1)}, u32[]{:S(2)}, u32[]{:S(2)}) collective-permute-start(bf16[128,512]{1,0:T(8,128)(2,1)} %get-tuple-element.191), channel_id=1, source_target_pairs={{0,3},{1,2},{2,1},{3,0},{4,7},{5,6},{6,5},{7,4},{8,11},{9,10},{10,... | collective-permute-start | bytes 393224 | tf_op jit(solution)/shard_map/ppermute | solution.py:600
  809.6 107.6 %collective-permute-start.5 = (bf16[512,384]{1,0:T(8,128)(2,1)}, bf16[512,384]{1,0:T(8,128)(2,1)}, u32[]{:S(2)}, u32[]{:S(2)}) collective-permute-start(bf16[512,384]{1,0:T(8,128)(2,1)} %get-tuple-element.179), channel_id=1, source_target_pairs={{0,3},{1,2},{2,1},{3,0},{4,7},{5,6},{6,5},{7,4},{8,11},{9,10},{10,... | collective-permute-start | bytes 1179656 | tf_op jit(solution)/shard_map/ppermute | solution.py:600
  810.8 107.2 %collective-permute-start.4 = (bf16[512,384]{1,0:T(8,128)(2,1)}, bf16[512,384]{1,0:T(8,128)(2,1)}, u32[]{:S(2)}, u32[]{:S(2)}) collective-permute-start(bf16[512,384]{1,0:T(8,128)(2,1)} %get-tuple-element.180), channel_id=1, source_target_pairs={{0,2},{1,3},{2,0},{3,1},{4,6},{5,7},{6,4},{7,5},{8,10},{9,11},{10,... | collective-permute-start | bytes 1179656 | tf_op jit(solution)/shard_map/ppermute | solution.py:600
  811.7 107.6 %collective-permute-start.3 = (bf16[512,384]{1,0:T(8,128)(2,1)}, bf16[512,384]{1,0:T(8,128)(2,1)}, u32[]{:S(2)}, u32[]{:S(2)}) collective-permute-start(bf16[512,384]{1,0:T(8,128)(2,1)} %get-tuple-element.181), channel_id=1, source_target_pairs={{0,1},{1,0},{2,3},{3,2},{4,5},{5,4},{6,7},{7,6},{8,9},{9,8},{10,11... | collective-permute-start | bytes 1179656 | tf_op jit(solution)/shard_map/ppermute | solution.py:600
  817.5 87.1 %copy-start.113 = (f32[512]{0:T(512)S(1)}, f32[512]{0:T(512)}, u32[]{:S(2)}) copy-start(f32[512]{0:T(512)} %copy-done.111) | copy-start | bytes 6148
  817.5 87.1 %copy-start.132 = (f32[128]{0:T(128)S(1)}, f32[128]{0:T(128)}, u32[]{:S(2)}) copy-start(f32[128]{0:T(128)} %add_rsqrt_fusion.2) | copy-start | bytes 1540
  817.5 91.1 %copy-start.126 = (f32[128]{0:T(128)S(1)}, f32[128]{0:T(128)}, u32[]{:S(2)}) copy-start(f32[128]{0:T(128)} %add_rsqrt_fusion.3) | copy-start | bytes 1540
  917.2 6.6 collective-permute-start.7
  918.0 11.7 %collective-permute-start.10 = (bf16[128,640]{1,0:T(8,128)(2,1)}, bf16[128,640]{1,0:T(8,128)(2,1)S(1)}, u32[]{:S(2)}, u32[]{:S(2)}) collective-permute-start(bf16[128,640]{1,0:T(8,128)(2,1)} %get-tuple-element.199), channel_id=1, source_target_pairs={{0,2},{1,3},{2,0},{3,1},{4,6},{5,7},{6,4},{7,5},{8,10},{9,11},{10,... | collective-permute-start | bytes 491528 | tf_op jit(solution)/shard_map/ppermute | solution.py:600
  919.3 10.4 collective-permute-start.9
  921.9 7.8 collective-permute-start.11
  (139 other events, 1062.4 us)
Sparse Core Ops, SparseCore 0:
  111.6 125.9 all-gather.3
  240.1 172.3 all-gather.5
  414.3 113.6 all-gather.7
  530.9 112.1 reduce-scatter.7
  646.1 134.9 reduce-scatter.5
  784.1 130.3 reduce-scatter.3
